TPU v7x, 512 devices: a whole 4x4x16 slice. The times are simulated.
512 devices in a mesh: ctx: 128 (over z, x, core), head: 4 (over y).
Axes of the slice: x: 4, y: 4, z: 16, core: 2. Of those that a mesh axis runs over, the one named last changes fastest.
Arguments:
- queries: bfloat16 [65536, 1024], P('ctx', 'head'), may hold values from -16 to 16
- keys: bfloat16 [65536, 128], P('ctx'), may hold values from -8 to 8
- values: bfloat16 [65536, 128], P('ctx'), may hold values from -6 to 6
- d_out: bfloat16 [65536, 1024], P('ctx', 'head'), may hold values from -6 to 6
- doc_lengths: int32 [128], replicated, may hold values from 1 to 1536, 65536 in all
Outputs:
- attended: bfloat16 [65536, 1024], P('ctx', 'head')
- d_queries: bfloat16 [65536, 1024], P('ctx', 'head')
- d_keys: bfloat16 [65536, 128], P('ctx')
- d_values: bfloat16 [65536, 128], P('ctx')
Inputs may be any that keep to these rules, and one draw needn't show every extreme that they name: `doc_lengths`: the documents lie end to end in order and their lengths sum to 65536; the longest is exactly 1536 tokens.
All inputs are finite; a program needn't handle non-finite values.
Results may differ from a plain program's by a relative error of at most 0.024.
Values may be sent and summed in bfloat16 or wider, within the bound.
No kernel may reach another device: no remote copies, remote signals or barrier semaphores. Data moves between devices by JAX's collectives and lax.ppermute only.
A program may use at most 64 MiB of HBM per device.

v0:
```python
import math

import jax
import jax.numpy as jnp
from jax import lax
from jax.sharding import PartitionSpec as P

SPAN = 3


def passed_along(value, axis, steps):
    count = lax.axis_size(axis)
    leading, last = (max(0, -steps), min(count, count - steps))
    return lax.ppermute(value, axis, [(source, source + steps) for source in range(leading, last)])


def on_device(queries, keys, values, d_out, doc_lengths):
    block_rows = queries.shape[0]
    head_width = keys.shape[1]
    local_heads = queries.shape[1] // head_width
    score_scale = 1.0 / math.sqrt(head_width)
    device = lax.axis_index("ctx")
    positions = device * block_rows + jnp.arange(block_rows, dtype=jnp.int32)
    doc_ends = jnp.cumsum(doc_lengths)
    doc_start = jnp.sum(
        jnp.where(doc_ends[None, :] <= positions[:, None], doc_lengths[None, :], 0), axis=1
    )
    query_heads = queries.reshape(block_rows, local_heads, head_width)
    grad_heads = d_out.reshape(block_rows, local_heads, head_width)
    kv_blocks = [(keys, values)]
    current = (keys, values)
    for offset in range(1, SPAN + 1):
        current = passed_along((current[0], current[1]), "ctx", 1)
        kv_blocks.append(current)
    live_flags = [jnp.array(True)]
    for offset in range(1, SPAN + 1):
        live_flags.append(
            (device >= offset) & (doc_start[0] <= (device - offset + 1) * block_rows - 1)
        )

    def scores_for(offset):
        key_positions = (device - offset) * block_rows + jnp.arange(block_rows, dtype=jnp.int32)
        allowed = (key_positions[None, :] >= doc_start[:, None]) & (
            key_positions[None, :] <= positions[:, None]
        )
        products = jnp.einsum(
            "thd,jd->htj", query_heads, kv_blocks[offset][0], preferred_element_type=jnp.float32
        )
        return jnp.where(allowed[None], products * score_scale, -jnp.inf)

    score_tiles = [scores_for(0)]
    for offset in range(1, SPAN + 1):
        score_tiles.append((lambda offset=offset: scores_for(offset))())
    row_max = jnp.max(score_tiles[0], axis=2)
    for offset in range(1, SPAN + 1):
        row_max = jnp.maximum(row_max, jnp.max(score_tiles[offset], axis=2))
    row_sum = jnp.zeros_like(row_max)
    for offset in range(SPAN + 1):
        row_sum = row_sum + jnp.sum(jnp.exp(score_tiles[offset] - row_max[..., None]), axis=2)
    log_total = row_max + jnp.log(row_sum)

    def forward_tile(offset, out_sum):
        weights = jnp.exp(score_tiles[offset] - log_total[..., None]).astype(jnp.bfloat16)
        return out_sum + jnp.einsum(
            "htj,jd->thd", weights, kv_blocks[offset][1], preferred_element_type=jnp.float32
        )

    out_sum = jnp.zeros((block_rows, local_heads, head_width), jnp.float32)
    for offset in range(SPAN + 1):
        out_sum = (lambda offset=offset, out_sum=out_sum: forward_tile(offset, out_sum))()
    attended = out_sum.astype(jnp.bfloat16)
    row_dot = jnp.transpose(
        jnp.sum(grad_heads.astype(jnp.float32) * attended.astype(jnp.float32), axis=2)
    )

    def backward_tile(offset, dq_sum):
        key_block, value_block = kv_blocks[offset]
        exponent = jnp.exp(score_tiles[offset] - log_total[..., None])
        weights = exponent.astype(jnp.bfloat16)
        d_weights = jnp.einsum(
            "thd,jd->htj", grad_heads, value_block, preferred_element_type=jnp.float32
        )
        d_scores = (exponent * (d_weights - row_dot[..., None])).astype(jnp.bfloat16)
        dq_sum = dq_sum + jnp.einsum(
            "htj,jd->thd", d_scores, key_block, preferred_element_type=jnp.float32
        )
        key_grad = (
            jnp.einsum("htj,thd->jd", d_scores, query_heads, preferred_element_type=jnp.float32)
            * score_scale
        )
        value_grad = jnp.einsum(
            "htj,thd->jd", weights, grad_heads, preferred_element_type=jnp.float32
        )
        return (dq_sum, key_grad, value_grad)

    dq_sum = jnp.zeros((block_rows, local_heads, head_width), jnp.float32)
    key_parts = []
    value_parts = []
    for offset in range(SPAN + 1):
        dq_sum, key_grad, value_grad = (
            lambda offset=offset, dq_sum=dq_sum: backward_tile(offset, dq_sum)
        )()
        key_parts.append(key_grad)
        value_parts.append(value_grad)
    d_queries = (
        (dq_sum * score_scale).astype(jnp.bfloat16).reshape(block_rows, local_heads * head_width)
    )
    key_total = key_parts[0]
    value_total = value_parts[0]
    for offset in range(1, SPAN + 1):
        key_back, value_back = passed_along(
            (key_parts[offset], value_parts[offset]), "ctx", -offset
        )
        key_total = key_total + key_back
        value_total = value_total + value_back
    key_total, value_total = lax.psum((key_total, value_total), "head")
    d_keys = key_total.astype(jnp.bfloat16)
    d_values = value_total.astype(jnp.bfloat16)
    return (attended.reshape(block_rows, local_heads * head_width), d_queries, d_keys, d_values)


def solution(mesh):
    in_specs = (P("ctx", "head"), P("ctx", None), P("ctx", None), P("ctx", "head"), P())
    out_specs = (P("ctx", "head"), P("ctx", "head"), P("ctx", None), P("ctx", None))
    return jax.shard_map(
        on_device, mesh=mesh, in_specs=in_specs, out_specs=out_specs, check_vma=False
    )
```

profile of v0, /device:TPU:390, one launch (start us, length us, event | category | flops | bytes accessed | tf_op | source)
XLA Modules:
  0.0 103.8 jit_solution(6360880624745111303)
XLA Ops:
  0.6 0.0 copy-start
  0.6 1.7 %copy.90 = bf16[512,128]{0,1:T(8,128)(2,1)} copy(bf16[512,128]{1,0:T(8,128)(2,1)} %param.7) | data formatting | bytes 262144 | tf_op args[2]
  2.4 1.9 %collective-permute-start.3 = (bf16[512,128]{0,1:T(8,128)(2,1)}, bf16[512,128]{0,1:T(8,128)(2,1)S(1)}, u32[]{:S(2)}, u32[]{:S(2)}) collective-permute-start(bf16[512,128]{0,1:T(8,128)(2,1)} %copy.90), channel_id=1, source_target_pairs={{0,4},{4,8},{8,12},{12,16},{16,20},{20,24},{24,28},{28,32},{32,36}... | collective-permute-start | bytes 393224 | tf_op jit(solution)/shard_map/ppermute | solution.py:14
  4.3 2.9 %collective-permute-start = (bf16[512,128]{1,0:T(8,128)(2,1)}, bf16[512,128]{1,0:T(8,128)(2,1)}, u32[]{:S(2)}, u32[]{:S(2)}) collective-permute-start(bf16[512,128]{1,0:T(8,128)(2,1)} %param.6), channel_id=1, source_target_pairs={{0,4},{4,8},{8,12},{12,16},{16,20},{20,24},{24,28},{28,32},{32,36}... | collective-permute-start | bytes 393224 | tf_op jit(solution)/shard_map/ppermute | solution.py:14
  7.2 0.0 copy-start.10
  7.2 0.8 copy.83
  8.1 0.2 reduce-window.8
  8.2 0.1 reduce
  8.4 0.9 select_reduce_fusion
  9.2 1.6 %compare_and_fusion.2 = (pred[512,512]{0,1:T(8,128)(4,1)S(1)}, pred[512,512]{0,1:T(8,128)(4,1)}, pred[512,512]{0,1:T(8,128)(4,1)S(1)}, pred[512,512]{0,1:T(8,128)(4,1)S(1)}) fusion(s32[512]{0:T(512)S(1)} %get-tuple-element.39, s32[512]{0:T(512)S(1)} %select_reduce_fusion, s32[512]{0:T(512)S(1)} %get-tuple-element.38, s32[512]{0:T(512)S(1)} %get-tuple-element.37, ...), kind=kLoop, calls=%fused_computation.57 | loop fusion | flops 3145728 | bytes 1058816 | tf_op jit(solution)/shard_map/and | solution.py:43
  10.8 1.4 %fusion.69 = (f32[2,512]{1,0:T(2,128)S(1)}, f32[2,512,512]{1,2,0:T(8,128)S(1)}) fusion(bf16[512,128]{1,0:T(8,128)(2,1)} %param.6, pred[512,512]{0,1:T(8,128)(4,1)S(1)} %get-tuple-element.25, bf16[512,256]{1,0:T(8,128)(2,1)S(1)} %copy-done), kind=kOutput, calls=%fused_computation.103 | convolution fusion | flops 135789568 | bytes 2756608 | tf_op jit(solution)/shard_map/thd,jd->htj/dot_general | solution.py:46
  12.3 0.1 copy.94
  12.4 0.0 copy-start.11
  12.4 0.0 collective-permute-done.3
  12.5 2.1 %collective-permute-start.4 = (bf16[512,128]{0,1:T(8,128)(2,1)S(1)}, bf16[512,128]{0,1:T(8,128)(2,1)S(1)}, u32[]{:S(2)}, u32[]{:S(2)}) collective-permute-start(bf16[512,128]{0,1:T(8,128)(2,1)S(1)} %collective-permute-done.3), channel_id=1, source_target_pairs={{0,4},{4,8},{8,12},{12,16},{16,20},{20,24},{24,28},{28,32},{32,36}... | collective-permute-start | bytes 393224 | tf_op jit(solution)/shard_map/ppermute | solution.py:14
  14.5 3.5 %collective-permute-start.1 = (bf16[512,128]{1,0:T(8,128)(2,1)}, bf16[512,128]{1,0:T(8,128)(2,1)S(1)}, u32[]{:S(2)}, u32[]{:S(2)}) collective-permute-start(bf16[512,128]{1,0:T(8,128)(2,1)} %collective-permute-done), channel_id=1, source_target_pairs={{0,4},{4,8},{8,12},{12,16},{16,20},{20,24},{24,28},{28,32},{32,36}... | collective-permute-start | bytes 393224 | tf_op jit(solution)/shard_map/ppermute | solution.py:14
  18.0 1.4 %fusion.70 = (f32[2,512]{1,0:T(2,128)S(1)}, f32[2,512,512]{1,2,0:T(8,128)S(1)}) fusion(bf16[512,128]{1,0:T(8,128)(2,1)} %collective-permute-done, pred[512,512]{0,1:T(8,128)(4,1)S(1)} %get-tuple-element.22, bf16[512,256]{1,0:T(8,128)(2,1)S(1)} %copy-done), kind=kOutput, calls=%fused_computation.104 | convolution fusion | flops 135789568 | bytes 2756608 | tf_op jit(solution)/shard_map/thd,jd->htj/dot_general | solution.py:46
  19.5 0.0 collective-permute-done.4
  19.5 1.9 %collective-permute-start.5 = (bf16[512,128]{0,1:T(8,128)(2,1)S(1)}, bf16[512,128]{0,1:T(8,128)(2,1)S(1)}, u32[]{:S(2)}, u32[]{:S(2)}) collective-permute-start(bf16[512,128]{0,1:T(8,128)(2,1)S(1)} %collective-permute-done.4), channel_id=1, source_target_pairs={{0,4},{4,8},{8,12},{12,16},{16,20},{20,24},{24,28},{28,32},{32,36}... | collective-permute-start | bytes 393224 | tf_op jit(solution)/shard_map/ppermute | solution.py:14
  21.4 0.0 collective-permute-done.1
  21.5 0.0 copy-start.12
  21.5 5.0 %collective-permute-start.2 = (bf16[512,128]{1,0:T(8,128)(2,1)S(1)}, bf16[512,128]{1,0:T(8,128)(2,1)S(1)}, u32[]{:S(2)}, u32[]{:S(2)}) collective-permute-start(bf16[512,128]{1,0:T(8,128)(2,1)S(1)} %collective-permute-done.1), channel_id=1, source_target_pairs={{0,4},{4,8},{8,12},{12,16},{16,20},{20,24},{24,28},{28,32},{32,36}... | collective-permute-start | bytes 393224 | tf_op jit(solution)/shard_map/ppermute | solution.py:14
  26.4 0.5 fusion.68
  27.0 0.8 collective-permute-done.2
  27.8 0.5 fusion.67
  28.3 0.1 copy-done.15
  28.4 1.1 %exponential_reduce_fusion.2 = (f32[2,512]{1,0:T(2,128)S(1)}, f32[2,512]{1,0:T(2,128)S(1)}, f32[2,512]{1,0:T(2,128)S(1)}, f32[2,512]{1,0:T(2,128)S(1)}) fusion(f32[2,512,512]{1,2,0:T(8,128)S(1)} %get-tuple-element.33, f32[2,512]{1,0:T(2,128)S(1)} %maximum_maximum_fusion, f32[2,512,512]{1,2,0:T(8,128)S(1)} %get-tuple-element.29, ...), kind=kLoop, calls=%fused_computation.22 | loop fusion | flops 4190208 | bytes 8409088 | tf_op jit(solution)/shard_map/reduce_sum | solution.py:59
  29.6 0.4 convolution_bitcast_fusion.2
  30.0 0.0 copy-start.9
  30.0 1.1 %convolution_bitcast_fusion.1 = f32[512,128]{1,0:T(8,128)} fusion(bf16[512,2,128]{0,2,1:T(8,128)(2,1)S(1)} %bitcast.204, f32[2,512,512]{1,2,0:T(8,128)S(1)} %get-tuple-element.29, f32[2,512]{1,0:T(2,128)S(1)} %log_add_fusion), kind=kOutput, calls=%fused_computation.38 | convolution fusion | flops 135266304 | bytes 2625536 | tf_op jit(solution)/shard_map/htj,thd->jd/dot_general | solution.py:91
  31.2 1.2 %convolution_bitcast_fusion = f32[512,128]{1,0:T(8,128)} fusion(bf16[512,2,128]{0,2,1:T(8,128)(2,1)S(1)} %bitcast.205, f32[2,512,512]{1,2,0:T(8,128)S(1)} %get-tuple-element.27, f32[2,512]{1,0:T(2,128)S(1)} %log_add_fusion), kind=kOutput, calls=%fused_computation.37 | convolution fusion | flops 135266304 | bytes 2625536 | tf_op jit(solution)/shard_map/htj,thd->jd/dot_general | solution.py:91
  32.4 0.5 fusion.32
  32.9 1.9 %collective-permute-start.11 = (f32[512,128]{1,0:T(8,128)}, f32[512,128]{1,0:T(8,128)}, u32[]{:S(2)}, u32[]{:S(2)}) collective-permute-start(f32[512,128]{1,0:T(8,128)} %convolution_bitcast_fusion), channel_id=1, source_target_pairs={{12,0},{16,4},{20,8},{24,12},{28,16},{32,20},{36,24},{40,28},{44,3... | collective-permute-start | bytes 786440 | tf_op jit(solution)/shard_map/ppermute | solution.py:14
  34.8 3.2 %collective-permute-start.10 = (f32[512,128]{1,0:T(8,128)}, f32[512,128]{1,0:T(8,128)}, u32[]{:S(2)}, u32[]{:S(2)}) collective-permute-start(f32[512,128]{1,0:T(8,128)} %convolution_bitcast_fusion.1), channel_id=1, source_target_pairs={{8,0},{12,4},{16,8},{20,12},{24,16},{28,20},{32,24},{36,28},{40,32... | collective-permute-start | bytes 786440 | tf_op jit(solution)/shard_map/ppermute | solution.py:14
  38.0 8.7 %collective-permute-start.9 = (f32[512,128]{1,0:T(8,128)S(1)}, f32[512,128]{1,0:T(8,128)}, u32[]{:S(2)}, u32[]{:S(2)}) collective-permute-start(f32[512,128]{1,0:T(8,128)S(1)} %convolution_bitcast_fusion.2), channel_id=1, source_target_pairs={{4,0},{8,4},{12,8},{16,12},{20,16},{24,20},{28,24},{32,28},{36,32}... | collective-permute-start | bytes 786440 | tf_op jit(solution)/shard_map/ppermute | solution.py:14
  46.7 0.5 convolution_add_fusion.2
  47.2 0.5 convolution_add_fusion.1
  47.7 0.0 collective-permute-done.5
  47.8 0.5 multiply_reduce_fusion
  48.3 1.5 %fusion.7 = bf16[2,512,512]{1,2,0:T(8,128)(2,1)} fusion(f32[2,512,512]{1,2,0:T(8,128)S(1)} %get-tuple-element.31, bf16[512,2,128]{0,2,1:T(8,128)(2,1)S(1)} %bitcast.206, f32[2,512]{1,0:T(2,128)S(1)} %bitcast.213, f32[2,512]{1,0:T(2,128)S(1)} %log_add_fusion, bf16[512,128]{1,0:T(8,128)(2,1)S(1)} %copy-done.9), kind=kOutput, calls=%fused_computation.11 | convolution fusion | flops 136314880 | bytes 3547136 | tf_op jit(solution)/shard_map/thd,jd->htj/dot_general | solution.py:80
  49.8 0.8 copy.118
  50.6 2.2 %fusion.3 = bf16[2,512,512]{1,2,0:T(8,128)(2,1)S(1)} fusion(f32[2,512,512]{1,2,0:T(8,128)} %copy-done.5, bf16[512,2,128]{0,2,1:T(8,128)(2,1)S(1)} %bitcast.207, f32[2,512]{1,0:T(2,128)S(1)} %bitcast.214, f32[2,512]{1,0:T(2,128)S(1)} %log_add_fusion, bf16[512,128]{0,1:T(8,128)(2,1)S(1)} %collective-permute-done.4), kind=kOutput, calls=%fused_computation.5 | convolution fusion | flops 136314880 | bytes 3547136 | tf_op jit(solution)/shard_map/thd,jd->htj/dot_general | solution.py:80
  52.9 1.1 %fusion.16 = f32[512,128]{1,0:T(8,128)} fusion(bf16[2,512,512]{1,2,0:T(8,128)(2,1)S(1)} %fusion.3, bf16[512,256]{1,0:T(8,128)(2,1)S(1)} %copy-done), kind=kOutput, calls=%fused_computation.44 | convolution fusion | flops 134283264 | bytes 1572864 | tf_op jit(solution)/shard_map/htj,thd->jd/dot_general | solution.py:88
  54.0 0.5 fusion.5
  54.5 1.1 %fusion.17 = f32[512,128]{1,0:T(8,128)} fusion(bf16[2,512,512]{1,2,0:T(8,128)(2,1)S(1)} %fusion.5, bf16[512,256]{1,0:T(8,128)(2,1)S(1)} %copy-done), kind=kOutput, calls=%fused_computation.46 | convolution fusion | flops 134283264 | bytes 1572864 | tf_op jit(solution)/shard_map/htj,thd->jd/dot_general | solution.py:88
  55.7 1.9 %collective-permute-start.6 = (f32[512,128]{1,0:T(8,128)}, f32[512,128]{1,0:T(8,128)S(1)}, u32[]{:S(2)}, u32[]{:S(2)}) collective-permute-start(f32[512,128]{1,0:T(8,128)} %fusion.17), channel_id=1, source_target_pairs={{4,0},{8,4},{12,8},{16,12},{20,16},{24,20},{28,24},{32,28},{36,32}... | collective-permute-start | bytes 786440 | tf_op jit(solution)/shard_map/ppermute | solution.py:14
  57.6 2.8 %collective-permute-start.7 = (f32[512,128]{1,0:T(8,128)}, f32[512,128]{1,0:T(8,128)}, u32[]{:S(2)}, u32[]{:S(2)}) collective-permute-start(f32[512,128]{1,0:T(8,128)} %fusion.16), channel_id=1, source_target_pairs={{8,0},{12,4},{16,8},{20,12},{24,16},{28,20},{32,24},{36,28},{40,32... | collective-permute-start | bytes 786440 | tf_op jit(solution)/shard_map/ppermute | solution.py:14
  60.4 0.3 fusion.56
  60.8 0.0 copy-start.13
  60.8 0.5 fusion.1
  61.3 0.0 copy-start.16
  61.3 1.5 %convolution_add_fusion.5 = f32[2,512,128]{1,2,0:T(8,128)S(1)} fusion(f32[2,512,128]{1,2,0:T(8,128)S(1)} %fusion.56, bf16[2,512,512]{1,2,0:T(8,128)(2,1)S(1)} %fusion.5, bf16[512,128]{1,0:T(8,128)(2,1)} %collective-permute-done), kind=kOutput, calls=%fused_computation.33 | convolution fusion | flops 134348800 | bytes 2228224 | tf_op jit(solution)/shard_map/htj,jd->thd/dot_general | solution.py:84
  62.8 0.4 convolution_add_fusion.4
  63.2 0.4 fusion.13
  63.6 0.8 copy.119
  64.4 1.7 %fusion.15 = f32[512,128]{1,0:T(8,128)S(1)} fusion(bf16[2,512,512]{1,2,0:T(8,128)(2,1)} %copy-done.8, bf16[512,256]{1,0:T(8,128)(2,1)S(1)} %copy-done), kind=kOutput, calls=%fused_computation.42 | convolution fusion | flops 134283264 | bytes 1572864 | tf_op jit(solution)/shard_map/htj,thd->jd/dot_general | solution.py:88
  66.1 0.0 collective-permute-done.11
  66.1 2.1 %collective-permute-start.8 = (f32[512,128]{1,0:T(8,128)S(1)}, f32[512,128]{1,0:T(8,128)S(1)}, u32[]{:S(2)}, u32[]{:S(2)}) collective-permute-start(f32[512,128]{1,0:T(8,128)S(1)} %fusion.15), channel_id=1, source_target_pairs={{12,0},{16,4},{20,8},{24,12},{28,16},{32,20},{36,24},{40,28},{44,3... | collective-permute-start | bytes 786440 | tf_op jit(solution)/shard_map/ppermute | solution.py:14
  68.2 0.0 collective-permute-done.9
  68.3 1.6 %fusion.24 = f32[512,128]{1,0:T(8,128)S(1)} fusion(f32[512,128]{1,0:T(8,128)} %collective-permute-done.11, f32[512,128]{1,0:T(8,128)} %collective-permute-done.10, f32[512,128]{1,0:T(8,128)} %collective-permute-done.9, bf16[512,2,128]{0,2,1:T(8,128)(2,1)S(1)} %bitcast.210, f32[2,512,512]{1,2,0:T(8,128)S(1)} %get-tuple-element.31, f32[2,512]{1,0:T(2,128)S(1)} %log_add_fusion), kind=kOutput, calls=%fused_computation.54 | convolution fusion | flops 135462912 | bytes 3411968 | tf_op jit(solution)/shard_map/htj,thd->jd/dot_general | solution.py:91
  69.8 0.8 collective-permute-done.7
  70.6 8.4 %collective-permute-done.8 = f32[512,128]{1,0:T(8,128)S(1)} collective-permute-done((f32[512,128]{1,0:T(8,128)S(1)}, f32[512,128]{1,0:T(8,128)S(1)}, u32[]{:S(2)}, u32[]{:S(2)}) %collective-permute-start.8) | collective-permute-done | bytes 262176 | tf_op jit(solution)/shard_map/ppermute | solution.py:14
  79.0 1.4 %fusion.21 = f32[512,128]{1,0:T(8,128)S(1)} fusion(f32[512,128]{1,0:T(8,128)S(1)} %collective-permute-done.8, f32[512,128]{1,0:T(8,128)} %collective-permute-done.7, f32[512,128]{1,0:T(8,128)S(1)} %collective-permute-done.6, bf16[2,512,512]{1,2,0:T(8,128)(2,1)S(1)} %copy-done.7, bf16[512,256]{1,0:T(8,128)(2,1)S(1)} %copy-done), kind=kOutput, calls=%fused_computation.51 | convolution fusion | flops 134479872 | bytes 2359296 | tf_op jit(solution)/shard_map/htj,thd->jd/dot_general | solution.py:88
  80.4 23.4 %all-reduce.2 = (bf16[512,128]{1,0:T(8,128)(2,1)}, bf16[512,128]{1,0:T(8,128)(2,1)}) all-reduce(f32[512,128]{1,0:T(8,128)S(1)} %fusion.21, f32[512,128]{1,0:T(8,128)S(1)} %fusion.24), channel_id=1, replica_groups=mesh['ctx'=128,'head'=4] {'head'}, use_global_device_ids=true, to_apply=%region_11.12 | all-reduce | flops 131072 | bytes 786432 | tf_op jit(solution)/shard_map/psum | solution.py:116
  (33 shorter events, 0.1 us)
Async XLA Ops:
  0.6 10.2 %copy-start = (bf16[512,256]{1,0:T(8,128)(2,1)S(1)}, bf16[512,256]{1,0:T(8,128)(2,1)}, u32[]{:S(2)}) copy-start(bf16[512,256]{1,0:T(8,128)(2,1)} %param.5) | copy-start | bytes 786436
  2.4 10.1 %collective-permute-start.3 = (bf16[512,128]{0,1:T(8,128)(2,1)}, bf16[512,128]{0,1:T(8,128)(2,1)S(1)}, u32[]{:S(2)}, u32[]{:S(2)}) collective-permute-start(bf16[512,128]{0,1:T(8,128)(2,1)} %copy.90), channel_id=1, source_target_pairs={{0,4},{4,8},{8,12},{12,16},{16,20},{20,24},{24,28},{28,32},{32,36}... | collective-permute-start | bytes 393224 | tf_op jit(solution)/shard_map/ppermute | solution.py:14
  4.3 10.3 %collective-permute-start = (bf16[512,128]{1,0:T(8,128)(2,1)}, bf16[512,128]{1,0:T(8,128)(2,1)}, u32[]{:S(2)}, u32[]{:S(2)}) collective-permute-start(bf16[512,128]{1,0:T(8,128)(2,1)} %param.6), channel_id=1, source_target_pairs={{0,4},{4,8},{8,12},{12,16},{16,20},{20,24},{24,28},{28,32},{32,36}... | collective-permute-start | bytes 393224 | tf_op jit(solution)/shard_map/ppermute | solution.py:14
  7.2 5.1 %copy-start.10 = (bf16[512,256]{1,0:T(8,128)(2,1)S(1)}, bf16[512,256]{1,0:T(8,128)(2,1)}, u32[]{:S(2)}) copy-start(bf16[512,256]{1,0:T(8,128)(2,1)} %param.8) | copy-start | bytes 786436
  12.4 14.0 %copy-start.11 = (pred[512,512]{0,1:T(8,128)(4,1)S(1)}, pred[512,512]{0,1:T(8,128)(4,1)}, u32[]{:S(2)}) copy-start(pred[512,512]{0,1:T(8,128)(4,1)} %get-tuple-element.23) | copy-start | bytes 786436
  12.5 7.0 %collective-permute-start.4 = (bf16[512,128]{0,1:T(8,128)(2,1)S(1)}, bf16[512,128]{0,1:T(8,128)(2,1)S(1)}, u32[]{:S(2)}, u32[]{:S(2)}) collective-permute-start(bf16[512,128]{0,1:T(8,128)(2,1)S(1)} %collective-permute-done.3), channel_id=1, source_target_pairs={{0,4},{4,8},{8,12},{12,16},{16,20},{20,24},{24,28},{28,32},{32,36}... | collective-permute-start | bytes 393224 | tf_op jit(solution)/shard_map/ppermute | solution.py:14
  14.5 6.9 %collective-permute-start.1 = (bf16[512,128]{1,0:T(8,128)(2,1)}, bf16[512,128]{1,0:T(8,128)(2,1)S(1)}, u32[]{:S(2)}, u32[]{:S(2)}) collective-permute-start(bf16[512,128]{1,0:T(8,128)(2,1)} %collective-permute-done), channel_id=1, source_target_pairs={{0,4},{4,8},{8,12},{12,16},{16,20},{20,24},{24,28},{28,32},{32,36}... | collective-permute-start | bytes 393224 | tf_op jit(solution)/shard_map/ppermute | solution.py:14
  19.5 27.2 %copy-start.1 = (f32[2,512,512]{1,2,0:T(8,128)}, f32[2,512,512]{1,2,0:T(8,128)S(1)}, u32[]{:S(2)}) copy-start(f32[2,512,512]{1,2,0:T(8,128)S(1)} %get-tuple-element.33) | copy-start | bytes 6291460
  19.5 28.2 %collective-permute-start.5 = (bf16[512,128]{0,1:T(8,128)(2,1)S(1)}, bf16[512,128]{0,1:T(8,128)(2,1)S(1)}, u32[]{:S(2)}, u32[]{:S(2)}) collective-permute-start(bf16[512,128]{0,1:T(8,128)(2,1)S(1)} %collective-permute-done.4), channel_id=1, source_target_pairs={{0,4},{4,8},{8,12},{12,16},{16,20},{20,24},{24,28},{28,32},{32,36}... | collective-permute-start | bytes 393224 | tf_op jit(solution)/shard_map/ppermute | solution.py:14
  21.5 6.8 %copy-start.12 = (bf16[512,128]{1,0:T(8,128)(2,1)}, bf16[512,128]{1,0:T(8,128)(2,1)S(1)}, u32[]{:S(2)}) copy-start(bf16[512,128]{1,0:T(8,128)(2,1)S(1)} %collective-permute-done.1) | copy-start | bytes 393220
  21.5 6.3 %collective-permute-start.2 = (bf16[512,128]{1,0:T(8,128)(2,1)S(1)}, bf16[512,128]{1,0:T(8,128)(2,1)S(1)}, u32[]{:S(2)}, u32[]{:S(2)}) collective-permute-start(bf16[512,128]{1,0:T(8,128)(2,1)S(1)} %collective-permute-done.1), channel_id=1, source_target_pairs={{0,4},{4,8},{8,12},{12,16},{16,20},{20,24},{24,28},{28,32},{32,36}... | collective-permute-start | bytes 393224 | tf_op jit(solution)/shard_map/ppermute | solution.py:14
  27.0 20.2 %copy-start.5 = (f32[2,512,512]{1,2,0:T(8,128)}, f32[2,512,512]{1,2,0:T(8,128)S(1)}, u32[]{:S(2)}) copy-start(f32[2,512,512]{1,2,0:T(8,128)S(1)} %get-tuple-element.29) | copy-start | bytes 6291460
  27.8 0.7 copy-start.15
  28.3 19.4 %copy-start.3 = (f32[2,512,512]{1,2,0:T(8,128)}, f32[2,512,512]{1,2,0:T(8,128)S(1)}, u32[]{:S(2)}) copy-start(f32[2,512,512]{1,2,0:T(8,128)S(1)} %get-tuple-element.27) | copy-start | bytes 6291460
  30.0 2.3 %copy-start.9 = (bf16[512,128]{1,0:T(8,128)(2,1)S(1)}, bf16[512,128]{1,0:T(8,128)(2,1)}, u32[]{:S(2)}) copy-start(bf16[512,128]{1,0:T(8,128)(2,1)} %param.7) | copy-start | bytes 393220
  32.9 33.2 %collective-permute-start.11 = (f32[512,128]{1,0:T(8,128)}, f32[512,128]{1,0:T(8,128)}, u32[]{:S(2)}, u32[]{:S(2)}) collective-permute-start(f32[512,128]{1,0:T(8,128)} %convolution_bitcast_fusion), channel_id=1, source_target_pairs={{12,0},{16,4},{20,8},{24,12},{28,16},{32,20},{36,24},{40,28},{44,3... | collective-permute-start | bytes 786440 | tf_op jit(solution)/shard_map/ppermute | solution.py:14
  34.8 33.5 %collective-permute-start.10 = (f32[512,128]{1,0:T(8,128)}, f32[512,128]{1,0:T(8,128)}, u32[]{:S(2)}, u32[]{:S(2)}) collective-permute-start(f32[512,128]{1,0:T(8,128)} %convolution_bitcast_fusion.1), channel_id=1, source_target_pairs={{8,0},{12,4},{16,8},{20,12},{24,16},{28,20},{32,24},{36,28},{40,32... | collective-permute-start | bytes 786440 | tf_op jit(solution)/shard_map/ppermute | solution.py:14
  38.0 30.2 %collective-permute-start.9 = (f32[512,128]{1,0:T(8,128)S(1)}, f32[512,128]{1,0:T(8,128)}, u32[]{:S(2)}, u32[]{:S(2)}) collective-permute-start(f32[512,128]{1,0:T(8,128)S(1)} %convolution_bitcast_fusion.2), channel_id=1, source_target_pairs={{4,0},{8,4},{12,8},{16,12},{20,16},{24,20},{28,24},{32,28},{36,32}... | collective-permute-start | bytes 786440 | tf_op jit(solution)/shard_map/ppermute | solution.py:14
  50.6 3.4 %copy-start.2 = (f32[2,512,512]{1,2,0:T(8,128)S(1)}, f32[2,512,512]{1,2,0:T(8,128)}, u32[]{:S(2)}) copy-start(f32[2,512,512]{1,2,0:T(8,128)} %copy-done.1) | copy-start | bytes 6291460
  54.0 6.4 %copy-start.6 = (bf16[2,512,512]{1,2,0:T(8,128)(2,1)S(1)}, bf16[2,512,512]{1,2,0:T(8,128)(2,1)}, u32[]{:S(2)}) copy-start(bf16[2,512,512]{1,2,0:T(8,128)(2,1)} %fusion.7) | copy-start | bytes 3145732
  54.0 6.4 %copy-start.14 = (bf16[512,128]{1,0:T(8,128)(2,1)S(1)}, bf16[512,128]{1,0:T(8,128)(2,1)}, u32[]{:S(2)}) copy-start(bf16[512,128]{1,0:T(8,128)(2,1)} %param.6) | copy-start | bytes 393220
  54.5 6.2 %copy-start.4 = (f32[2,512,512]{1,2,0:T(8,128)S(1)}, f32[2,512,512]{1,2,0:T(8,128)}, u32[]{:S(2)}) copy-start(f32[2,512,512]{1,2,0:T(8,128)} %copy-done.3) | copy-start | bytes 6291460
  55.7 14.1 %collective-permute-start.6 = (f32[512,128]{1,0:T(8,128)}, f32[512,128]{1,0:T(8,128)S(1)}, u32[]{:S(2)}, u32[]{:S(2)}) collective-permute-start(f32[512,128]{1,0:T(8,128)} %fusion.17), channel_id=1, source_target_pairs={{4,0},{8,4},{12,8},{16,12},{20,16},{24,20},{28,24},{32,28},{36,32}... | collective-permute-start | bytes 786440 | tf_op jit(solution)/shard_map/ppermute | solution.py:14
  57.6 13.0 %collective-permute-start.7 = (f32[512,128]{1,0:T(8,128)}, f32[512,128]{1,0:T(8,128)}, u32[]{:S(2)}, u32[]{:S(2)}) collective-permute-start(f32[512,128]{1,0:T(8,128)} %fusion.16), channel_id=1, source_target_pairs={{8,0},{12,4},{16,8},{20,12},{24,16},{28,20},{32,24},{36,28},{40,32... | collective-permute-start | bytes 786440 | tf_op jit(solution)/shard_map/ppermute | solution.py:14
  60.8 2.0 %copy-start.13 = (bf16[512,128]{1,0:T(8,128)(2,1)S(1)}, bf16[512,128]{1,0:T(8,128)(2,1)}, u32[]{:S(2)}) copy-start(bf16[512,128]{1,0:T(8,128)(2,1)} %copy-done.12) | copy-start | bytes 393220
  61.3 1.9 %copy-start.8 = (bf16[2,512,512]{1,2,0:T(8,128)(2,1)}, bf16[2,512,512]{1,2,0:T(8,128)(2,1)S(1)}, u32[]{:S(2)}) copy-start(bf16[2,512,512]{1,2,0:T(8,128)(2,1)S(1)} %fusion.1) | copy-start | bytes 3145732
  61.3 1.9 %copy-start.16 = (bf16[512,128]{1,0:T(8,128)(2,1)S(1)}, bf16[512,128]{1,0:T(8,128)(2,1)}, u32[]{:S(2)}) copy-start(bf16[512,128]{1,0:T(8,128)(2,1)} %copy-done.15) | copy-start | bytes 393220
  66.1 13.0 %copy-start.7 = (bf16[2,512,512]{1,2,0:T(8,128)(2,1)S(1)}, bf16[2,512,512]{1,2,0:T(8,128)(2,1)}, u32[]{:S(2)}) copy-start(bf16[2,512,512]{1,2,0:T(8,128)(2,1)} %fusion.7) | copy-start | bytes 3145732
  66.1 12.9 %collective-permute-start.8 = (f32[512,128]{1,0:T(8,128)S(1)}, f32[512,128]{1,0:T(8,128)S(1)}, u32[]{:S(2)}, u32[]{:S(2)}) collective-permute-start(f32[512,128]{1,0:T(8,128)S(1)} %fusion.15), channel_id=1, source_target_pairs={{12,0},{16,4},{20,8},{24,12},{28,16},{32,20},{36,24},{40,28},{44,3... | collective-permute-start | bytes 786440 | tf_op jit(solution)/shard_map/ppermute | solution.py:14
where the time goes:
time: 104 us
  starting transfers between devices  37.9 us (36%)
  blocking collectives  23.4 us (22%)
  matrix products  22.9 us (22%)
  waiting for transfers between devices  9.98 us (10%)
  local copies, waits for them, and re-layouts  4.51 us (4%)
  other arithmetic  3.91 us (4%)
  between operations  1.17 us (1%)
    ppermute x12, starting transfers between devices, passed_along(): lax.ppermute(value, axis, [(source, source + steps) for source in range(l...  37.9 us
    psum x1, blocking collectives, on_device(): key_total, value_total = lax.psum((key_total, value_total), 'head')  23.4 us
    ppermute x12, waiting for transfers between devices, passed_along(): lax.ppermute(value, axis, [(source, source + steps) for source in range(l...  9.98 us
    dot_general x4, matrix products, backward_tile(): jnp.einsum('htj,thd->jd', d_scores, query_heads, preferred_element_type=j...  5.32 us
    dot_general x4, matrix products, backward_tile(): jnp.einsum('thd,jd->htj', grad_heads, value_block, preferred_element_type...  4.74 us
    dot_general x4, matrix products, backward_tile(): jnp.einsum('htj,thd->jd', weights, grad_heads, preferred_element_type=jnp...  4.32 us
    dot_general x4, matrix products, scores_for(): jnp.einsum('thd,jd->htj', query_heads, kv_blocks[offset][0], preferred_el...  3.98 us
    unnamed x38, local copies, waits for them, and re-layouts  3.7 us
  transfers between devices with their start and end apart: 12, of which 3 were waited for; matrix products, arithmetic and copies ran while one was open for 27% of the time, Pallas kernels for 0%

commit v1 on v0

v1 whole, which is shorter than its diff:
```python
import functools
import math

import jax
import jax.numpy as jnp
from jax import lax
from jax.experimental import pallas as pl
from jax.experimental.pallas import tpu as pltpu
from jax.sharding import PartitionSpec as P

SPAN = 3
TILE = 256
BF = jnp.bfloat16
F32 = jnp.float32


def dot_nt(a, b):
    return lax.dot_general(a, b, (((1,), (1,)), ((), ())), preferred_element_type=F32)


def dot_nn(a, b):
    return jnp.dot(a, b, preferred_element_type=F32)


def attention_kernel(
    place_ref,
    lengths_ref,
    q_ref,
    do_ref,
    own_ref,
    two_ref,
    mixed_ref,
    swapped_ref,
    att_ref,
    dq_ref,
    own_part_ref,
    two_part_ref,
    mixed_part_ref,
    swapped_part_ref,
    window,
    parts,
    tiles,
    starts,
    top,
    total,
    out_sum,
    dq_sum,
    qt,
    dot_,
):
    rows, width = q_ref.shape
    head = own_ref.shape[1] // 2
    heads = width // head
    lead = SPAN * rows
    n_tiles = (lead + rows) // TILE
    scale = 1.0 / math.sqrt(head)
    to_exp2 = scale * math.log2(math.e)
    device = place_ref[0]
    odd = lax.rem(device, 2)
    mixed_row = pl.multiple_of(jnp.where(odd == 1, lead - rows, 0), rows)
    swapped_row = pl.multiple_of(jnp.where(odd == 1, 0, lead - rows), rows)

    window[pl.ds(lead, rows), :] = own_ref[...]
    window[pl.ds(lead - 2 * rows, rows), :] = two_ref[...]
    window[pl.ds(mixed_row, rows), :] = mixed_ref[...]
    window[pl.ds(swapped_row, rows), :] = swapped_ref[...]

    lengths = lengths_ref[...]
    docs = lengths.shape[1]
    along = jnp.broadcast_to(lengths.astype(F32), (docs, docs))
    earlier = lax.broadcasted_iota(jnp.int32, (docs, docs), 0)
    later = lax.broadcasted_iota(jnp.int32, (docs, docs), 1)
    ends = jnp.sum(jnp.where(earlier <= later, along.T, 0.0), axis=0, keepdims=True)
    first = (device * rows).astype(F32)
    positions = first + lax.broadcasted_iota(jnp.int32, (rows, docs), 0).astype(F32)
    doc_start = jnp.sum(
        jnp.where(ends <= positions, lengths.astype(F32), 0.0), axis=1, keepdims=True
    )
    start_row = (doc_start - (first - lead)).astype(jnp.int32)
    starts[...] = jnp.broadcast_to(start_row, (rows, TILE))
    low = jnp.minimum(jnp.maximum(jnp.min(start_row), 0) // TILE, n_tiles - 1)

    top[...] = jnp.full(top.shape, -jnp.inf, F32)
    total[...] = jnp.zeros(total.shape, F32)
    out_sum[...] = jnp.zeros(out_sum.shape, F32)
    dq_sum[...] = jnp.zeros(dq_sum.shape, F32)
    for h in range(heads):
        cols = pl.ds(h * head, head)
        qt[h] = q_ref[:, cols].T
        dot_[h] = do_ref[:, cols].T

    column = lax.broadcasted_iota(jnp.int32, (rows, TILE), 1)
    row = lax.broadcasted_iota(jnp.int32, (rows, TILE), 0) + lead

    def score_tile(t, carry):
        at = pl.multiple_of(t * TILE, TILE)
        keys = window[pl.ds(at, TILE), pl.ds(0, head)]
        key = column + t * TILE
        allowed = (key >= starts[...]) & (key <= row)
        for h in range(heads):
            s = dot_nt(q_ref[:, pl.ds(h * head, head)], keys)
            s = jnp.where(allowed, s, -jnp.inf)
            tiles[h, t] = s
            m = top[h]
            for c in range(0, TILE, head):
                m = jnp.maximum(m, s[:, c : c + head])
            top[h] = m
        return carry

    lax.fori_loop(low, n_tiles, score_tile, 0)

    for h in range(heads):
        top[h] = jnp.broadcast_to(jnp.max(top[h], axis=1, keepdims=True), (rows, head))

    def wide(x):
        return jnp.concatenate([x] * (TILE // head), axis=1)

    def out_tile(t, carry):
        at = pl.multiple_of(t * TILE, TILE)
        values = window[pl.ds(at, TILE), pl.ds(head, head)]
        for h in range(heads):
            e = jnp.exp2((tiles[h, t] - wide(top[h])) * to_exp2)
            tiles[h, t] = e
            m = total[h]
            for c in range(0, TILE, head):
                m = m + e[:, c : c + head]
            total[h] = m
            out_sum[h] += dot_nn(e.astype(BF), values)
        return carry

    lax.fori_loop(low, n_tiles, out_tile, 0)

    for h in range(heads):
        cols = pl.ds(h * head, head)
        inverse = 1.0 / jnp.sum(total[h], axis=1, keepdims=True)
        attended = (out_sum[h] * inverse).astype(BF)
        att_ref[:, cols] = attended
        row_dot = jnp.sum(
            do_ref[:, cols].astype(F32) * attended.astype(F32), axis=1, keepdims=True
        )
        total[h] = jnp.broadcast_to(inverse, (rows, head))
        top[h] = jnp.broadcast_to(row_dot, (rows, head))

    def zero_tile(t, carry):
        at = pl.multiple_of(t * TILE, TILE)
        parts[pl.ds(at, TILE), :] = jnp.zeros((TILE, 2 * head), BF)
        return carry

    lax.fori_loop(0, low, zero_tile, 0)

    def grad_tile(t, carry):
        at = pl.multiple_of(t * TILE, TILE)
        keys = window[pl.ds(at, TILE), pl.ds(0, head)]
        values = window[pl.ds(at, TILE), pl.ds(head, head)]
        dv = jnp.zeros((head, TILE), F32)
        dk = jnp.zeros((head, TILE), F32)
        for h in range(heads):
            dw = dot_nt(do_ref[:, pl.ds(h * head, head)], values)
            w = tiles[h, t] * wide(total[h])
            ds = (w * (dw - wide(top[h]))).astype(BF)
            dv = dv + dot_nn(dot_[h], w.astype(BF))
            dk = dk + dot_nn(qt[h], ds)
            dq_sum[h] += dot_nn(ds, keys)
        parts[pl.ds(at, TILE), pl.ds(0, head)] = (dk * scale).T.astype(BF)
        parts[pl.ds(at, TILE), pl.ds(head, head)] = dv.T.astype(BF)
        return carry

    lax.fori_loop(low, n_tiles, grad_tile, 0)

    for h in range(heads):
        dq_ref[:, pl.ds(h * head, head)] = (dq_sum[h] * scale).astype(BF)
    own_part_ref[...] = parts[pl.ds(lead, rows), :]
    two_part_ref[...] = parts[pl.ds(lead - 2 * rows, rows), :]
    mixed_part_ref[...] = parts[pl.ds(mixed_row, rows), :]
    swapped_part_ref[...] = parts[pl.ds(swapped_row, rows), :]


def attention(place, lengths, q, do, own, two, mixed, swapped):
    rows, width = q.shape
    head = own.shape[1] // 2
    heads = width // head
    span = (SPAN + 1) * rows
    vmem = pl.BlockSpec(memory_space=pltpu.VMEM)
    like_q = jax.ShapeDtypeStruct(q.shape, BF)
    like_kv = jax.ShapeDtypeStruct(own.shape, BF)
    return pl.pallas_call(
        attention_kernel,
        out_shape=(like_q, like_q) + (like_kv,) * 4,
        in_specs=[pl.BlockSpec(memory_space=pltpu.SMEM)] + [vmem] * 7,
        out_specs=(vmem,) * 6,
        scratch_shapes=[
            pltpu.VMEM((span, 2 * head), BF),
            pltpu.VMEM((span, 2 * head), BF),
            pltpu.VMEM((heads, span // TILE, rows, TILE), F32),
            pltpu.VMEM((rows, TILE), jnp.int32),
            pltpu.VMEM((heads, rows, head), F32),
            pltpu.VMEM((heads, rows, head), F32),
            pltpu.VMEM((heads, rows, head), F32),
            pltpu.VMEM((heads, rows, head), F32),
            pltpu.VMEM((heads, head, rows), BF),
            pltpu.VMEM((heads, head, rows), BF),
        ],
        compiler_params=pltpu.CompilerParams(vmem_limit_bytes=40 << 20),
        cost_estimate=pl.CostEstimate(
            flops=6_000_000_000, bytes_accessed=4 << 20, transcendentals=2 << 20
        ),
        name="attention",
    )(place, lengths, q, do, own, two, mixed, swapped)


def moved(value, pairs):
    return lax.ppermute(value, "ctx", pairs)


def on_device(queries, keys, values, d_out, doc_lengths):
    count = lax.axis_size("ctx")
    head = keys.shape[1]
    place = lax.axis_index("ctx").reshape(1).astype(jnp.int32)
    two_on = [(i, i + 2) for i in range(count - 2)]
    mixed_on = [(i, i + (3 if i % 2 else 1)) for i in range(count) if i + (3 if i % 2 else 1) < count]
    across = [(i, i ^ 1) for i in range(count)]

    def back(pairs):
        return [(there, here) for here, there in pairs]

    own = jnp.concatenate([keys, values], axis=1)
    two = moved(own, two_on)
    mixed = moved(own, mixed_on)
    swapped = moved(two, across)
    attended, d_queries, own_part, two_part, mixed_part, swapped_part = attention(
        place, doc_lengths.reshape(1, -1), queries, d_out, own, two, mixed, swapped
    )
    from_core = moved(swapped_part, across)
    from_mixed = moved(mixed_part, back(mixed_on))
    passed = (two_part.astype(F32) + from_core.astype(F32)).astype(BF)
    from_two = moved(passed, back(two_on))
    mine = (own_part.astype(F32) + from_mixed.astype(F32) + from_two.astype(F32)).astype(BF)
    everyone = lax.all_gather(mine, "head", axis=0)
    summed = jnp.sum(everyone.astype(F32), axis=0).astype(BF)
    return (attended, d_queries, summed[:, :head], summed[:, head:])


def solution(mesh):
    in_specs = (P("ctx", "head"), P("ctx", None), P("ctx", None), P("ctx", "head"), P())
    out_specs = (P("ctx", "head"), P("ctx", "head"), P("ctx", None), P("ctx", None))
    return jax.shard_map(
        on_device, mesh=mesh, in_specs=in_specs, out_specs=out_specs, check_vma=False
    )
```

time: 104 us -> 100 us (0.962)
  the two profiles are of different devices: /device:TPU:390 before, /device:TPU:2 now
where the time goes in v1:
time: 100 us; the launch traced here: 99.8 us
  waiting for transfers between devices  59.3 us (59%)
  starting transfers between devices  14.8 us (15%)
  between operations  14.1 us (14%)
  Pallas kernels  5.95 us (6%)
  local copies, waits for them, and re-layouts  3.29 us (3%)
  other arithmetic  2.33 us (2%)
    all_gather x1, waiting for transfers between devices, on_device(): everyone = lax.all_gather(mine, 'head', axis=0)  37.5 us
    ppermute x6, waiting for transfers between devices, moved(): return lax.ppermute(value, 'ctx', pairs)  21.8 us
    ppermute x6, starting transfers between devices, moved(): return lax.ppermute(value, 'ctx', pairs)  14.7 us
    pallas_call x1, Pallas kernels, attention(): pl.pallas_call(attention_kernel, out_shape=(like_q, like_q) + (like_kv,)...  5.95 us
  transfers between devices with their start and end apart: 7, of which 5 were waited for; matrix products, arithmetic and copies ran while one was open for 0% of the time, Pallas kernels for 0%

profile of v1, /device:TPU:2, one launch (start us, length us, event | category | flops | bytes accessed | tf_op | source)
XLA Modules:
  0.0 99.8 jit_solution(6253352681049433177)
XLA Ops:
  7.2 0.0 copy-start.1
  7.2 0.0 copy-start
  7.2 0.0 all-gather.3.cloned.1.call-start
  7.2 1.0 constant_dynamic-update-slice_fusion.1
  8.2 0.9 constant_dynamic-update-slice_fusion.own_ref
  9.1 3.4 %collective-permute-start = (bf16[512,256]{1,0:T(8,128)(2,1)S(1)}, bf16[512,256]{1,0:T(8,128)(2,1)S(1)}, u32[]{:S(2)}, u32[]{:S(2)}) collective-permute-start(bf16[512,256]{1,0:T(8,128)(2,1)S(1)} %constant_dynamic-update-slice_fusion.own_ref), channel_id=1, source_target_pairs={{0,8},{4,12},{8,16},{12,20},{16,24},{20,28},{24,32},{28,36},{32,40... | collective-permute-start | bytes 786440 | tf_op jit(solution)/shard_map/ppermute | solution.py:212
  12.6 1.5 %collective-permute-start.1 = (bf16[512,256]{1,0:T(8,128)(2,1)S(1)}, bf16[512,256]{1,0:T(8,128)(2,1)S(1)}, u32[]{:S(2)}, u32[]{:S(2)}) collective-permute-start(bf16[512,256]{1,0:T(8,128)(2,1)S(1)} %constant_dynamic-update-slice_fusion.own_ref), channel_id=1, source_target_pairs={{0,4},{4,16},{8,12},{12,24},{16,20},{20,32},{24,28},{28,40},{32,36... | collective-permute-start | bytes 786440 | tf_op jit(solution)/shard_map/ppermute | solution.py:212
  14.0 8.7 %collective-permute-done.two_ref = bf16[512,256]{1,0:T(8,128)(2,1)S(1)} collective-permute-done((bf16[512,256]{1,0:T(8,128)(2,1)S(1)}, bf16[512,256]{1,0:T(8,128)(2,1)S(1)}, u32[]{:S(2)}, u32[]{:S(2)}) %collective-permute-start) | collective-permute-done | bytes 262176 | tf_op jit(solution)/shard_map/ppermute | solution.py:212
  22.7 1.9 %collective-permute-start.2 = (bf16[512,256]{1,0:T(8,128)(2,1)S(1)}, bf16[512,256]{1,0:T(8,128)(2,1)S(1)}, u32[]{:S(2)}, u32[]{:S(2)}) collective-permute-start(bf16[512,256]{1,0:T(8,128)(2,1)S(1)} %collective-permute-done.two_ref), channel_id=1, source_target_pairs={{0,4},{4,0},{8,12},{12,8},{16,20},{20,16},{24,28},{28,24},{32,36},... | collective-permute-start | bytes 786440 | tf_op jit(solution)/shard_map/ppermute | solution.py:212
  24.6 0.0 collective-permute-done.1.mixed_ref
  24.6 1.5 %collective-permute-done.2.swapped_ref = bf16[512,256]{1,0:T(8,128)(2,1)S(1)} collective-permute-done((bf16[512,256]{1,0:T(8,128)(2,1)S(1)}, bf16[512,256]{1,0:T(8,128)(2,1)S(1)}, u32[]{:S(2)}, u32[]{:S(2)}) %collective-permute-start.2) | collective-permute-done | bytes 262176 | tf_op jit(solution)/shard_map/ppermute | solution.py:212
  26.1 0.0 copy-start.2
  26.1 0.0 copy-done.1
  26.1 0.0 copy-done
  26.1 0.6 copy-done.2
  26.8 5.9 %attention.1 = (bf16[512,256]{1,0:T(8,128)(2,1)}, bf16[512,256]{1,0:T(8,128)(2,1)}, bf16[512,256]{1,0:T(8,128)(2,1)S(1)}, bf16[512,256]{1,0:T(8,128)(2,1)S(1)}, ...) custom-call(s32[1]{0:T(128)} %bitcast.place_ref, s32[1,128]{1,0:T(1,128)S(1)} %bitcast.3, ...), custom_call_target="tpu_custom_call" | custom-call | flops 6000000000 | bytes 4194304 | tf_op jit(solution)/shard_map/attention/pallas_call | solution.py:186
  32.7 4.7 %collective-permute-start.4 = (bf16[512,256]{1,0:T(8,128)(2,1)S(1)}, bf16[512,256]{1,0:T(8,128)(2,1)S(1)}, u32[]{:S(2)}, u32[]{:S(2)}) collective-permute-start(bf16[512,256]{1,0:T(8,128)(2,1)S(1)} %get-tuple-element.15), channel_id=1, source_target_pairs={{0,4},{4,0},{8,12},{12,8},{16,20},{20,16},{24,28},{28,24},{32,36},... | collective-permute-start | bytes 786440 | tf_op jit(solution)/shard_map/ppermute | solution.py:212
  37.5 1.3 %collective-permute-start.3 = (bf16[512,256]{1,0:T(8,128)(2,1)S(1)}, bf16[512,256]{1,0:T(8,128)(2,1)S(1)}, u32[]{:S(2)}, u32[]{:S(2)}) collective-permute-start(bf16[512,256]{1,0:T(8,128)(2,1)S(1)} %get-tuple-element.13), channel_id=1, source_target_pairs={{4,0},{16,4},{12,8},{24,12},{20,16},{32,20},{28,24},{40,28},{36,32... | collective-permute-start | bytes 786440 | tf_op jit(solution)/shard_map/ppermute | solution.py:212
  38.8 0.0 collective-permute-done.4
  38.8 0.1 add_convert_fusion.1
  38.9 1.9 %collective-permute-start.5 = (bf16[512,256]{1,0:T(8,128)(2,1)S(1)}, bf16[512,256]{1,0:T(8,128)(2,1)S(1)}, u32[]{:S(2)}, u32[]{:S(2)}) collective-permute-start(bf16[512,256]{1,0:T(8,128)(2,1)S(1)} %add_convert_fusion.1), channel_id=1, source_target_pairs={{8,0},{12,4},{16,8},{20,12},{24,16},{28,20},{32,24},{36,28},{40,32... | collective-permute-start | bytes 786440 | tf_op jit(solution)/shard_map/ppermute | solution.py:212
  40.8 0.1 collective-permute-done.3
  40.9 11.6 %collective-permute-done.5 = bf16[512,256]{1,0:T(8,128)(2,1)S(1)} collective-permute-done((bf16[512,256]{1,0:T(8,128)(2,1)S(1)}, bf16[512,256]{1,0:T(8,128)(2,1)S(1)}, u32[]{:S(2)}, u32[]{:S(2)}) %collective-permute-start.5) | collective-permute-done | bytes 262176 | tf_op jit(solution)/shard_map/ppermute | solution.py:212
  52.5 0.8 add_convert_fusion
  53.3 0.0 all-gather.3.cloned.1.call-update
  53.3 37.5 %all-gather.3.cloned.1.call-done = bf16[2048,256]{1,0:T(8,128)(2,1)} async-done(((bf16[512,256]{1,0:T(8,128)(2,1)}), bf16[2048,256]{1,0:T(8,128)(2,1)}) %all-gather.3.cloned.1.call-update) | async-done | bytes 1048592 | tf_op jit(solution)/shard_map/all_gather | solution.py:238
  90.8 1.5 %reduce_sum.12 = bf16[512,256]{1,0:T(8,128)(2,1)S(1)} reduce(bf16[4,512,256]{2,1,0:T(8,128)(2,1)} %bitcast.4, bf16[]{:T(256)} %constant.8.clone.1), dimensions={0}, to_apply=%region_0.0 | reduce | flops 393216 | bytes 1310722 | tf_op jit(solution)/shard_map/reduce_sum | solution.py:239
  92.2 0.7 fusion
Async XLA Ops:
  7.2 19.0 %copy-start.1 = (bf16[512,256]{1,0:T(8,128)(2,1)S(1)}, bf16[512,256]{1,0:T(8,128)(2,1)}, u32[]{:S(2)}) copy-start(bf16[512,256]{1,0:T(8,128)(2,1)} %do_ref.1) | copy-start | bytes 786436
  7.2 19.0 %copy-start = (bf16[512,256]{1,0:T(8,128)(2,1)S(1)}, bf16[512,256]{1,0:T(8,128)(2,1)}, u32[]{:S(2)}) copy-start(bf16[512,256]{1,0:T(8,128)(2,1)} %q_ref.1) | copy-start | bytes 786436
  7.2 83.6 %all-gather.3.cloned.1.call-start = ((), (), s32[]{:S(2)}) async-start(), calls=%async_computation | async-start | bytes 1310720 | tf_op jit(solution)/shard_map/all_gather | solution.py:238
  9.1 13.6 %collective-permute-start = (bf16[512,256]{1,0:T(8,128)(2,1)S(1)}, bf16[512,256]{1,0:T(8,128)(2,1)S(1)}, u32[]{:S(2)}, u32[]{:S(2)}) collective-permute-start(bf16[512,256]{1,0:T(8,128)(2,1)S(1)} %constant_dynamic-update-slice_fusion.own_ref), channel_id=1, source_target_pairs={{0,8},{4,12},{8,16},{12,20},{16,24},{20,28},{24,32},{28,36},{32,40... | collective-permute-start | bytes 786440 | tf_op jit(solution)/shard_map/ppermute | solution.py:212
  12.6 12.1 %collective-permute-start.1 = (bf16[512,256]{1,0:T(8,128)(2,1)S(1)}, bf16[512,256]{1,0:T(8,128)(2,1)S(1)}, u32[]{:S(2)}, u32[]{:S(2)}) collective-permute-start(bf16[512,256]{1,0:T(8,128)(2,1)S(1)} %constant_dynamic-update-slice_fusion.own_ref), channel_id=1, source_target_pairs={{0,4},{4,16},{8,12},{12,24},{16,20},{20,32},{24,28},{28,40},{32,36... | collective-permute-start | bytes 786440 | tf_op jit(solution)/shard_map/ppermute | solution.py:212
  22.7 3.4 %collective-permute-start.2 = (bf16[512,256]{1,0:T(8,128)(2,1)S(1)}, bf16[512,256]{1,0:T(8,128)(2,1)S(1)}, u32[]{:S(2)}, u32[]{:S(2)}) collective-permute-start(bf16[512,256]{1,0:T(8,128)(2,1)S(1)} %collective-permute-done.two_ref), channel_id=1, source_target_pairs={{0,4},{4,0},{8,12},{12,8},{16,20},{20,16},{24,28},{28,24},{32,36},... | collective-permute-start | bytes 786440 | tf_op jit(solution)/shard_map/ppermute | solution.py:212
  26.1 0.7 copy-start.2
  32.7 6.0 %collective-permute-start.4 = (bf16[512,256]{1,0:T(8,128)(2,1)S(1)}, bf16[512,256]{1,0:T(8,128)(2,1)S(1)}, u32[]{:S(2)}, u32[]{:S(2)}) collective-permute-start(bf16[512,256]{1,0:T(8,128)(2,1)S(1)} %get-tuple-element.15), channel_id=1, source_target_pairs={{0,4},{4,0},{8,12},{12,8},{16,20},{20,16},{24,28},{28,24},{32,36},... | collective-permute-start | bytes 786440 | tf_op jit(solution)/shard_map/ppermute | solution.py:212
  37.5 3.4 %collective-permute-start.3 = (bf16[512,256]{1,0:T(8,128)(2,1)S(1)}, bf16[512,256]{1,0:T(8,128)(2,1)S(1)}, u32[]{:S(2)}, u32[]{:S(2)}) collective-permute-start(bf16[512,256]{1,0:T(8,128)(2,1)S(1)} %get-tuple-element.13), channel_id=1, source_target_pairs={{4,0},{16,4},{12,8},{24,12},{20,16},{32,20},{28,24},{40,28},{36,32... | collective-permute-start | bytes 786440 | tf_op jit(solution)/shard_map/ppermute | solution.py:212
  38.9 13.6 %collective-permute-start.5 = (bf16[512,256]{1,0:T(8,128)(2,1)S(1)}, bf16[512,256]{1,0:T(8,128)(2,1)S(1)}, u32[]{:S(2)}, u32[]{:S(2)}) collective-permute-start(bf16[512,256]{1,0:T(8,128)(2,1)S(1)} %add_convert_fusion.1), channel_id=1, source_target_pairs={{8,0},{12,4},{16,8},{20,12},{24,16},{28,20},{32,24},{36,28},{40,32... | collective-permute-start | bytes 786440 | tf_op jit(solution)/shard_map/ppermute | solution.py:212
Sparse Core Ops, SparseCore 0:
  53.4 37.2 all-gather.2

commit v2 on v1

--- a/solution.py
+++ b/solution.py
@@ -37,8 +37,10 @@
     two_part_ref,
     mixed_part_ref,
     swapped_part_ref,
-    window,
-    parts,
+    key_window,
+    value_window,
+    key_parts,
+    value_parts,
     tiles,
     starts,
     top,
@@ -49,7 +51,7 @@
     dot_,
 ):
     rows, width = q_ref.shape
-    head = own_ref.shape[1] // 2
+    head = own_ref.shape[1]
     heads = width // head
     lead = SPAN * rows
     n_tiles = (lead + rows) // TILE
@@ -60,10 +62,15 @@
     mixed_row = pl.multiple_of(jnp.where(odd == 1, lead - rows, 0), rows)
     swapped_row = pl.multiple_of(jnp.where(odd == 1, 0, lead - rows), rows)
 
-    window[pl.ds(lead, rows), :] = own_ref[...]
-    window[pl.ds(lead - 2 * rows, rows), :] = two_ref[...]
-    window[pl.ds(mixed_row, rows), :] = mixed_ref[...]
-    window[pl.ds(swapped_row, rows), :] = swapped_ref[...]
+    slots = (
+        (own_ref, own_part_ref, lead),
+        (two_ref, two_part_ref, lead - 2 * rows),
+        (mixed_ref, mixed_part_ref, mixed_row),
+        (swapped_ref, swapped_part_ref, swapped_row),
+    )
+    for block, _, at in slots:
+        key_window[pl.ds(at, rows), :] = block[pl.ds(0, rows), :]
+        value_window[pl.ds(at, rows), :] = block[pl.ds(rows, rows), :]
 
     lengths = lengths_ref[...]
     docs = lengths.shape[1]
@@ -94,7 +101,7 @@
 
     def score_tile(t, carry):
         at = pl.multiple_of(t * TILE, TILE)
-        keys = window[pl.ds(at, TILE), pl.ds(0, head)]
+        keys = key_window[pl.ds(at, TILE), :]
         key = column + t * TILE
         allowed = (key >= starts[...]) & (key <= row)
         for h in range(heads):
@@ -117,7 +124,7 @@
 
     def out_tile(t, carry):
         at = pl.multiple_of(t * TILE, TILE)
-        values = window[pl.ds(at, TILE), pl.ds(head, head)]
+        values = value_window[pl.ds(at, TILE), :]
         for h in range(heads):
             e = jnp.exp2((tiles[h, t] - wide(top[h])) * to_exp2)
             tiles[h, t] = e
@@ -143,15 +150,16 @@
 
     def zero_tile(t, carry):
         at = pl.multiple_of(t * TILE, TILE)
-        parts[pl.ds(at, TILE), :] = jnp.zeros((TILE, 2 * head), BF)
+        key_parts[pl.ds(at, TILE), :] = jnp.zeros((TILE, head), BF)
+        value_parts[pl.ds(at, TILE), :] = jnp.zeros((TILE, head), BF)
         return carry
 
     lax.fori_loop(0, low, zero_tile, 0)
 
     def grad_tile(t, carry):
         at = pl.multiple_of(t * TILE, TILE)
-        keys = window[pl.ds(at, TILE), pl.ds(0, head)]
-        values = window[pl.ds(at, TILE), pl.ds(head, head)]
+        keys = key_window[pl.ds(at, TILE), :]
+        values = value_window[pl.ds(at, TILE), :]
         dv = jnp.zeros((head, TILE), F32)
         dk = jnp.zeros((head, TILE), F32)
         for h in range(heads):
@@ -161,23 +169,22 @@
             dv = dv + dot_nn(dot_[h], w.astype(BF))
             dk = dk + dot_nn(qt[h], ds)
             dq_sum[h] += dot_nn(ds, keys)
-        parts[pl.ds(at, TILE), pl.ds(0, head)] = (dk * scale).T.astype(BF)
-        parts[pl.ds(at, TILE), pl.ds(head, head)] = dv.T.astype(BF)
+        key_parts[pl.ds(at, TILE), :] = (dk * scale).T.astype(BF)
+        value_parts[pl.ds(at, TILE), :] = dv.T.astype(BF)
         return carry
 
     lax.fori_loop(low, n_tiles, grad_tile, 0)
 
     for h in range(heads):
         dq_ref[:, pl.ds(h * head, head)] = (dq_sum[h] * scale).astype(BF)
-    own_part_ref[...] = parts[pl.ds(lead, rows), :]
-    two_part_ref[...] = parts[pl.ds(lead - 2 * rows, rows), :]
-    mixed_part_ref[...] = parts[pl.ds(mixed_row, rows), :]
-    swapped_part_ref[...] = parts[pl.ds(swapped_row, rows), :]
+    for _, part, at in slots:
+        part[pl.ds(0, rows), :] = key_parts[pl.ds(at, rows), :]
+        part[pl.ds(rows, rows), :] = value_parts[pl.ds(at, rows), :]
 
 
 def attention(place, lengths, q, do, own, two, mixed, swapped):
     rows, width = q.shape
-    head = own.shape[1] // 2
+    head = own.shape[1]
     heads = width // head
     span = (SPAN + 1) * rows
     vmem = pl.BlockSpec(memory_space=pltpu.VMEM)
@@ -189,8 +196,10 @@
         in_specs=[pl.BlockSpec(memory_space=pltpu.SMEM)] + [vmem] * 7,
         out_specs=(vmem,) * 6,
         scratch_shapes=[
-            pltpu.VMEM((span, 2 * head), BF),
-            pltpu.VMEM((span, 2 * head), BF),
+            pltpu.VMEM((span, head), BF),
+            pltpu.VMEM((span, head), BF),
+            pltpu.VMEM((span, head), BF),
+            pltpu.VMEM((span, head), BF),
             pltpu.VMEM((heads, span // TILE, rows, TILE), F32),
             pltpu.VMEM((rows, TILE), jnp.int32),
             pltpu.VMEM((heads, rows, head), F32),
@@ -208,13 +217,46 @@
     )(place, lengths, q, do, own, two, mixed, swapped)
 
 
+def pack_kernel(key_ref, value_ref, both_ref, sems):
+    rows = key_ref.shape[0]
+    copies = [
+        pltpu.make_async_copy(key_ref, both_ref.at[pl.ds(0, rows)], sems.at[0]),
+        pltpu.make_async_copy(value_ref, both_ref.at[pl.ds(rows, rows)], sems.at[1]),
+    ]
+    for copy in copies:
+        copy.start()
+    for copy in copies:
+        copy.wait()
+
+
+def packed(keys, values):
+    rows, head = keys.shape
+    return pl.pallas_call(
+        pack_kernel,
+        out_shape=jax.ShapeDtypeStruct((2 * rows, head), BF),
+        in_specs=[pl.BlockSpec(memory_space=pl.ANY)] * 2,
+        out_specs=pl.BlockSpec(memory_space=pltpu.VMEM),
+        scratch_shapes=[pltpu.SemaphoreType.DMA((2,))],
+        name="pack",
+    )(keys, values)
+
+
+def head_sum(part):
+    heads = lax.axis_size("head")
+    pieces = part.reshape(heads, part.shape[0] // heads, part.shape[1])
+    theirs = lax.all_to_all(pieces, "head", split_axis=0, concat_axis=0)
+    mine = jnp.sum(theirs.astype(F32), axis=0).astype(BF)
+    mine = jnp.broadcast_to(mine[None], pieces.shape)
+    return lax.all_to_all(mine, "head", split_axis=0, concat_axis=0).reshape(part.shape)
+
+
 def moved(value, pairs):
     return lax.ppermute(value, "ctx", pairs)
 
 
 def on_device(queries, keys, values, d_out, doc_lengths):
     count = lax.axis_size("ctx")
-    head = keys.shape[1]
+    rows = keys.shape[0]
     place = lax.axis_index("ctx").reshape(1).astype(jnp.int32)
     two_on = [(i, i + 2) for i in range(count - 2)]
     mixed_on = [(i, i + (3 if i % 2 else 1)) for i in range(count) if i + (3 if i % 2 else 1) < count]
@@ -223,7 +265,7 @@
     def back(pairs):
         return [(there, here) for here, there in pairs]
 
-    own = jnp.concatenate([keys, values], axis=1)
+    own = packed(keys, values)
     two = moved(own, two_on)
     mixed = moved(own, mixed_on)
     swapped = moved(two, across)
@@ -235,9 +277,8 @@
     passed = (two_part.astype(F32) + from_core.astype(F32)).astype(BF)
     from_two = moved(passed, back(two_on))
     mine = (own_part.astype(F32) + from_mixed.astype(F32) + from_two.astype(F32)).astype(BF)
-    everyone = lax.all_gather(mine, "head", axis=0)
-    summed = jnp.sum(everyone.astype(F32), axis=0).astype(BF)
-    return (attended, d_queries, summed[:, :head], summed[:, head:])
+    summed = head_sum(mine)
+    return (attended, d_queries, summed[:rows], summed[rows:])
 
 
 def solution(mesh):

time: 100 us -> 72.1 us (0.72)
  the two profiles are of different devices: /device:TPU:2 before, /device:TPU:230 now
where the time goes in v2:
time: 72.1 us; the launch traced here: 71.8 us
  waiting for transfers between devices  20.8 us (29%)
  blocking collectives  20 us (28%)
  starting transfers between devices  17.3 us (24%)
  Pallas kernels  10.3 us (14%)
  local copies, waits for them, and re-layouts  2.36 us (3%)
  between operations  0.75 us (1%)
    ppermute x6, waiting for transfers between devices, moved(): return lax.ppermute(value, 'ctx', pairs)  20.8 us
    ppermute x6, starting transfers between devices, moved(): return lax.ppermute(value, 'ctx', pairs)  17.3 us
    all_to_all x1, blocking collectives, head_sum(): theirs = lax.all_to_all(pieces, 'head', split_axis=0, concat_axis=0)  10.9 us
    all_to_all x1, blocking collectives, head_sum(): lax.all_to_all(mine, 'head', split_axis=0, concat_axis=0)  9.07 us
    pallas_call x1, Pallas kernels, attention(): pl.pallas_call(attention_kernel, out_shape=(like_q, like_q) + (like_kv,)...  8.59 us
    pallas_call x1, Pallas kernels, packed(): pl.pallas_call(pack_kernel, out_shape=jax.ShapeDtypeStruct((2 * rows, hea...  1.74 us
    unnamed x8, local copies, waits for them, and re-layouts  1.61 us
  transfers between devices with their start and end apart: 6, of which 4 were waited for; matrix products, arithmetic and copies ran while one was open for 0% of the time, Pallas kernels for 0%

profile of v2, /device:TPU:230, one launch (start us, length us, event | category | flops | bytes accessed | tf_op | source)
XLA Modules:
  0.0 71.8 jit_solution(3741285371203690733)
XLA Ops:
  0.6 0.0 copy-start.2
  0.6 0.0 copy-start.1
  0.7 1.7 %pack.1.own_ref = bf16[1024,128]{1,0:T(8,128)(2,1)} custom-call(bf16[512,128]{1,0:T(8,128)(2,1)} %key_ref.1, bf16[512,128]{1,0:T(8,128)(2,1)} %value_ref.1), custom_call_target="tpu_custom_call" | custom-call | tf_op jit(solution)/shard_map/pack/pallas_call | solution.py:234
  2.4 5.0 %collective-permute-start = (bf16[1024,128]{1,0:T(8,128)(2,1)}, bf16[1024,128]{1,0:T(8,128)(2,1)S(1)}, u32[]{:S(2)}, u32[]{:S(2)}) collective-permute-start(bf16[1024,128]{1,0:T(8,128)(2,1)} %pack.1.own_ref), channel_id=1, source_target_pairs={{0,8},{4,12},{8,16},{12,20},{16,24},{20,28},{24,32},{28,36},{32,40... | collective-permute-start | bytes 786440 | tf_op jit(solution)/shard_map/ppermute | solution.py:254
  7.4 1.9 %collective-permute-start.1 = (bf16[1024,128]{1,0:T(8,128)(2,1)}, bf16[1024,128]{1,0:T(8,128)(2,1)S(1)}, u32[]{:S(2)}, u32[]{:S(2)}) collective-permute-start(bf16[1024,128]{1,0:T(8,128)(2,1)} %pack.1.own_ref), channel_id=1, source_target_pairs={{0,4},{4,16},{8,12},{12,24},{16,20},{20,32},{24,28},{28,40},{32,36... | collective-permute-start | bytes 786440 | tf_op jit(solution)/shard_map/ppermute | solution.py:254
  9.3 6.1 %collective-permute-done.two_ref = bf16[1024,128]{1,0:T(8,128)(2,1)S(1)} collective-permute-done((bf16[1024,128]{1,0:T(8,128)(2,1)}, bf16[1024,128]{1,0:T(8,128)(2,1)S(1)}, u32[]{:S(2)}, u32[]{:S(2)}) %collective-permute-start) | collective-permute-done | bytes 262176 | tf_op jit(solution)/shard_map/ppermute | solution.py:254
  15.4 1.9 %collective-permute-start.2 = (bf16[1024,128]{1,0:T(8,128)(2,1)S(1)}, bf16[1024,128]{1,0:T(8,128)(2,1)S(1)}, u32[]{:S(2)}, u32[]{:S(2)}) collective-permute-start(bf16[1024,128]{1,0:T(8,128)(2,1)S(1)} %collective-permute-done.two_ref), channel_id=1, source_target_pairs={{0,4},{4,0},{8,12},{12,8},{16,20},{20,16},{24,28},{28,24},{32,36},... | collective-permute-start | bytes 786440 | tf_op jit(solution)/shard_map/ppermute | solution.py:254
  17.3 0.0 collective-permute-done.1.mixed_ref
  17.3 1.5 %collective-permute-done.2.swapped_ref = bf16[1024,128]{1,0:T(8,128)(2,1)S(1)} collective-permute-done((bf16[1024,128]{1,0:T(8,128)(2,1)S(1)}, bf16[1024,128]{1,0:T(8,128)(2,1)S(1)}, u32[]{:S(2)}, u32[]{:S(2)}) %collective-permute-start.2) | collective-permute-done | bytes 262176 | tf_op jit(solution)/shard_map/ppermute | solution.py:254
  18.8 0.0 copy-start.3
  18.8 0.0 copy-done.2
  18.8 0.0 copy-done.1
  18.8 0.6 copy-done.3
  19.4 0.0 copy-start
  19.4 0.9 %copy-done = bf16[1024,128]{1,0:T(8,128)(2,1)S(1)} copy-done((bf16[1024,128]{1,0:T(8,128)(2,1)S(1)}, bf16[1024,128]{1,0:T(8,128)(2,1)}, u32[]{:S(2)}) %copy-start) | copy-done | bytes 262168
  20.4 8.6 %attention.1 = (bf16[512,256]{1,0:T(8,128)(2,1)}, bf16[512,256]{1,0:T(8,128)(2,1)}, bf16[1024,128]{1,0:T(8,128)(2,1)S(1)}, bf16[1024,128]{1,0:T(8,128)(2,1)S(1)}...) custom-call(s32[1]{0:T(128)} %bitcast.place_ref, s32[1,128]{1,0:T(1,128)S(1)} %bitcast.5, ...), custom_call_target="tpu_custom_call" | custom-call | flops 6000000000 | bytes 4194304 | tf_op jit(solution)/shard_map/attention/pallas_call | solution.py:193
  29.0 4.7 %collective-permute-start.4 = (bf16[1024,128]{1,0:T(8,128)(2,1)S(1)}, bf16[1024,128]{1,0:T(8,128)(2,1)S(1)}, u32[]{:S(2)}, u32[]{:S(2)}) collective-permute-start(bf16[1024,128]{1,0:T(8,128)(2,1)S(1)} %get-tuple-element.15), channel_id=1, source_target_pairs={{0,4},{4,0},{8,12},{12,8},{16,20},{20,16},{24,28},{28,24},{32,36},... | collective-permute-start | bytes 786440 | tf_op jit(solution)/shard_map/ppermute | solution.py:254
  33.6 1.9 %collective-permute-start.3 = (bf16[1024,128]{1,0:T(8,128)(2,1)S(1)}, bf16[1024,128]{1,0:T(8,128)(2,1)S(1)}, u32[]{:S(2)}, u32[]{:S(2)}) collective-permute-start(bf16[1024,128]{1,0:T(8,128)(2,1)S(1)} %get-tuple-element.13), channel_id=1, source_target_pairs={{4,0},{16,4},{12,8},{24,12},{20,16},{32,20},{28,24},{40,28},{36,32... | collective-permute-start | bytes 786440 | tf_op jit(solution)/shard_map/ppermute | solution.py:254
  35.6 0.0 collective-permute-done.4
  35.6 0.1 add_convert_fusion.1
  35.7 1.9 %collective-permute-start.5 = (bf16[1024,128]{1,0:T(8,128)(2,1)S(1)}, bf16[1024,128]{1,0:T(8,128)(2,1)S(1)}, u32[]{:S(2)}, u32[]{:S(2)}) collective-permute-start(bf16[1024,128]{1,0:T(8,128)(2,1)S(1)} %add_convert_fusion.1), channel_id=1, source_target_pairs={{8,0},{12,4},{16,8},{20,12},{24,16},{28,20},{32,24},{36,28},{40,32... | collective-permute-start | bytes 786440 | tf_op jit(solution)/shard_map/ppermute | solution.py:254
  37.6 2.8 %collective-permute-done.3 = bf16[1024,128]{1,0:T(8,128)(2,1)S(1)} collective-permute-done((bf16[1024,128]{1,0:T(8,128)(2,1)S(1)}, bf16[1024,128]{1,0:T(8,128)(2,1)S(1)}, u32[]{:S(2)}, u32[]{:S(2)}) %collective-permute-start.3) | collective-permute-done | bytes 262176 | tf_op jit(solution)/shard_map/ppermute | solution.py:254
  40.4 10.5 %collective-permute-done.5 = bf16[1024,128]{1,0:T(8,128)(2,1)S(1)} collective-permute-done((bf16[1024,128]{1,0:T(8,128)(2,1)S(1)}, bf16[1024,128]{1,0:T(8,128)(2,1)S(1)}, u32[]{:S(2)}, u32[]{:S(2)}) %collective-permute-start.5) | collective-permute-done | bytes 262176 | tf_op jit(solution)/shard_map/ppermute | solution.py:254
  50.9 0.1 add_convert_fusion
  51.0 10.9 %all_to_all.10 = bf16[4,256,128]{2,1,0:T(8,128)(2,1)S(1)} all-to-all(bf16[4,256,128]{2,1,0:T(8,128)(2,1)S(1)} %bitcast.6), channel_id=1, replica_groups=mesh['ctx'=128,'head'=4] {'head'}, dimensions={0} | all-to-all | bytes 524288 | tf_op jit(solution)/shard_map/all_to_all | solution.py:247
  62.0 9.1 %all_to_all.11 = bf16[4,256,128]{2,1,0:T(8,128)(2,1)S(1)} all-to-all(bf16[4,256,128]{2,1,0:T(8,128)(2,1)S(1)} %broadcast_in_dim.2), channel_id=1, replica_groups=mesh['ctx'=128,'head'=4] {'head'}, dimensions={0} | all-to-all | bytes 524288 | tf_op jit(solution)/shard_map/all_to_all | solution.py:250
  71.1 0.7 fusion
  (2 shorter events, 0.1 us)
Async XLA Ops:
  0.6 18.2 %copy-start.2 = (bf16[512,256]{1,0:T(8,128)(2,1)S(1)}, bf16[512,256]{1,0:T(8,128)(2,1)}, u32[]{:S(2)}) copy-start(bf16[512,256]{1,0:T(8,128)(2,1)} %do_ref.1) | copy-start | bytes 786436
  0.6 18.1 %copy-start.1 = (bf16[512,256]{1,0:T(8,128)(2,1)S(1)}, bf16[512,256]{1,0:T(8,128)(2,1)}, u32[]{:S(2)}) copy-start(bf16[512,256]{1,0:T(8,128)(2,1)} %q_ref.1) | copy-start | bytes 786436
  2.4 13.0 %collective-permute-start = (bf16[1024,128]{1,0:T(8,128)(2,1)}, bf16[1024,128]{1,0:T(8,128)(2,1)S(1)}, u32[]{:S(2)}, u32[]{:S(2)}) collective-permute-start(bf16[1024,128]{1,0:T(8,128)(2,1)} %pack.1.own_ref), channel_id=1, source_target_pairs={{0,8},{4,12},{8,16},{12,20},{16,24},{20,28},{24,32},{28,36},{32,40... | collective-permute-start | bytes 786440 | tf_op jit(solution)/shard_map/ppermute | solution.py:254
  7.4 9.9 %collective-permute-start.1 = (bf16[1024,128]{1,0:T(8,128)(2,1)}, bf16[1024,128]{1,0:T(8,128)(2,1)S(1)}, u32[]{:S(2)}, u32[]{:S(2)}) collective-permute-start(bf16[1024,128]{1,0:T(8,128)(2,1)} %pack.1.own_ref), channel_id=1, source_target_pairs={{0,4},{4,16},{8,12},{12,24},{16,20},{20,32},{24,28},{28,40},{32,36... | collective-permute-start | bytes 786440 | tf_op jit(solution)/shard_map/ppermute | solution.py:254
  15.4 3.4 %collective-permute-start.2 = (bf16[1024,128]{1,0:T(8,128)(2,1)S(1)}, bf16[1024,128]{1,0:T(8,128)(2,1)S(1)}, u32[]{:S(2)}, u32[]{:S(2)}) collective-permute-start(bf16[1024,128]{1,0:T(8,128)(2,1)S(1)} %collective-permute-done.two_ref), channel_id=1, source_target_pairs={{0,4},{4,0},{8,12},{12,8},{16,20},{20,16},{24,28},{28,24},{32,36},... | collective-permute-start | bytes 786440 | tf_op jit(solution)/shard_map/ppermute | solution.py:254
  18.8 0.7 copy-start.3
  19.4 0.9 %copy-start = (bf16[1024,128]{1,0:T(8,128)(2,1)S(1)}, bf16[1024,128]{1,0:T(8,128)(2,1)}, u32[]{:S(2)}) copy-start(bf16[1024,128]{1,0:T(8,128)(2,1)} %pack.1.own_ref) | copy-start | bytes 786436
  29.0 6.6 %collective-permute-start.4 = (bf16[1024,128]{1,0:T(8,128)(2,1)S(1)}, bf16[1024,128]{1,0:T(8,128)(2,1)S(1)}, u32[]{:S(2)}, u32[]{:S(2)}) collective-permute-start(bf16[1024,128]{1,0:T(8,128)(2,1)S(1)} %get-tuple-element.15), channel_id=1, source_target_pairs={{0,4},{4,0},{8,12},{12,8},{16,20},{20,16},{24,28},{28,24},{32,36},... | collective-permute-start | bytes 786440 | tf_op jit(solution)/shard_map/ppermute | solution.py:254
  33.6 6.7 %collective-permute-start.3 = (bf16[1024,128]{1,0:T(8,128)(2,1)S(1)}, bf16[1024,128]{1,0:T(8,128)(2,1)S(1)}, u32[]{:S(2)}, u32[]{:S(2)}) collective-permute-start(bf16[1024,128]{1,0:T(8,128)(2,1)S(1)} %get-tuple-element.13), channel_id=1, source_target_pairs={{4,0},{16,4},{12,8},{24,12},{20,16},{32,20},{28,24},{40,28},{36,32... | collective-permute-start | bytes 786440 | tf_op jit(solution)/shard_map/ppermute | solution.py:254
  35.7 15.2 %collective-permute-start.5 = (bf16[1024,128]{1,0:T(8,128)(2,1)S(1)}, bf16[1024,128]{1,0:T(8,128)(2,1)S(1)}, u32[]{:S(2)}, u32[]{:S(2)}) collective-permute-start(bf16[1024,128]{1,0:T(8,128)(2,1)S(1)} %add_convert_fusion.1), channel_id=1, source_target_pairs={{8,0},{12,4},{16,8},{20,12},{24,16},{28,20},{32,24},{36,28},{40,32... | collective-permute-start | bytes 786440 | tf_op jit(solution)/shard_map/ppermute | solution.py:254

commit v3 on v2

v3 whole, which is shorter than its diff:
```python
import functools
import math

import jax
import jax.numpy as jnp
from jax import lax
from jax.experimental import pallas as pl
from jax.experimental.pallas import tpu as pltpu
from jax.sharding import PartitionSpec as P

SPAN = 3
BF = jnp.bfloat16
F32 = jnp.float32


def dot_nt(a, b):
    return lax.dot_general(a, b, (((1,), (1,)), ((), ())), preferred_element_type=F32)


def dot_nn(a, b):
    return jnp.dot(a, b, preferred_element_type=F32)


def diagonal_kernel(
    place_ref, lengths_ref, q_ref, do_ref, own_ref,
    first_ref, starts_ref, top_ref, total_ref, out_ref, qt_ref, dot_ref,
):
    rows, width = q_ref.shape
    head = own_ref.shape[1]
    heads = width // head
    lead = SPAN * rows
    lengths = lengths_ref[...].astype(F32)
    docs = lengths.shape[1]
    along = jnp.broadcast_to(lengths, (docs, docs))
    earlier = lax.broadcasted_iota(jnp.int32, (docs, docs), 0)
    later = lax.broadcasted_iota(jnp.int32, (docs, docs), 1)
    ends = jnp.sum(jnp.where(earlier <= later, along.T, 0.0), axis=0, keepdims=True)
    begin = (place_ref[0] * rows).astype(F32)
    positions = begin + lax.broadcasted_iota(jnp.int32, (rows, docs), 0).astype(F32)
    doc_start = jnp.sum(jnp.where(ends <= positions, lengths, 0.0), axis=1, keepdims=True)
    start = (doc_start - begin).astype(jnp.int32)
    starts_ref[...] = jnp.broadcast_to(start, starts_ref.shape)
    first_ref[0] = jnp.min(start) + lead

    column = lax.broadcasted_iota(jnp.int32, (rows, rows), 1)
    row = lax.broadcasted_iota(jnp.int32, (rows, rows), 0)
    allowed = (column >= start) & (column <= row)
    keys = own_ref[pl.ds(0, rows), :]
    values = own_ref[pl.ds(rows, rows), :]
    for h in range(heads):
        cols = pl.ds(h * head, head)
        s = jnp.where(allowed, dot_nt(q_ref[:, cols], keys), -jnp.inf)
        m = jnp.max(s, axis=1, keepdims=True)
        e = jnp.exp2((s - m) * exp2_scale(head))
        top_ref[h] = jnp.broadcast_to(m, (rows, head))
        total_ref[h] = jnp.broadcast_to(jnp.sum(e, axis=1, keepdims=True), (rows, head))
        out_ref[h] = dot_nn(e.astype(BF), values)
        qt_ref[h] = q_ref[:, cols].T
        dot_ref[h] = do_ref[:, cols].T


def earlier_kernel(
    place_ref, first_ref, q_ref, do_ref, qt_ref, dot_ref, starts_ref, top0_ref, total0_ref, out0_ref,
    two_ref, mixed_ref, swapped_ref,
    att_ref, top_ref, inverse_ref, row_dot_ref, dq_ref, two_part_ref, mixed_part_ref, swapped_part_ref,
    key_window, value_window, key_parts, value_parts, tiles, lanes,
):
    rows, width = q_ref.shape
    head = two_ref.shape[1]
    heads = width // head
    to_exp2 = exp2_scale(head)
    scale = score_scale(head)
    odd = lax.rem(place_ref[0], 2)
    last = (SPAN - 1) * rows
    mixed_row = pl.multiple_of(jnp.where(odd == 1, last, 0), rows)
    swapped_row = pl.multiple_of(jnp.where(odd == 1, 0, last), rows)
    slots = (
        (two_ref, two_part_ref, last - rows),
        (mixed_ref, mixed_part_ref, mixed_row),
        (swapped_ref, swapped_part_ref, swapped_row),
    )
    low = jnp.minimum(jnp.maximum(first_ref[0], 0) // rows, SPAN)
    column = lax.broadcasted_iota(jnp.int32, (rows, rows), 1)

    def wide(x):
        return jnp.concatenate([x] * (rows // head), axis=1)

    def folded(x, op):
        parts = [x[:, c : c + head] for c in range(0, rows, head)]
        return functools.reduce(op, parts)

    def score_tile(t, carry):
        at = pl.multiple_of(t * rows, rows)
        keys = key_window[pl.ds(at, rows), :]
        allowed = column >= wide(starts_ref[...] + (SPAN * rows - at))
        for h in range(heads):
            s = dot_nt(q_ref[:, pl.ds(h * head, head)], keys)
            s = jnp.where(allowed, s, -jnp.inf)
            tiles[h, t] = s
            lanes[h] = jnp.maximum(lanes[h], folded(s, jnp.maximum))
        return carry

    def out_tile(t, carry):
        at = pl.multiple_of(t * rows, rows)
        values = value_window[pl.ds(at, rows), :]
        for h in range(heads):
            e = jnp.exp2((tiles[h, t] - wide(top_ref[h])) * to_exp2)
            tiles[h, t] = e
            lanes[h] += folded(e, jnp.add)
            dq_ref[h] += dot_nn(e.astype(BF), values)
        return carry

    def grad_tile(t, carry):
        at = pl.multiple_of(t * rows, rows)
        keys = key_window[pl.ds(at, rows), :]
        values = value_window[pl.ds(at, rows), :]
        dv = jnp.zeros((head, rows), F32)
        dk = jnp.zeros((head, rows), F32)
        for h in range(heads):
            dw = dot_nt(do_ref[:, pl.ds(h * head, head)], values)
            w = tiles[h, t] * wide(inverse_ref[h])
            ds = (w * (dw - wide(row_dot_ref[h]))).astype(BF)
            dv = dv + dot_nn(dot_ref[h], w.astype(BF))
            dk = dk + dot_nn(qt_ref[h], ds)
            dq_ref[h] += dot_nn(ds, keys)
        key_parts[pl.ds(at, rows), :] = (dk * scale).T.astype(BF)
        value_parts[pl.ds(at, rows), :] = dv.T.astype(BF)
        return carry

    def zero_tile(t, carry):
        at = pl.multiple_of(t * rows, rows)
        key_parts[pl.ds(at, rows), :] = jnp.zeros((rows, head), BF)
        value_parts[pl.ds(at, rows), :] = jnp.zeros((rows, head), BF)
        return carry

    reaches = low < SPAN

    @pl.when(reaches)
    def _():
        for block, _, at in slots:
            key_window[pl.ds(at, rows), :] = block[pl.ds(0, rows), :]
            value_window[pl.ds(at, rows), :] = block[pl.ds(rows, rows), :]
        lanes[...] = top0_ref[...]
        lax.fori_loop(low, SPAN, score_tile, 0)
        for h in range(heads):
            top = jnp.broadcast_to(jnp.max(lanes[h], axis=1, keepdims=True), (rows, head))
            top_ref[h] = top
            kept = jnp.exp2((top0_ref[h] - top) * to_exp2)
            inverse_ref[h] = total0_ref[h] * kept
            dq_ref[h] = out0_ref[h] * kept
        lanes[...] = jnp.zeros(lanes.shape, F32)
        lax.fori_loop(low, SPAN, out_tile, 0)
        for h in range(heads):
            inverse_ref[h] += jnp.sum(lanes[h], axis=1, keepdims=True)

    @pl.when(jnp.logical_not(reaches))
    def _():
        top_ref[...] = top0_ref[...]
        inverse_ref[...] = total0_ref[...]
        dq_ref[...] = out0_ref[...]

    for h in range(heads):
        cols = pl.ds(h * head, head)
        inverse = 1.0 / inverse_ref[h]
        inverse_ref[h] = inverse
        attended = (dq_ref[h] * inverse).astype(BF)
        att_ref[:, cols] = attended
        row_dot = jnp.sum(do_ref[:, cols].astype(F32) * attended.astype(F32), axis=1, keepdims=True)
        row_dot_ref[h] = jnp.broadcast_to(row_dot, (rows, head))
    dq_ref[...] = jnp.zeros(dq_ref.shape, F32)
    lax.fori_loop(0, low, zero_tile, 0)
    lax.fori_loop(low, SPAN, grad_tile, 0)
    for _, part, at in slots:
        part[pl.ds(0, rows), :] = key_parts[pl.ds(at, rows), :]
        part[pl.ds(rows, rows), :] = value_parts[pl.ds(at, rows), :]


def own_kernel(
    q_ref, do_ref, qt_ref, dot_ref, own_ref, starts_ref, top_ref, inverse_ref, row_dot_ref, earlier_ref,
    dq_ref, part_ref,
):
    rows, width = q_ref.shape
    head = own_ref.shape[1]
    heads = width // head
    to_exp2 = exp2_scale(head)
    scale = score_scale(head)
    column = lax.broadcasted_iota(jnp.int32, (rows, rows), 1)
    row = lax.broadcasted_iota(jnp.int32, (rows, rows), 0)

    def wide(x):
        return jnp.concatenate([x] * (rows // head), axis=1)

    allowed = (column >= wide(starts_ref[...])) & (column <= row)
    keys = own_ref[pl.ds(0, rows), :]
    values = own_ref[pl.ds(rows, rows), :]
    dv = jnp.zeros((head, rows), F32)
    dk = jnp.zeros((head, rows), F32)
    for h in range(heads):
        cols = pl.ds(h * head, head)
        s = jnp.where(allowed, dot_nt(q_ref[:, cols], keys), -jnp.inf)
        w = jnp.exp2((s - wide(top_ref[h])) * to_exp2) * wide(inverse_ref[h])
        dw = dot_nt(do_ref[:, cols], values)
        ds = (w * (dw - wide(row_dot_ref[h]))).astype(BF)
        dv = dv + dot_nn(dot_ref[h], w.astype(BF))
        dk = dk + dot_nn(qt_ref[h], ds)
        dq_ref[:, cols] = ((earlier_ref[h] + dot_nn(ds, keys)) * scale).astype(BF)
    part_ref[pl.ds(0, rows), :] = (dk * scale).T.astype(BF)
    part_ref[pl.ds(rows, rows), :] = dv.T.astype(BF)


def score_scale(head):
    return 1.0 / math.sqrt(head)


def exp2_scale(head):
    return score_scale(head) * math.log2(math.e)


VMEM = pl.BlockSpec(memory_space=pltpu.VMEM)
SMEM = pl.BlockSpec(memory_space=pltpu.SMEM)


def shape(dims, dtype):
    return jax.ShapeDtypeStruct(dims, dtype)


def on_core(kernel, name, mflop, outs, ins, scratch=()):
    return pl.pallas_call(
        kernel,
        out_shape=tuple(outs),
        in_specs=[SMEM if x.ndim == 1 else VMEM for x in ins],
        out_specs=tuple(SMEM if len(x.shape) == 1 else VMEM for x in outs),
        scratch_shapes=list(scratch),
        compiler_params=pltpu.CompilerParams(vmem_limit_bytes=40 << 20),
        cost_estimate=pl.CostEstimate(
            flops=mflop * 1_000_000, bytes_accessed=2 << 20, transcendentals=1 << 19
        ),
        name=name,
    )(*ins)


def attention_before(place, lengths, q, do, own):
    rows, width = q.shape
    head = own.shape[1]
    heads = width // head
    state = shape((heads, rows, head), F32)
    turned = shape((heads, head, rows), BF)
    outs = [shape((1,), jnp.int32), shape((rows, head), jnp.int32), state, state, state, turned, turned]
    return on_core(diagonal_kernel, "diagonal", 1200, outs, (place, lengths, q, do, own))


def attention_earlier(place, first, q, do, qt, dot_, starts, top, total, out, two, mixed, swapped):
    rows, width = q.shape
    head = two.shape[1]
    heads = width // head
    state = shape((heads, rows, head), F32)
    part = shape(two.shape, BF)
    span = SPAN * rows
    return on_core(
        earlier_kernel,
        "earlier",
        5000,
        [shape(q.shape, BF), state, state, state, state, part, part, part],
        (place, first, q, do, qt, dot_, starts, top, total, out, two, mixed, swapped),
        [pltpu.VMEM((span, head), BF)] * 4
        + [pltpu.VMEM((heads, SPAN, rows, rows), F32), pltpu.VMEM((heads, rows, head), F32)],
    )


def attention_own(q, do, qt, dot_, own, starts, top, inverse, row_dot, dq):
    outs = [shape(q.shape, BF), shape(own.shape, BF)]
    ins = (q, do, qt, dot_, own, starts, top, inverse, row_dot, dq)
    return on_core(own_kernel, "own", 2500, outs, ins)


def pack_kernel(key_ref, value_ref, both_ref, sems):
    rows = key_ref.shape[0]
    copies = [
        pltpu.make_async_copy(key_ref, both_ref.at[pl.ds(0, rows)], sems.at[0]),
        pltpu.make_async_copy(value_ref, both_ref.at[pl.ds(rows, rows)], sems.at[1]),
    ]
    for copy in copies:
        copy.start()
    for copy in copies:
        copy.wait()


def packed(keys, values):
    rows, head = keys.shape
    return pl.pallas_call(
        pack_kernel,
        out_shape=jax.ShapeDtypeStruct((2 * rows, head), BF),
        in_specs=[pl.BlockSpec(memory_space=pl.ANY)] * 2,
        out_specs=pl.BlockSpec(memory_space=pltpu.VMEM),
        scratch_shapes=[pltpu.SemaphoreType.DMA((2,))],
        name="pack",
    )(keys, values)


def head_sum(part):
    heads = lax.axis_size("head")
    pieces = part.reshape(heads, part.shape[0] // heads, part.shape[1])
    theirs = lax.all_to_all(pieces, "head", split_axis=0, concat_axis=0)
    mine = jnp.sum(theirs.astype(F32), axis=0).astype(BF)
    mine = jnp.broadcast_to(mine[None], pieces.shape)
    return lax.all_to_all(mine, "head", split_axis=0, concat_axis=0).reshape(part.shape)


def moved(value, pairs):
    return lax.ppermute(value, "ctx", pairs)


def on_device(queries, keys, values, d_out, doc_lengths):
    count = lax.axis_size("ctx")
    rows = keys.shape[0]
    place = lax.axis_index("ctx").reshape(1).astype(jnp.int32)
    two_on = [(i, i + 2) for i in range(count - 2)]
    mixed_on = [(i, i + (3 if i % 2 else 1)) for i in range(count) if i + (3 if i % 2 else 1) < count]
    across = [(i, i ^ 1) for i in range(count)]

    def back(pairs):
        return [(there, here) for here, there in pairs]

    lengths = doc_lengths.reshape(1, -1)
    own = packed(keys, values)
    two = moved(own, two_on)
    mixed = moved(own, mixed_on)
    first, starts, top, total, out, qt, dot_ = attention_before(place, lengths, queries, d_out, own)
    swapped = moved(two, across)
    attended, top, inverse, row_dot, dq, two_part, mixed_part, swapped_part = attention_earlier(
        place, first, queries, d_out, qt, dot_, starts, top, total, out, two, mixed, swapped
    )
    d_queries, own_part = attention_own(
        queries, d_out, qt, dot_, own, starts, top, inverse, row_dot, dq
    )
    from_core = moved(swapped_part, across)
    from_mixed = moved(mixed_part, back(mixed_on))
    passed = (two_part.astype(F32) + from_core.astype(F32)).astype(BF)
    from_two = moved(passed, back(two_on))
    mine = (own_part.astype(F32) + from_mixed.astype(F32) + from_two.astype(F32)).astype(BF)
    summed = head_sum(mine)
    return (attended, d_queries, summed[:rows], summed[rows:])


def solution(mesh):
    in_specs = (P("ctx", "head"), P("ctx", None), P("ctx", None), P("ctx", "head"), P())
    out_specs = (P("ctx", "head"), P("ctx", "head"), P("ctx", None), P("ctx", None))
    return jax.shard_map(
        on_device, mesh=mesh, in_specs=in_specs, out_specs=out_specs, check_vma=False
    )
```

time: 72.1 us -> 69.1 us (0.958)
  the two profiles are of different devices: /device:TPU:230 before, /device:TPU:102 now
where the time goes in v3:
time: 69.1 us; the launch traced here: 68.7 us
  blocking collectives  20 us (29%)
  starting transfers between devices  18.9 us (27%)
  waiting for transfers between devices  17.1 us (25%)
  Pallas kernels  9.28 us (13%)
  local copies, waits for them, and re-layouts  2.35 us (3%)
  between operations  0.81 us (1%)
    ppermute x6, starting transfers between devices, moved(): return lax.ppermute(value, 'ctx', pairs)  18.9 us
    ppermute x6, waiting for transfers between devices, moved(): return lax.ppermute(value, 'ctx', pairs)  17.1 us
    all_to_all x1, blocking collectives, head_sum(): theirs = lax.all_to_all(pieces, 'head', split_axis=0, concat_axis=0)  11 us
    all_to_all x1, blocking collectives, head_sum(): lax.all_to_all(mine, 'head', split_axis=0, concat_axis=0)  9.07 us
    pallas_call x3, Pallas kernels, on_core(): pl.pallas_call(kernel, out_shape=tuple(outs), in_specs=[SMEM if x.ndim ==...  7.54 us
    pallas_call x1, Pallas kernels, packed(): pl.pallas_call(pack_kernel, out_shape=jax.ShapeDtypeStruct((2 * rows, hea...  1.74 us
    unnamed x10, local copies, waits for them, and re-layouts  1.59 us
  transfers between devices with their start and end apart: 6, of which 2 were waited for; matrix products, arithmetic and copies ran while one was open for 0% of the time, Pallas kernels for 5%

profile of v3, /device:TPU:102, one launch (start us, length us, event | category | flops | bytes accessed | tf_op | source)
XLA Modules:
  0.0 68.7 jit_solution(2260143295050217474)
XLA Ops:
  0.6 0.0 copy-start.3
  0.6 0.0 copy-start.2
  0.7 1.7 %pack.1.own_ref = bf16[1024,128]{1,0:T(8,128)(2,1)} custom-call(bf16[512,128]{1,0:T(8,128)(2,1)} %key_ref.1, bf16[512,128]{1,0:T(8,128)(2,1)} %value_ref.1), custom_call_target="tpu_custom_call" | custom-call | tf_op jit(solution)/shard_map/pack/pallas_call | solution.py:290
  2.4 5.0 %collective-permute-start = (bf16[1024,128]{1,0:T(8,128)(2,1)}, bf16[1024,128]{1,0:T(8,128)(2,1)S(1)}, u32[]{:S(2)}, u32[]{:S(2)}) collective-permute-start(bf16[1024,128]{1,0:T(8,128)(2,1)} %pack.1.own_ref), channel_id=1, source_target_pairs={{0,8},{4,12},{8,16},{12,20},{16,24},{20,28},{24,32},{28,36},{32,40... | collective-permute-start | bytes 786440 | tf_op jit(solution)/shard_map/ppermute | solution.py:310
  7.4 1.9 %collective-permute-start.1 = (bf16[1024,128]{1,0:T(8,128)(2,1)}, bf16[1024,128]{1,0:T(8,128)(2,1)S(1)}, u32[]{:S(2)}, u32[]{:S(2)}) collective-permute-start(bf16[1024,128]{1,0:T(8,128)(2,1)} %pack.1.own_ref), channel_id=1, source_target_pairs={{0,4},{4,16},{8,12},{12,24},{16,20},{20,32},{24,28},{28,40},{32,36... | collective-permute-start | bytes 786440 | tf_op jit(solution)/shard_map/ppermute | solution.py:310
  9.3 6.1 %collective-permute-done.two_ref = bf16[1024,128]{1,0:T(8,128)(2,1)S(1)} collective-permute-done((bf16[1024,128]{1,0:T(8,128)(2,1)}, bf16[1024,128]{1,0:T(8,128)(2,1)S(1)}, u32[]{:S(2)}, u32[]{:S(2)}) %collective-permute-start) | collective-permute-done | bytes 262176 | tf_op jit(solution)/shard_map/ppermute | solution.py:310
  15.4 1.9 %collective-permute-start.2 = (bf16[1024,128]{1,0:T(8,128)(2,1)S(1)}, bf16[1024,128]{1,0:T(8,128)(2,1)S(1)}, u32[]{:S(2)}, u32[]{:S(2)}) collective-permute-start(bf16[1024,128]{1,0:T(8,128)(2,1)S(1)} %collective-permute-done.two_ref), channel_id=1, source_target_pairs={{0,4},{4,0},{8,12},{12,8},{16,20},{20,16},{24,28},{28,24},{32,36},... | collective-permute-start | bytes 786440 | tf_op jit(solution)/shard_map/ppermute | solution.py:310
  17.3 0.0 copy-start.4
  17.3 0.0 copy-done.3
  17.3 0.0 copy-done.2
  17.3 0.6 copy-done.4
  17.9 0.0 copy-start
  17.9 0.9 %copy-done = bf16[1024,128]{1,0:T(8,128)(2,1)S(1)} copy-done((bf16[1024,128]{1,0:T(8,128)(2,1)S(1)}, bf16[1024,128]{1,0:T(8,128)(2,1)}, u32[]{:S(2)}) %copy-start) | copy-done | bytes 262168
  18.9 1.2 %diagonal.1 = (s32[1]{0:T(128)}, s32[512,128]{1,0:T(8,128)S(1)}, f32[2,512,128]{2,1,0:T(8,128)S(1)}, f32[2,512,128]{2,1,0:T(8,128)S(1)}, f32[2,512,128]{2,1,0:T(...) custom-call(s32[1]{0:T(128)} %bitcast.place_ref, s32[1,128]{1,0:T(1,128)S(1)} %bitcast.5, ...), custom_call_target="tpu_custom_call" | custom-call | flops 1200000000 | bytes 2097152 | tf_op jit(solution)/shard_map/diagonal/pallas_call | solution.py:228
  20.1 0.0 collective-permute-done.1.mixed_ref
  20.1 0.0 collective-permute-done.2.swapped_ref
  20.1 4.2 %earlier.1 = (bf16[512,256]{1,0:T(8,128)(2,1)}, f32[2,512,128]{2,1,0:T(8,128)S(1)}, f32[2,512,128]{2,1,0:T(8,128)S(1)}, f32[2,512,128]{2,1,0:T(8,128)S(1)}, f32[...) custom-call(s32[1]{0:T(128)} %bitcast.place_ref, ...), custom_call_target="tpu_custom_call" | custom-call | flops 5000000000 | bytes 2097152 | tf_op jit(solution)/shard_map/earlier/pallas_call | solution.py:228
  24.3 2.4 %collective-permute-start.4 = (bf16[1024,128]{1,0:T(8,128)(2,1)S(1)}, bf16[1024,128]{1,0:T(8,128)(2,1)S(1)}, u32[]{:S(2)}, u32[]{:S(2)}) collective-permute-start(bf16[1024,128]{1,0:T(8,128)(2,1)S(1)} %get-tuple-element.37), channel_id=1, source_target_pairs={{0,4},{4,0},{8,12},{12,8},{16,20},{20,16},{24,28},{28,24},{32,36},... | collective-permute-start | bytes 786440 | tf_op jit(solution)/shard_map/ppermute | solution.py:310
  26.7 1.9 %collective-permute-start.3 = (bf16[1024,128]{1,0:T(8,128)(2,1)S(1)}, bf16[1024,128]{1,0:T(8,128)(2,1)S(1)}, u32[]{:S(2)}, u32[]{:S(2)}) collective-permute-start(bf16[1024,128]{1,0:T(8,128)(2,1)S(1)} %get-tuple-element.35), channel_id=1, source_target_pairs={{4,0},{16,4},{12,8},{24,12},{20,16},{32,20},{28,24},{40,28},{36,32... | collective-permute-start | bytes 786440 | tf_op jit(solution)/shard_map/ppermute | solution.py:310
  28.6 0.0 collective-permute-done.4
  28.6 0.0 copy-start.1
  28.6 0.1 add_convert_fusion.1
  28.7 5.8 %collective-permute-start.5 = (bf16[1024,128]{1,0:T(8,128)(2,1)S(1)}, bf16[1024,128]{1,0:T(8,128)(2,1)S(1)}, u32[]{:S(2)}, u32[]{:S(2)}) collective-permute-start(bf16[1024,128]{1,0:T(8,128)(2,1)S(1)} %add_convert_fusion.1), channel_id=1, source_target_pairs={{8,0},{12,4},{16,8},{20,12},{24,16},{28,20},{32,24},{36,28},{40,32... | collective-permute-start | bytes 786440 | tf_op jit(solution)/shard_map/ppermute | solution.py:310
  34.5 0.0 copy-done.1
  34.5 2.2 %own.1 = (bf16[512,256]{1,0:T(8,128)(2,1)}, bf16[1024,128]{1,0:T(8,128)(2,1)S(1)}) custom-call(bf16[512,256]{1,0:T(8,128)(2,1)S(1)} %copy-done.2, bf16[512,256]{1,0:T(8,128)(2,1)S(1)} %copy-done.3, bf16[2,128,512]{2,1,0:T(8,128)(2,1)S(1)} %get-tuple-element.22.qt_ref, bf16[2,128,512]{2,1,0:T(8,128)(2,1)S(1)} %get-tuple-element.23.dot_ref, ...), custom_call_target="tpu_custom_call" | custom-call | flops 2500000000 | bytes 2097152 | tf_op jit(solution)/shard_map/own/pallas_call | solution.py:228
  36.7 0.0 collective-permute-done.3
  36.7 11.1 %collective-permute-done.5 = bf16[1024,128]{1,0:T(8,128)(2,1)S(1)} collective-permute-done((bf16[1024,128]{1,0:T(8,128)(2,1)S(1)}, bf16[1024,128]{1,0:T(8,128)(2,1)S(1)}, u32[]{:S(2)}, u32[]{:S(2)}) %collective-permute-start.5) | collective-permute-done | bytes 262176 | tf_op jit(solution)/shard_map/ppermute | solution.py:310
  47.7 0.1 add_convert_fusion
  47.8 11.0 %all_to_all.10 = bf16[4,256,128]{2,1,0:T(8,128)(2,1)S(1)} all-to-all(bf16[4,256,128]{2,1,0:T(8,128)(2,1)S(1)} %bitcast.6), channel_id=1, replica_groups=mesh['ctx'=128,'head'=4] {'head'}, dimensions={0} | all-to-all | bytes 524288 | tf_op jit(solution)/shard_map/all_to_all | solution.py:303
  58.9 9.1 %all_to_all.11 = bf16[4,256,128]{2,1,0:T(8,128)(2,1)S(1)} all-to-all(bf16[4,256,128]{2,1,0:T(8,128)(2,1)S(1)} %broadcast_in_dim.2), channel_id=1, replica_groups=mesh['ctx'=128,'head'=4] {'head'}, dimensions={0} | all-to-all | bytes 524288 | tf_op jit(solution)/shard_map/all_to_all | solution.py:306
  68.0 0.7 %fusion = (bf16[2,256,128]{2,1,0:T(8,128)(2,1)}, bf16[2,256,128]{2,1,0:T(8,128)(2,1)}) fusion(bf16[4,256,128]{2,1,0:T(8,128)(2,1)S(1)} %all_to_all.11), kind=kLoop, calls=%fused_computation.2 | loop fusion | bytes 524288 | tf_op jit(solution)/shard_map/slice | solution.py:342
  (2 shorter events, 0.1 us)
Async XLA Ops:
  0.6 16.7 %copy-start.3 = (bf16[512,256]{1,0:T(8,128)(2,1)S(1)}, bf16[512,256]{1,0:T(8,128)(2,1)}, u32[]{:S(2)}) copy-start(bf16[512,256]{1,0:T(8,128)(2,1)} %do_ref.5) | copy-start | bytes 786436
  0.6 16.7 %copy-start.2 = (bf16[512,256]{1,0:T(8,128)(2,1)S(1)}, bf16[512,256]{1,0:T(8,128)(2,1)}, u32[]{:S(2)}) copy-start(bf16[512,256]{1,0:T(8,128)(2,1)} %q_ref.5) | copy-start | bytes 786436
  2.4 13.0 %collective-permute-start = (bf16[1024,128]{1,0:T(8,128)(2,1)}, bf16[1024,128]{1,0:T(8,128)(2,1)S(1)}, u32[]{:S(2)}, u32[]{:S(2)}) collective-permute-start(bf16[1024,128]{1,0:T(8,128)(2,1)} %pack.1.own_ref), channel_id=1, source_target_pairs={{0,8},{4,12},{8,16},{12,20},{16,24},{20,28},{24,32},{28,36},{32,40... | collective-permute-start | bytes 786440 | tf_op jit(solution)/shard_map/ppermute | solution.py:310
  7.4 12.7 %collective-permute-start.1 = (bf16[1024,128]{1,0:T(8,128)(2,1)}, bf16[1024,128]{1,0:T(8,128)(2,1)S(1)}, u32[]{:S(2)}, u32[]{:S(2)}) collective-permute-start(bf16[1024,128]{1,0:T(8,128)(2,1)} %pack.1.own_ref), channel_id=1, source_target_pairs={{0,4},{4,16},{8,12},{12,24},{16,20},{20,32},{24,28},{28,40},{32,36... | collective-permute-start | bytes 786440 | tf_op jit(solution)/shard_map/ppermute | solution.py:310
  15.4 4.7 %collective-permute-start.2 = (bf16[1024,128]{1,0:T(8,128)(2,1)S(1)}, bf16[1024,128]{1,0:T(8,128)(2,1)S(1)}, u32[]{:S(2)}, u32[]{:S(2)}) collective-permute-start(bf16[1024,128]{1,0:T(8,128)(2,1)S(1)} %collective-permute-done.two_ref), channel_id=1, source_target_pairs={{0,4},{4,0},{8,12},{12,8},{16,20},{20,16},{24,28},{28,24},{32,36},... | collective-permute-start | bytes 786440 | tf_op jit(solution)/shard_map/ppermute | solution.py:310
  17.3 0.7 copy-start.4
  17.9 0.9 %copy-start = (bf16[1024,128]{1,0:T(8,128)(2,1)S(1)}, bf16[1024,128]{1,0:T(8,128)(2,1)}, u32[]{:S(2)}) copy-start(bf16[1024,128]{1,0:T(8,128)(2,1)} %pack.1.own_ref) | copy-start | bytes 786436
  24.3 4.3 %collective-permute-start.4 = (bf16[1024,128]{1,0:T(8,128)(2,1)S(1)}, bf16[1024,128]{1,0:T(8,128)(2,1)S(1)}, u32[]{:S(2)}, u32[]{:S(2)}) collective-permute-start(bf16[1024,128]{1,0:T(8,128)(2,1)S(1)} %get-tuple-element.37), channel_id=1, source_target_pairs={{0,4},{4,0},{8,12},{12,8},{16,20},{20,16},{24,28},{28,24},{32,36},... | collective-permute-start | bytes 786440 | tf_op jit(solution)/shard_map/ppermute | solution.py:310
  26.7 10.0 %collective-permute-start.3 = (bf16[1024,128]{1,0:T(8,128)(2,1)S(1)}, bf16[1024,128]{1,0:T(8,128)(2,1)S(1)}, u32[]{:S(2)}, u32[]{:S(2)}) collective-permute-start(bf16[1024,128]{1,0:T(8,128)(2,1)S(1)} %get-tuple-element.35), channel_id=1, source_target_pairs={{4,0},{16,4},{12,8},{24,12},{20,16},{32,20},{28,24},{40,28},{36,32... | collective-permute-start | bytes 786440 | tf_op jit(solution)/shard_map/ppermute | solution.py:310
  28.6 5.9 %copy-start.1 = (bf16[1024,128]{1,0:T(8,128)(2,1)S(1)}, bf16[1024,128]{1,0:T(8,128)(2,1)}, u32[]{:S(2)}) copy-start(bf16[1024,128]{1,0:T(8,128)(2,1)} %pack.1.own_ref) | copy-start | bytes 786436
  28.7 19.0 %collective-permute-start.5 = (bf16[1024,128]{1,0:T(8,128)(2,1)S(1)}, bf16[1024,128]{1,0:T(8,128)(2,1)S(1)}, u32[]{:S(2)}, u32[]{:S(2)}) collective-permute-start(bf16[1024,128]{1,0:T(8,128)(2,1)S(1)} %add_convert_fusion.1), channel_id=1, source_target_pairs={{8,0},{12,4},{16,8},{20,12},{24,16},{28,20},{32,24},{36,28},{40,32... | collective-permute-start | bytes 786440 | tf_op jit(solution)/shard_map/ppermute | solution.py:310

commit v4 on v3

--- a/solution.py
+++ b/solution.py
@@ -177,7 +177,7 @@
 
 def own_kernel(
     q_ref, do_ref, qt_ref, dot_ref, own_ref, starts_ref, top_ref, inverse_ref, row_dot_ref, earlier_ref,
-    dq_ref, part_ref,
+    attended_ref, dq_ref, part_ref, att_ref,
 ):
     rows, width = q_ref.shape
     head = own_ref.shape[1]
@@ -195,6 +195,7 @@
     values = own_ref[pl.ds(rows, rows), :]
     dv = jnp.zeros((head, rows), F32)
     dk = jnp.zeros((head, rows), F32)
+    att_ref[...] = attended_ref[...]
     for h in range(heads):
         cols = pl.ds(h * head, head)
         s = jnp.where(allowed, dot_nt(q_ref[:, cols], keys), -jnp.inf)
@@ -267,9 +268,9 @@
     )
 
 
-def attention_own(q, do, qt, dot_, own, starts, top, inverse, row_dot, dq):
-    outs = [shape(q.shape, BF), shape(own.shape, BF)]
-    ins = (q, do, qt, dot_, own, starts, top, inverse, row_dot, dq)
+def attention_own(q, do, qt, dot_, own, starts, top, inverse, row_dot, dq, attended):
+    outs = [shape(q.shape, BF), shape(own.shape, BF), shape(q.shape, BF)]
+    ins = (q, do, qt, dot_, own, starts, top, inverse, row_dot, dq, attended)
     return on_core(own_kernel, "own", 2500, outs, ins)
 
 
@@ -318,26 +319,26 @@
     mixed_on = [(i, i + (3 if i % 2 else 1)) for i in range(count) if i + (3 if i % 2 else 1) < count]
     across = [(i, i ^ 1) for i in range(count)]
 
-    def back(pairs):
-        return [(there, here) for here, there in pairs]
-
     lengths = doc_lengths.reshape(1, -1)
     own = packed(keys, values)
     two = moved(own, two_on)
-    mixed = moved(own, mixed_on)
     first, starts, top, total, out, qt, dot_ = attention_before(place, lengths, queries, d_out, own)
+    own_later, first = lax.optimization_barrier((own, first))
+    mixed = moved(own_later, mixed_on)
     swapped = moved(two, across)
     attended, top, inverse, row_dot, dq, two_part, mixed_part, swapped_part = attention_earlier(
         place, first, queries, d_out, qt, dot_, starts, top, total, out, two, mixed, swapped
     )
-    d_queries, own_part = attention_own(
-        queries, d_out, qt, dot_, own, starts, top, inverse, row_dot, dq
-    )
-    from_core = moved(swapped_part, across)
-    from_mixed = moved(mixed_part, back(mixed_on))
-    passed = (two_part.astype(F32) + from_core.astype(F32)).astype(BF)
-    from_two = moved(passed, back(two_on))
-    mine = (own_part.astype(F32) + from_mixed.astype(F32) + from_two.astype(F32)).astype(BF)
+    from_next = moved(mixed_part, [(i + 1, i) for i in range(count - 1)]).astype(F32)
+    from_core = moved(swapped_part, across).astype(F32)
+    odd = (place[0] & 1) == 1
+    passed = two_part.astype(F32) + from_core + jnp.where(odd, from_next, 0.0)
+    from_two = moved(passed.astype(BF), [(there, here) for here, there in two_on]).astype(F32)
+    d_queries, own_part, attended = attention_own(
+        queries, d_out, qt, dot_, own, starts, top, inverse, row_dot, dq, attended
+    )
+    mine = own_part.astype(F32) + from_two + jnp.where(odd, 0.0, from_next)
+    mine = mine.astype(BF)
     summed = head_sum(mine)
     return (attended, d_queries, summed[:rows], summed[rows:])
 

time: 69.1 us -> 71.6 us (1.036)
  the two profiles are of different devices: /device:TPU:102 before, /device:TPU:384 now
where the time goes in v4:
time: 71.6 us; the launch traced here: 71.1 us
  blocking collectives  21.8 us (30%)
  waiting for transfers between devices  16 us (22%)
  starting transfers between devices  13 us (18%)
  Pallas kernels  12.5 us (17%)
  local copies, waits for them, and re-layouts  5.69 us (8%)
  other arithmetic  1.32 us (2%)
  between operations  0.82 us (1%)
    ppermute x6, waiting for transfers between devices, moved(): return lax.ppermute(value, 'ctx', pairs)  16 us
    ppermute x6, starting transfers between devices, moved(): return lax.ppermute(value, 'ctx', pairs)  13 us
    all_to_all x1, blocking collectives, head_sum(): theirs = lax.all_to_all(pieces, 'head', split_axis=0, concat_axis=0)  12.3 us
    pallas_call x3, Pallas kernels, on_core(): pl.pallas_call(kernel, out_shape=tuple(outs), in_specs=[SMEM if x.ndim ==...  10.8 us
    all_to_all x1, blocking collectives, head_sum(): lax.all_to_all(mine, 'head', split_axis=0, concat_axis=0)  9.55 us
    unnamed x22, local copies, waits for them, and re-layouts  4.94 us
    pallas_call x1, Pallas kernels, packed(): pl.pallas_call(pack_kernel, out_shape=jax.ShapeDtypeStruct((2 * rows, hea...  1.74 us
  transfers between devices with their start and end apart: 6, of which 4 were waited for; matrix products, arithmetic and copies ran while one was open for 0% of the time, Pallas kernels for 5%

profile of v4, /device:TPU:384, one launch (start us, length us, event | category | flops | bytes accessed | tf_op | source)
XLA Modules:
  0.0 71.1 jit_solution(2366165486946122384)
XLA Ops:
  0.6 0.0 copy-start.2
  0.6 0.0 copy-start.3
  0.7 1.7 %pack.1.own_ref = bf16[1024,128]{1,0:T(8,128)(2,1)} custom-call(bf16[512,128]{1,0:T(8,128)(2,1)} %key_ref.1, bf16[512,128]{1,0:T(8,128)(2,1)} %value_ref.1), custom_call_target="tpu_custom_call" | custom-call | tf_op jit(solution)/shard_map/pack/pallas_call | solution.py:291
  2.4 3.4 %collective-permute-start = (bf16[1024,128]{1,0:T(8,128)(2,1)}, bf16[1024,128]{1,0:T(8,128)(2,1)S(1)}, u32[]{:S(2)}, u32[]{:S(2)}) collective-permute-start(bf16[1024,128]{1,0:T(8,128)(2,1)} %pack.1.own_ref), channel_id=1, source_target_pairs={{0,8},{4,12},{8,16},{12,20},{16,24},{20,28},{24,32},{28,36},{32,40... | collective-permute-start | bytes 786440 | tf_op jit(solution)/shard_map/ppermute | solution.py:311
  5.8 0.0 copy-start.4
  5.8 0.0 copy-done.2
  5.8 0.0 copy-done.3
  5.8 0.6 copy-done.4
  6.5 0.0 copy-start
  6.5 0.9 %copy-done = bf16[1024,128]{1,0:T(8,128)(2,1)S(1)} copy-done((bf16[1024,128]{1,0:T(8,128)(2,1)S(1)}, bf16[1024,128]{1,0:T(8,128)(2,1)}, u32[]{:S(2)}) %copy-start) | copy-done | bytes 262168
  7.4 1.2 %diagonal.1 = (s32[1]{0:T(128)}, s32[512,128]{1,0:T(8,128)S(1)}, f32[2,512,128]{2,1,0:T(8,128)S(1)}, f32[2,512,128]{2,1,0:T(8,128)S(1)}, f32[2,512,128]{2,1,0:T(...) custom-call(s32[1]{0:T(128)} %bitcast.place_ref, s32[1,128]{1,0:T(1,128)S(1)} %bitcast.5, ...), custom_call_target="tpu_custom_call" | custom-call | flops 1200000000 | bytes 2097152 | tf_op jit(solution)/shard_map/diagonal/pallas_call | solution.py:229
  8.6 1.9 %collective-permute-start.1 = (bf16[1024,128]{1,0:T(8,128)(2,1)S(1)}, bf16[1024,128]{1,0:T(8,128)(2,1)S(1)}, u32[]{:S(2)}, u32[]{:S(2)}) collective-permute-start(bf16[1024,128]{1,0:T(8,128)(2,1)S(1)} %copy-done), channel_id=1, source_target_pairs={{0,4},{4,16},{8,12},{12,24},{16,20},{20,32},{24,28},{28,40},{32,36... | collective-permute-start | bytes 786440 | tf_op jit(solution)/shard_map/ppermute | solution.py:311
  10.5 5.3 %collective-permute-done.two_ref = bf16[1024,128]{1,0:T(8,128)(2,1)S(1)} collective-permute-done((bf16[1024,128]{1,0:T(8,128)(2,1)}, bf16[1024,128]{1,0:T(8,128)(2,1)S(1)}, u32[]{:S(2)}, u32[]{:S(2)}) %collective-permute-start) | collective-permute-done | bytes 262176 | tf_op jit(solution)/shard_map/ppermute | solution.py:311
  15.9 1.9 %collective-permute-start.2 = (bf16[1024,128]{1,0:T(8,128)(2,1)S(1)}, bf16[1024,128]{1,0:T(8,128)(2,1)S(1)}, u32[]{:S(2)}, u32[]{:S(2)}) collective-permute-start(bf16[1024,128]{1,0:T(8,128)(2,1)S(1)} %collective-permute-done.two_ref), channel_id=1, source_target_pairs={{0,4},{4,0},{8,12},{12,8},{16,20},{20,16},{24,28},{28,24},{32,36},... | collective-permute-start | bytes 786440 | tf_op jit(solution)/shard_map/ppermute | solution.py:311
  17.8 2.1 %collective-permute-done.1.mixed_ref = bf16[1024,128]{1,0:T(8,128)(2,1)S(1)} collective-permute-done((bf16[1024,128]{1,0:T(8,128)(2,1)S(1)}, bf16[1024,128]{1,0:T(8,128)(2,1)S(1)}, u32[]{:S(2)}, u32[]{:S(2)}) %collective-permute-start.1) | collective-permute-done | bytes 262176 | tf_op jit(solution)/shard_map/ppermute | solution.py:311
  19.9 0.0 collective-permute-done.2.swapped_ref
  19.9 7.4 %earlier.1 = (bf16[512,256]{1,0:T(8,128)(2,1)S(1)}, f32[2,512,128]{2,1,0:T(8,128)S(1)}, f32[2,512,128]{2,1,0:T(8,128)S(1)}, f32[2,512,128]{2,1,0:T(8,128)S(1)}, ...) custom-call(s32[1]{0:T(128)} %bitcast.place_ref, ...), custom_call_target="tpu_custom_call" | custom-call | flops 5000000000 | bytes 2097152 | tf_op jit(solution)/shard_map/earlier/pallas_call | solution.py:229
  27.3 0.0 copy-start.5
  27.4 0.8 %copy-done.5 = f32[2,512,128]{2,1,0:T(8,128)} copy-done((f32[2,512,128]{2,1,0:T(8,128)}, f32[2,512,128]{2,1,0:T(8,128)S(1)}, u32[]{:S(2)}) %copy-start.5) | copy-done | bytes 524312
  28.1 0.0 copy-start.7
  28.1 0.8 %copy-done.7 = f32[2,512,128]{2,1,0:T(8,128)} copy-done((f32[2,512,128]{2,1,0:T(8,128)}, f32[2,512,128]{2,1,0:T(8,128)S(1)}, u32[]{:S(2)}) %copy-start.7) | copy-done | bytes 524312
  28.9 0.0 copy-start.9
  29.0 0.7 copy-done.9
  29.7 1.9 %collective-permute-start.3 = (bf16[1024,128]{1,0:T(8,128)(2,1)S(1)}, bf16[1024,128]{1,0:T(8,128)(2,1)}, u32[]{:S(2)}, u32[]{:S(2)}) collective-permute-start(bf16[1024,128]{1,0:T(8,128)(2,1)S(1)} %get-tuple-element.42), channel_id=1, source_target_pairs={{0,4},{4,0},{8,12},{12,8},{16,20},{20,16},{24,28},{28,24},{32,36},... | collective-permute-start | bytes 786440 | tf_op jit(solution)/shard_map/ppermute | solution.py:311
  31.6 1.9 %collective-permute-start.4 = (bf16[1024,128]{1,0:T(8,128)(2,1)S(1)}, bf16[1024,128]{1,0:T(8,128)(2,1)S(1)}, u32[]{:S(2)}, u32[]{:S(2)}) collective-permute-start(bf16[1024,128]{1,0:T(8,128)(2,1)S(1)} %get-tuple-element.43), channel_id=1, source_target_pairs={{4,0},{8,4},{12,8},{16,12},{20,16},{24,20},{28,24},{32,28},{36,32}... | collective-permute-start | bytes 786440 | tf_op jit(solution)/shard_map/ppermute | solution.py:311
  33.5 0.0 collective-permute-done.3
  33.5 3.9 %collective-permute-done.4 = bf16[1024,128]{1,0:T(8,128)(2,1)S(1)} collective-permute-done((bf16[1024,128]{1,0:T(8,128)(2,1)S(1)}, bf16[1024,128]{1,0:T(8,128)(2,1)S(1)}, u32[]{:S(2)}, u32[]{:S(2)}) %collective-permute-start.4) | collective-permute-done | bytes 262176 | tf_op jit(solution)/shard_map/ppermute | solution.py:311
  37.4 0.0 copy-start.1
  37.4 0.0 copy-start.6
  37.4 0.0 copy-start.10
  37.4 1.2 %fusion.1 = bf16[1024,128]{1,0:T(8,128)(2,1)S(1)} fusion(bf16[1024,128]{1,0:T(8,128)(2,1)S(1)} %collective-permute-done.4, bf16[1024,128]{1,0:T(8,128)(2,1)} %collective-permute-done.3, bf16[1024,128]{1,0:T(8,128)(2,1)S(1)} %get-tuple-element.41, pred[]{:T(512)S(6)} %eq.3), kind=kLoop, calls=%fused_computation.3 | loop fusion | flops 917504 | bytes 1048577 | tf_op jit(solution)/shard_map/convert_element_type | solution.py:336
  38.5 1.9 %collective-permute-start.5 = (bf16[1024,128]{1,0:T(8,128)(2,1)S(1)}, bf16[1024,128]{1,0:T(8,128)(2,1)S(1)}, u32[]{:S(2)}, u32[]{:S(2)}) collective-permute-start(bf16[1024,128]{1,0:T(8,128)(2,1)S(1)} %fusion.1), channel_id=1, source_target_pairs={{8,0},{12,4},{16,8},{20,12},{24,16},{28,20},{32,24},{36,28},{40,32... | collective-permute-start | bytes 786440 | tf_op jit(solution)/shard_map/ppermute | solution.py:311
  40.5 0.0 copy-done.1
  40.5 0.0 copy-done.6
  40.5 0.0 copy-done.10
  40.5 0.0 copy-start.8
  40.5 1.0 %copy-done.8 = f32[2,512,128]{2,1,0:T(8,128)S(1)} copy-done((f32[2,512,128]{2,1,0:T(8,128)S(1)}, f32[2,512,128]{2,1,0:T(8,128)}, u32[]{:S(2)}) %copy-start.8) | copy-done | bytes 524312
  41.5 2.2 %own.1 = (bf16[512,256]{1,0:T(8,128)(2,1)}, bf16[1024,128]{1,0:T(8,128)(2,1)S(1)}, bf16[512,256]{1,0:T(8,128)(2,1)}) custom-call(bf16[512,256]{1,0:T(8,128)(2,1)S(1)} %copy-done.2, bf16[512,256]{1,0:T(8,128)(2,1)S(1)} %copy-done.3, bf16[2,128,512]{2,1,0:T(8,128)(2,1)S(1)} %get-tuple-element.24.qt_ref, bf16[2,128,512]{2,1,0:T(8,128)(2,1)S(1)} %get-tuple-element.25.dot_ref, ...), custom_call_target="tpu_custom_call" | custom-call | flops 2500000000 | bytes 2097152 | tf_op jit(solution)/shard_map/own/pallas_call | solution.py:229
  43.7 4.6 %collective-permute-done.5 = bf16[1024,128]{1,0:T(8,128)(2,1)S(1)} collective-permute-done((bf16[1024,128]{1,0:T(8,128)(2,1)S(1)}, bf16[1024,128]{1,0:T(8,128)(2,1)S(1)}, u32[]{:S(2)}, u32[]{:S(2)}) %collective-permute-start.5) | collective-permute-done | bytes 262176 | tf_op jit(solution)/shard_map/ppermute | solution.py:311
  48.3 0.1 fusion.3
  48.5 12.3 %all_to_all.10 = bf16[4,256,128]{2,1,0:T(8,128)(2,1)S(1)} all-to-all(bf16[4,256,128]{2,1,0:T(8,128)(2,1)S(1)} %bitcast.6), channel_id=1, replica_groups=mesh['ctx'=128,'head'=4] {'head'}, dimensions={0} | all-to-all | bytes 524288 | tf_op jit(solution)/shard_map/all_to_all | solution.py:304
  60.8 9.5 %all_to_all.11 = bf16[4,256,128]{2,1,0:T(8,128)(2,1)S(1)} all-to-all(bf16[4,256,128]{2,1,0:T(8,128)(2,1)S(1)} %broadcast_in_dim.13), channel_id=1, replica_groups=mesh['ctx'=128,'head'=4] {'head'}, dimensions={0} | all-to-all | bytes 524288 | tf_op jit(solution)/shard_map/all_to_all | solution.py:307
  70.4 0.7 %fusion.4 = (bf16[2,256,128]{2,1,0:T(8,128)(2,1)}, bf16[2,256,128]{2,1,0:T(8,128)(2,1)}) fusion(bf16[4,256,128]{2,1,0:T(8,128)(2,1)S(1)} %all_to_all.11), kind=kLoop, calls=%fused_computation.6 | loop fusion | bytes 524288 | tf_op jit(solution)/shard_map/slice | solution.py:343
  (2 shorter events, 0.1 us)
Async XLA Ops:
  0.6 5.2 %copy-start.2 = (bf16[512,256]{1,0:T(8,128)(2,1)S(1)}, bf16[512,256]{1,0:T(8,128)(2,1)}, u32[]{:S(2)}) copy-start(bf16[512,256]{1,0:T(8,128)(2,1)} %q_ref.5) | copy-start | bytes 786436
  0.6 5.2 %copy-start.3 = (bf16[512,256]{1,0:T(8,128)(2,1)S(1)}, bf16[512,256]{1,0:T(8,128)(2,1)}, u32[]{:S(2)}) copy-start(bf16[512,256]{1,0:T(8,128)(2,1)} %do_ref.5) | copy-start | bytes 786436
  2.4 13.5 %collective-permute-start = (bf16[1024,128]{1,0:T(8,128)(2,1)}, bf16[1024,128]{1,0:T(8,128)(2,1)S(1)}, u32[]{:S(2)}, u32[]{:S(2)}) collective-permute-start(bf16[1024,128]{1,0:T(8,128)(2,1)} %pack.1.own_ref), channel_id=1, source_target_pairs={{0,8},{4,12},{8,16},{12,20},{16,24},{20,28},{24,32},{28,36},{32,40... | collective-permute-start | bytes 786440 | tf_op jit(solution)/shard_map/ppermute | solution.py:311
  5.8 0.7 copy-start.4
  6.5 0.9 %copy-start = (bf16[1024,128]{1,0:T(8,128)(2,1)S(1)}, bf16[1024,128]{1,0:T(8,128)(2,1)}, u32[]{:S(2)}) copy-start(bf16[1024,128]{1,0:T(8,128)(2,1)} %pack.1.own_ref) | copy-start | bytes 786436
  8.6 11.3 %collective-permute-start.1 = (bf16[1024,128]{1,0:T(8,128)(2,1)S(1)}, bf16[1024,128]{1,0:T(8,128)(2,1)S(1)}, u32[]{:S(2)}, u32[]{:S(2)}) collective-permute-start(bf16[1024,128]{1,0:T(8,128)(2,1)S(1)} %copy-done), channel_id=1, source_target_pairs={{0,4},{4,16},{8,12},{12,24},{16,20},{20,32},{24,28},{28,40},{32,36... | collective-permute-start | bytes 786440 | tf_op jit(solution)/shard_map/ppermute | solution.py:311
  15.9 4.0 %collective-permute-start.2 = (bf16[1024,128]{1,0:T(8,128)(2,1)S(1)}, bf16[1024,128]{1,0:T(8,128)(2,1)S(1)}, u32[]{:S(2)}, u32[]{:S(2)}) collective-permute-start(bf16[1024,128]{1,0:T(8,128)(2,1)S(1)} %collective-permute-done.two_ref), channel_id=1, source_target_pairs={{0,4},{4,0},{8,12},{12,8},{16,20},{20,16},{24,28},{28,24},{32,36},... | collective-permute-start | bytes 786440 | tf_op jit(solution)/shard_map/ppermute | solution.py:311
  27.3 0.8 %copy-start.5 = (f32[2,512,128]{2,1,0:T(8,128)}, f32[2,512,128]{2,1,0:T(8,128)S(1)}, u32[]{:S(2)}) copy-start(f32[2,512,128]{2,1,0:T(8,128)S(1)} %get-tuple-element.35.row_dot_ref) | copy-start | bytes 1572868
  28.1 0.8 %copy-start.7 = (f32[2,512,128]{2,1,0:T(8,128)}, f32[2,512,128]{2,1,0:T(8,128)S(1)}, u32[]{:S(2)}) copy-start(f32[2,512,128]{2,1,0:T(8,128)S(1)} %get-tuple-element.36.earlier_ref) | copy-start | bytes 1572868
  28.9 0.7 copy-start.9
  29.7 3.8 %collective-permute-start.3 = (bf16[1024,128]{1,0:T(8,128)(2,1)S(1)}, bf16[1024,128]{1,0:T(8,128)(2,1)}, u32[]{:S(2)}, u32[]{:S(2)}) collective-permute-start(bf16[1024,128]{1,0:T(8,128)(2,1)S(1)} %get-tuple-element.42), channel_id=1, source_target_pairs={{0,4},{4,0},{8,12},{12,8},{16,20},{20,16},{24,28},{28,24},{32,36},... | collective-permute-start | bytes 786440 | tf_op jit(solution)/shard_map/ppermute | solution.py:311
  31.6 5.8 %collective-permute-start.4 = (bf16[1024,128]{1,0:T(8,128)(2,1)S(1)}, bf16[1024,128]{1,0:T(8,128)(2,1)S(1)}, u32[]{:S(2)}, u32[]{:S(2)}) collective-permute-start(bf16[1024,128]{1,0:T(8,128)(2,1)S(1)} %get-tuple-element.43), channel_id=1, source_target_pairs={{4,0},{8,4},{12,8},{16,12},{20,16},{24,20},{28,24},{32,28},{36,32}... | collective-permute-start | bytes 786440 | tf_op jit(solution)/shard_map/ppermute | solution.py:311
  37.4 3.1 %copy-start.1 = (bf16[1024,128]{1,0:T(8,128)(2,1)S(1)}, bf16[1024,128]{1,0:T(8,128)(2,1)}, u32[]{:S(2)}) copy-start(bf16[1024,128]{1,0:T(8,128)(2,1)} %pack.1.own_ref) | copy-start | bytes 786436
  37.4 3.1 %copy-start.6 = (f32[2,512,128]{2,1,0:T(8,128)S(1)}, f32[2,512,128]{2,1,0:T(8,128)}, u32[]{:S(2)}) copy-start(f32[2,512,128]{2,1,0:T(8,128)} %copy-done.5) | copy-start | bytes 1572868
  37.4 3.1 %copy-start.10 = (bf16[512,256]{1,0:T(8,128)(2,1)S(1)}, bf16[512,256]{1,0:T(8,128)(2,1)}, u32[]{:S(2)}) copy-start(bf16[512,256]{1,0:T(8,128)(2,1)} %copy-done.9) | copy-start | bytes 786436
  38.5 9.8 %collective-permute-start.5 = (bf16[1024,128]{1,0:T(8,128)(2,1)S(1)}, bf16[1024,128]{1,0:T(8,128)(2,1)S(1)}, u32[]{:S(2)}, u32[]{:S(2)}) collective-permute-start(bf16[1024,128]{1,0:T(8,128)(2,1)S(1)} %fusion.1), channel_id=1, source_target_pairs={{8,0},{12,4},{16,8},{20,12},{24,16},{28,20},{32,24},{36,28},{40,32... | collective-permute-start | bytes 786440 | tf_op jit(solution)/shard_map/ppermute | solution.py:311
  40.5 1.0 %copy-start.8 = (f32[2,512,128]{2,1,0:T(8,128)S(1)}, f32[2,512,128]{2,1,0:T(8,128)}, u32[]{:S(2)}) copy-start(f32[2,512,128]{2,1,0:T(8,128)} %copy-done.7) | copy-start | bytes 1572868

commit v5 on v4

--- a/solution.py
+++ b/solution.py
@@ -19,6 +19,22 @@
 
 def dot_nn(a, b):
     return jnp.dot(a, b, preferred_element_type=F32)
+
+
+def wide(x, width):
+    return jnp.concatenate([x] * (width // x.shape[1]), axis=1)
+
+
+def folded(x, width, op):
+    return functools.reduce(op, [x[:, c : c + width] for c in range(0, x.shape[1], width)])
+
+
+def across_lanes(x, op, like):
+    return jnp.broadcast_to(op(x, axis=1, keepdims=True), like.shape)
+
+
+def lowest_block(first_ref, rows):
+    return jnp.minimum(jnp.maximum(first_ref[0], 0) // rows, SPAN)
 
 
 def diagonal_kernel(
@@ -59,54 +75,81 @@
         dot_ref[h] = do_ref[:, cols].T
 
 
-def earlier_kernel(
+def second_kernel(
+    first_ref, q_ref, starts_ref, top0_ref, total0_ref, out0_ref, block_ref,
+    top_ref, total_ref, out_ref, tile_ref,
+):
+    rows, width = q_ref.shape
+    head = block_ref.shape[1]
+    heads = width // head
+    to_exp2 = exp2_scale(head)
+    place = SPAN - 2
+    live = lowest_block(first_ref, rows) <= place
+
+    @pl.when(live)
+    def _():
+        keys = block_ref[pl.ds(0, rows), :]
+        values = block_ref[pl.ds(rows, rows), :]
+        column = lax.broadcasted_iota(jnp.int32, (rows, rows), 1)
+        allowed = column >= wide(starts_ref[...] + (SPAN - place) * rows, rows)
+        for h in range(heads):
+            s = jnp.where(allowed, dot_nt(q_ref[:, pl.ds(h * head, head)], keys), -jnp.inf)
+            top0 = top0_ref[h]
+            top = across_lanes(jnp.maximum(folded(s, head, jnp.maximum), top0), jnp.max, top0)
+            e = jnp.exp2((s - wide(top, rows)) * to_exp2)
+            kept = jnp.exp2((top0 - top) * to_exp2)
+            tile_ref[h] = e
+            top_ref[h] = top
+            total_ref[h] = total0_ref[h] * kept + across_lanes(folded(e, head, jnp.add), jnp.sum, top)
+            out_ref[h] = out0_ref[h] * kept + dot_nn(e.astype(BF), values)
+
+    @pl.when(jnp.logical_not(live))
+    def _():
+        top_ref[...] = top0_ref[...]
+        total_ref[...] = total0_ref[...]
+        out_ref[...] = out0_ref[...]
+
+
+def far_kernel(
     place_ref, first_ref, q_ref, do_ref, qt_ref, dot_ref, starts_ref, top0_ref, total0_ref, out0_ref,
-    two_ref, mixed_ref, swapped_ref,
-    att_ref, top_ref, inverse_ref, row_dot_ref, dq_ref, two_part_ref, mixed_part_ref, swapped_part_ref,
+    mixed_ref, swapped_ref,
+    att_ref, top_ref, inverse_ref, row_dot_ref, second_ref, dq_ref, mixed_part_ref, swapped_part_ref,
     key_window, value_window, key_parts, value_parts, tiles, lanes,
 ):
     rows, width = q_ref.shape
-    head = two_ref.shape[1]
+    head = mixed_ref.shape[1]
     heads = width // head
     to_exp2 = exp2_scale(head)
     scale = score_scale(head)
     odd = lax.rem(place_ref[0], 2)
-    last = (SPAN - 1) * rows
-    mixed_row = pl.multiple_of(jnp.where(odd == 1, last, 0), rows)
-    swapped_row = pl.multiple_of(jnp.where(odd == 1, 0, last), rows)
+    mixed_row = pl.multiple_of((1 - odd) * rows, rows)
+    swapped_row = pl.multiple_of(odd * rows, rows)
     slots = (
-        (two_ref, two_part_ref, last - rows),
         (mixed_ref, mixed_part_ref, mixed_row),
         (swapped_ref, swapped_part_ref, swapped_row),
     )
-    low = jnp.minimum(jnp.maximum(first_ref[0], 0) // rows, SPAN)
+    low = lowest_block(first_ref, rows)
+    live = (low < SPAN).astype(jnp.int32) + (low < 1).astype(jnp.int32)
     column = lax.broadcasted_iota(jnp.int32, (rows, rows), 1)
-
-    def wide(x):
-        return jnp.concatenate([x] * (rows // head), axis=1)
-
-    def folded(x, op):
-        parts = [x[:, c : c + head] for c in range(0, rows, head)]
-        return functools.reduce(op, parts)
 
     def score_tile(t, carry):
         at = pl.multiple_of(t * rows, rows)
         keys = key_window[pl.ds(at, rows), :]
-        allowed = column >= wide(starts_ref[...] + (SPAN * rows - at))
+        allowed = column >= wide(starts_ref[...] + (rows + 2 * at), rows)
         for h in range(heads):
             s = dot_nt(q_ref[:, pl.ds(h * head, head)], keys)
             s = jnp.where(allowed, s, -jnp.inf)
             tiles[h, t] = s
-            lanes[h] = jnp.maximum(lanes[h], folded(s, jnp.maximum))
+            lanes[h] = jnp.maximum(lanes[h], folded(s, head, jnp.maximum))
         return carry
 
     def out_tile(t, carry):
         at = pl.multiple_of(t * rows, rows)
         values = value_window[pl.ds(at, rows), :]
         for h in range(heads):
-            e = jnp.exp2((tiles[h, t] - wide(top_ref[h])) * to_exp2)
+            e = jnp.exp2((tiles[h, t] - wide(top_ref[h], rows)) * to_exp2)
             tiles[h, t] = e
-            lanes[h] += folded(e, jnp.add)
+            lanes[h] += folded(e, head, jnp.add)
             dq_ref[h] += dot_nn(e.astype(BF), values)
         return carry
 
@@ -118,8 +161,8 @@
         dk = jnp.zeros((head, rows), F32)
         for h in range(heads):
             dw = dot_nt(do_ref[:, pl.ds(h * head, head)], values)
-            w = tiles[h, t] * wide(inverse_ref[h])
-            ds = (w * (dw - wide(row_dot_ref[h]))).astype(BF)
+            w = tiles[h, t] * wide(inverse_ref[h], rows)
+            ds = (w * (dw - wide(row_dot_ref[h], rows))).astype(BF)
             dv = dv + dot_nn(dot_ref[h], w.astype(BF))
             dk = dk + dot_nn(qt_ref[h], ds)
             dq_ref[h] += dot_nn(ds, keys)
@@ -133,29 +176,29 @@
         value_parts[pl.ds(at, rows), :] = jnp.zeros((rows, head), BF)
         return carry
 
-    reaches = low < SPAN
-
-    @pl.when(reaches)
+    @pl.when(live > 0)
     def _():
         for block, _, at in slots:
             key_window[pl.ds(at, rows), :] = block[pl.ds(0, rows), :]
             value_window[pl.ds(at, rows), :] = block[pl.ds(rows, rows), :]
         lanes[...] = top0_ref[...]
-        lax.fori_loop(low, SPAN, score_tile, 0)
-        for h in range(heads):
-            top = jnp.broadcast_to(jnp.max(lanes[h], axis=1, keepdims=True), (rows, head))
+        lax.fori_loop(0, live, score_tile, 0)
+        for h in range(heads):
+            top = across_lanes(lanes[h], jnp.max, lanes[h])
             top_ref[h] = top
             kept = jnp.exp2((top0_ref[h] - top) * to_exp2)
+            second_ref[h] = kept
             inverse_ref[h] = total0_ref[h] * kept
             dq_ref[h] = out0_ref[h] * kept
         lanes[...] = jnp.zeros(lanes.shape, F32)
-        lax.fori_loop(low, SPAN, out_tile, 0)
+        lax.fori_loop(0, live, out_tile, 0)
         for h in range(heads):
             inverse_ref[h] += jnp.sum(lanes[h], axis=1, keepdims=True)
 
-    @pl.when(jnp.logical_not(reaches))
+    @pl.when(live == 0)
     def _():
         top_ref[...] = top0_ref[...]
+        second_ref[...] = jnp.ones(second_ref.shape, F32)
         inverse_ref[...] = total0_ref[...]
         dq_ref[...] = out0_ref[...]
 
@@ -163,16 +206,47 @@
         cols = pl.ds(h * head, head)
         inverse = 1.0 / inverse_ref[h]
         inverse_ref[h] = inverse
+        second_ref[h] = second_ref[h] * inverse
         attended = (dq_ref[h] * inverse).astype(BF)
         att_ref[:, cols] = attended
         row_dot = jnp.sum(do_ref[:, cols].astype(F32) * attended.astype(F32), axis=1, keepdims=True)
         row_dot_ref[h] = jnp.broadcast_to(row_dot, (rows, head))
     dq_ref[...] = jnp.zeros(dq_ref.shape, F32)
-    lax.fori_loop(0, low, zero_tile, 0)
-    lax.fori_loop(low, SPAN, grad_tile, 0)
+    lax.fori_loop(0, live, grad_tile, 0)
+    lax.fori_loop(live, 2, zero_tile, 0)
     for _, part, at in slots:
         part[pl.ds(0, rows), :] = key_parts[pl.ds(at, rows), :]
         part[pl.ds(rows, rows), :] = value_parts[pl.ds(at, rows), :]
+
+
+def second_back_kernel(
+    first_ref, do_ref, qt_ref, dot_ref, block_ref, tile_ref, factor_ref, row_dot_ref, far_ref,
+    dq_ref, part_ref,
+):
+    heads, rows, head = far_ref.shape
+    scale = score_scale(head)
+    live = lowest_block(first_ref, rows) <= SPAN - 2
+
+    @pl.when(live)
+    def _():
+        keys = block_ref[pl.ds(0, rows), :]
+        values = block_ref[pl.ds(rows, rows), :]
+        dv = jnp.zeros((head, rows), F32)
+        dk = jnp.zeros((head, rows), F32)
+        for h in range(heads):
+            dw = dot_nt(do_ref[:, pl.ds(h * head, head)], values)
+            w = tile_ref[h] * wide(factor_ref[h], rows)
+            ds = (w * (dw - wide(row_dot_ref[h], rows))).astype(BF)
+            dv = dv + dot_nn(dot_ref[h], w.astype(BF))
+            dk = dk + dot_nn(qt_ref[h], ds)
+            dq_ref[h] = far_ref[h] + dot_nn(ds, keys)
+        part_ref[pl.ds(0, rows), :] = (dk * scale).T.astype(BF)
+        part_ref[pl.ds(rows, rows), :] = dv.T.astype(BF)
+
+    @pl.when(jnp.logical_not(live))
+    def _():
+        dq_ref[...] = far_ref[...]
+        part_ref[...] = jnp.zeros(part_ref.shape, BF)
 
 
 def own_kernel(
@@ -186,11 +260,7 @@
     scale = score_scale(head)
     column = lax.broadcasted_iota(jnp.int32, (rows, rows), 1)
     row = lax.broadcasted_iota(jnp.int32, (rows, rows), 0)
-
-    def wide(x):
-        return jnp.concatenate([x] * (rows // head), axis=1)
-
-    allowed = (column >= wide(starts_ref[...])) & (column <= row)
+    allowed = (column >= wide(starts_ref[...], rows)) & (column <= row)
     keys = own_ref[pl.ds(0, rows), :]
     values = own_ref[pl.ds(rows, rows), :]
     dv = jnp.zeros((head, rows), F32)
@@ -199,9 +269,9 @@
     for h in range(heads):
         cols = pl.ds(h * head, head)
         s = jnp.where(allowed, dot_nt(q_ref[:, cols], keys), -jnp.inf)
-        w = jnp.exp2((s - wide(top_ref[h])) * to_exp2) * wide(inverse_ref[h])
+        w = jnp.exp2((s - wide(top_ref[h], rows)) * to_exp2) * wide(inverse_ref[h], rows)
         dw = dot_nt(do_ref[:, cols], values)
-        ds = (w * (dw - wide(row_dot_ref[h]))).astype(BF)
+        ds = (w * (dw - wide(row_dot_ref[h], rows))).astype(BF)
         dv = dv + dot_nn(dot_ref[h], w.astype(BF))
         dk = dk + dot_nn(qt_ref[h], ds)
         dq_ref[:, cols] = ((earlier_ref[h] + dot_nn(ds, keys)) * scale).astype(BF)
@@ -209,6 +279,12 @@
     part_ref[pl.ds(rows, rows), :] = dv.T.astype(BF)
 
 
+def merge_kernel(weight_ref, a_ref, b_ref, c_ref, out_ref):
+    weight = weight_ref[0].astype(F32)
+    out = a_ref[...].astype(F32) + b_ref[...].astype(F32) + weight * c_ref[...].astype(F32)
+    out_ref[...] = out.astype(BF)
+
+
 def score_scale(head):
     return 1.0 / math.sqrt(head)
 
@@ -225,14 +301,15 @@
     return jax.ShapeDtypeStruct(dims, dtype)
 
 
-def on_core(kernel, name, mflop, outs, ins, scratch=()):
+def on_core(kernel, name, mflop, mib, outs, ins, scratch=(), aliases={}):
     return pl.pallas_call(
         kernel,
         out_shape=tuple(outs),
         in_specs=[SMEM if x.ndim == 1 else VMEM for x in ins],
         out_specs=tuple(SMEM if len(x.shape) == 1 else VMEM for x in outs),
         scratch_shapes=list(scratch),
-        compiler_params=pltpu.CompilerParams(vmem_limit_bytes=40 << 20),
+        input_output_aliases=aliases,
+        compiler_params=pltpu.CompilerParams(vmem_limit_bytes=mib << 20),
         cost_estimate=pl.CostEstimate(
             flops=mflop * 1_000_000, bytes_accessed=2 << 20, transcendentals=1 << 19
         ),
@@ -240,38 +317,58 @@
     )(*ins)
 
 
-def attention_before(place, lengths, q, do, own):
+def sizes(q, own):
     rows, width = q.shape
     head = own.shape[1]
     heads = width // head
     state = shape((heads, rows, head), F32)
     turned = shape((heads, head, rows), BF)
-    outs = [shape((1,), jnp.int32), shape((rows, head), jnp.int32), state, state, state, turned, turned]
-    return on_core(diagonal_kernel, "diagonal", 1200, outs, (place, lengths, q, do, own))
-
-
-def attention_earlier(place, first, q, do, qt, dot_, starts, top, total, out, two, mixed, swapped):
-    rows, width = q.shape
-    head = two.shape[1]
-    heads = width // head
-    state = shape((heads, rows, head), F32)
-    part = shape(two.shape, BF)
-    span = SPAN * rows
+    tile = shape((heads, rows, rows), F32)
+    return state, turned, tile, shape(q.shape, BF), shape(own.shape, BF)
+
+
+def attention_before(place, lengths, q, do, own):
+    state, turned, _, _, _ = sizes(q, own)
+    starts = shape(state.shape[1:], jnp.int32)
+    outs = [shape((1,), jnp.int32), starts, state, state, state, turned, turned]
+    return on_core(diagonal_kernel, "diagonal", 1200, 20, outs, (place, lengths, q, do, own))
+
+
+def attention_second(first, q, starts, top, total, out, two):
+    state, _, tile, _, _ = sizes(q, two)
+    ins = (first, q, starts, top, total, out, two)
+    return on_core(second_kernel, "second", 1200, 20, [state, state, state, tile], ins)
+
+
+def attention_far(place, first, q, do, qt, dot_, starts, top, total, out, mixed, swapped):
+    state, _, tile, like_q, part = sizes(q, mixed)
+    rows, head = state.shape[1:]
     return on_core(
-        earlier_kernel,
-        "earlier",
-        5000,
-        [shape(q.shape, BF), state, state, state, state, part, part, part],
-        (place, first, q, do, qt, dot_, starts, top, total, out, two, mixed, swapped),
-        [pltpu.VMEM((span, head), BF)] * 4
-        + [pltpu.VMEM((heads, SPAN, rows, rows), F32), pltpu.VMEM((heads, rows, head), F32)],
-    )
+        far_kernel,
+        "far",
+        3000,
+        24,
+        [like_q] + [state] * 5 + [part] * 2,
+        (place, first, q, do, qt, dot_, starts, top, total, out, mixed, swapped),
+        [pltpu.VMEM((2 * rows, head), BF)] * 4
+        + [pltpu.VMEM((state.shape[0], 2, rows, rows), F32), pltpu.VMEM(state.shape, F32)],
+    )
+
+
+def attention_second_back(first, q, do, qt, dot_, two, tile, factor, row_dot, dq):
+    state, _, _, _, part = sizes(q, two)
+    ins = (first, do, qt, dot_, two, tile, factor, row_dot, dq)
+    return on_core(second_back_kernel, "second_back", 1500, 20, [state, part], ins)
 
 
 def attention_own(q, do, qt, dot_, own, starts, top, inverse, row_dot, dq, attended):
-    outs = [shape(q.shape, BF), shape(own.shape, BF), shape(q.shape, BF)]
+    _, _, _, like_q, part = sizes(q, own)
     ins = (q, do, qt, dot_, own, starts, top, inverse, row_dot, dq, attended)
-    return on_core(own_kernel, "own", 2500, outs, ins)
+    return on_core(own_kernel, "own", 2500, 20, [like_q, part, like_q], ins)
+
+
+def merged(weight, a, b, c):
+    return on_core(merge_kernel, "merge", 1, 6, [shape(a.shape, BF)], (weight, a, b, c))[0]
 
 
 def pack_kernel(key_ref, value_ref, both_ref, sems):
@@ -292,7 +389,7 @@
         pack_kernel,
         out_shape=jax.ShapeDtypeStruct((2 * rows, head), BF),
         in_specs=[pl.BlockSpec(memory_space=pl.ANY)] * 2,
-        out_specs=pl.BlockSpec(memory_space=pltpu.VMEM),
+        out_specs=pl.BlockSpec(memory_space=pl.ANY),
         scratch_shapes=[pltpu.SemaphoreType.DMA((2,))],
         name="pack",
     )(keys, values)
@@ -326,19 +423,22 @@
     own_later, first = lax.optimization_barrier((own, first))
     mixed = moved(own_later, mixed_on)
     swapped = moved(two, across)
-    attended, top, inverse, row_dot, dq, two_part, mixed_part, swapped_part = attention_earlier(
-        place, first, queries, d_out, qt, dot_, starts, top, total, out, two, mixed, swapped
-    )
-    from_next = moved(mixed_part, [(i + 1, i) for i in range(count - 1)]).astype(F32)
-    from_core = moved(swapped_part, across).astype(F32)
-    odd = (place[0] & 1) == 1
-    passed = two_part.astype(F32) + from_core + jnp.where(odd, from_next, 0.0)
-    from_two = moved(passed.astype(BF), [(there, here) for here, there in two_on]).astype(F32)
+    top, total, out, tile = attention_second(first, queries, starts, top, total, out, two)
+    attended, top, inverse, row_dot, factor, dq, mixed_part, swapped_part = attention_far(
+        place, first, queries, d_out, qt, dot_, starts, top, total, out, mixed, swapped
+    )
+    from_next = moved(mixed_part, [(i + 1, i) for i in range(count - 1)])
+    from_core = moved(swapped_part, across)
+    dq, two_part = attention_second_back(
+        first, queries, d_out, qt, dot_, two, tile, factor, row_dot, dq
+    )
+    odd = place & 1
+    passed = merged(odd, two_part, from_core, from_next)
+    from_two = moved(passed, [(there, here) for here, there in two_on])
     d_queries, own_part, attended = attention_own(
         queries, d_out, qt, dot_, own, starts, top, inverse, row_dot, dq, attended
     )
-    mine = own_part.astype(F32) + from_two + jnp.where(odd, 0.0, from_next)
-    mine = mine.astype(BF)
+    mine = merged(1 - odd, own_part, from_two, from_next)
     summed = head_sum(mine)
     return (attended, d_queries, summed[:rows], summed[rows:])
 

time: 71.6 us -> 76.4 us (1.067)
  Pallas kernels: 12.5 us -> 21.8 us
  waiting for transfers between devices: 16 us -> 11.4 us
  starting transfers between devices: 13 us -> 16.9 us
  local copies, waits for them, and re-layouts: 5.69 us -> 3.31 us
  other arithmetic: 1.32 us -> 0.04 us
    pallas_call x1, Pallas kernels: 1.74 us -> 9.06 us  [packed(): pl.pallas_call(pack_kernel, out_shape=jax.ShapeDtypeStruct((2 * rows, hea...]
    ppermute x6, waiting for transfers between devices: 16 us -> 11.4 us  [moved(): return lax.ppermute(value, 'ctx', pairs)]
    ppermute x6, starting transfers between devices: 13 us -> 16.9 us  [moved(): return lax.ppermute(value, 'ctx', pairs)]
    unnamed x22 -> x10, local copies, waits for them, and re-layouts: 4.94 us -> 2.56 us
    pallas_call x3 -> x7, Pallas kernels: 10.8 us -> 12.8 us  [on_core(): pl.pallas_call(kernel, out_shape=tuple(outs), in_specs=[SMEM if x.ndim ==...]
    convert_element_type x2 -> x0, other arithmetic: 1.28 us -> none  [the longest x1 1.16 us: on_device(): passed.astype(BF)]
  transfers between devices with their start and end apart: 6 -> 6, of which waited for: 4 -> 4; matrix products, arithmetic and copies ran while one was open for 0% -> 0% of each run, Pallas kernels for 5% -> 12%
where the time goes in v5:
time: 76.4 us; the launch traced here: 75.9 us
  Pallas kernels  21.8 us (29%)
  blocking collectives  21.7 us (28%)
  starting transfers between devices  16.9 us (22%)
  waiting for transfers between devices  11.4 us (15%)
  local copies, waits for them, and re-layouts  3.31 us (4%)
  between operations  0.78 us (1%)
    ppermute x6, starting transfers between devices, moved(): return lax.ppermute(value, 'ctx', pairs)  16.9 us
    pallas_call x7, Pallas kernels, on_core(): pl.pallas_call(kernel, out_shape=tuple(outs), in_specs=[SMEM if x.ndim ==...  12.8 us
    all_to_all x1, blocking collectives, head_sum(): theirs = lax.all_to_all(pieces, 'head', split_axis=0, concat_axis=0)  11.7 us
    ppermute x6, waiting for transfers between devices, moved(): return lax.ppermute(value, 'ctx', pairs)  11.4 us
    all_to_all x1, blocking collectives, head_sum(): lax.all_to_all(mine, 'head', split_axis=0, concat_axis=0)  9.96 us
    pallas_call x1, Pallas kernels, packed(): pl.pallas_call(pack_kernel, out_shape=jax.ShapeDtypeStruct((2 * rows, hea...  9.06 us
    unnamed x10, local copies, waits for them, and re-layouts  2.56 us
  transfers between devices with their start and end apart: 6, of which 4 were waited for; matrix products, arithmetic and copies ran while one was open for 0% of the time, Pallas kernels for 12%

profile of v5, /device:TPU:384, one launch (start us, length us, event | category | flops | bytes accessed | tf_op | source)
XLA Modules:
  0.0 75.9 jit_solution(13810409192502054510)
XLA Ops:
  0.6 9.1 %pack.1.own_ref = bf16[1024,128]{1,0:T(8,128)(2,1)} custom-call(bf16[512,128]{1,0:T(8,128)(2,1)} %key_ref.1, bf16[512,128]{1,0:T(8,128)(2,1)} %value_ref.1), custom_call_target="tpu_custom_call" | custom-call | tf_op jit(solution)/shard_map/pack/pallas_call | solution.py:388
  9.7 3.4 %collective-permute-start = (bf16[1024,128]{1,0:T(8,128)(2,1)}, bf16[1024,128]{1,0:T(8,128)(2,1)S(1)}, u32[]{:S(2)}, u32[]{:S(2)}) collective-permute-start(bf16[1024,128]{1,0:T(8,128)(2,1)} %pack.1.own_ref), channel_id=1, source_target_pairs={{0,8},{4,12},{8,16},{12,20},{16,24},{20,28},{24,32},{28,36},{32,40... | collective-permute-start | bytes 786440 | tf_op jit(solution)/shard_map/ppermute | solution.py:408
  13.1 0.0 copy-start
  13.1 0.9 %copy-done = bf16[512,256]{1,0:T(8,128)(2,1)S(1)} copy-done((bf16[512,256]{1,0:T(8,128)(2,1)S(1)}, bf16[512,256]{1,0:T(8,128)(2,1)}, u32[]{:S(2)}) %copy-start) | copy-done | bytes 262168
  14.1 0.0 copy-start.2
  14.1 0.9 %copy-done.2 = bf16[512,256]{1,0:T(8,128)(2,1)S(1)} copy-done((bf16[512,256]{1,0:T(8,128)(2,1)S(1)}, bf16[512,256]{1,0:T(8,128)(2,1)}, u32[]{:S(2)}) %copy-start.2) | copy-done | bytes 262168
  15.0 0.0 copy-start.4
  15.0 0.7 copy-done.4
  15.7 0.0 copy-start.1
  15.7 2.2 %diagonal.1 = (s32[1]{0:T(128)}, s32[512,128]{1,0:T(8,128)S(1)}, f32[2,512,128]{2,1,0:T(8,128)S(1)}, f32[2,512,128]{2,1,0:T(8,128)S(1)}, f32[2,512,128]{2,1,0:T(...) custom-call(s32[1]{0:T(128)} %bitcast.place_ref, s32[1,128]{1,0:T(1,128)S(1)} %bitcast.6, ...), custom_call_target="tpu_custom_call" | custom-call | flops 1200000000 | bytes 2097152 | tf_op jit(solution)/shard_map/diagonal/pallas_call | solution.py:305
  17.9 1.9 %collective-permute-start.1 = (bf16[1024,128]{1,0:T(8,128)(2,1)}, bf16[1024,128]{1,0:T(8,128)(2,1)S(1)}, u32[]{:S(2)}, u32[]{:S(2)}) collective-permute-start(bf16[1024,128]{1,0:T(8,128)(2,1)} %pack.1.own_ref), channel_id=1, source_target_pairs={{0,4},{4,16},{8,12},{12,24},{16,20},{20,32},{24,28},{28,40},{32,36... | collective-permute-start | bytes 786440 | tf_op jit(solution)/shard_map/ppermute | solution.py:408
  19.8 3.4 %collective-permute-done.block_ref = bf16[1024,128]{1,0:T(8,128)(2,1)S(1)} collective-permute-done((bf16[1024,128]{1,0:T(8,128)(2,1)}, bf16[1024,128]{1,0:T(8,128)(2,1)S(1)}, u32[]{:S(2)}, u32[]{:S(2)}) %collective-permute-start) | collective-permute-done | bytes 262176 | tf_op jit(solution)/shard_map/ppermute | solution.py:408
  23.2 1.9 %collective-permute-start.2 = (bf16[1024,128]{1,0:T(8,128)(2,1)S(1)}, bf16[1024,128]{1,0:T(8,128)(2,1)S(1)}, u32[]{:S(2)}, u32[]{:S(2)}) collective-permute-start(bf16[1024,128]{1,0:T(8,128)(2,1)S(1)} %collective-permute-done.block_ref), channel_id=1, source_target_pairs={{0,4},{4,0},{8,12},{12,8},{16,20},{20,16},{24,28},{28,24},{32,36},... | collective-permute-start | bytes 786440 | tf_op jit(solution)/shard_map/ppermute | solution.py:408
  25.1 0.0 copy-done.1
  25.1 0.0 copy-start.3
  25.1 1.9 %second.1 = (f32[2,512,128]{2,1,0:T(8,128)S(1)}, f32[2,512,128]{2,1,0:T(8,128)S(1)}, f32[2,512,128]{2,1,0:T(8,128)S(1)}, f32[2,512,512]{2,1,0:T(8,128)S(1)}) custom-call(s32[1]{0:T(128)} %get-tuple-element.34.first_ref, bf16[512,256]{1,0:T(8,128)(2,1)S(1)} %copy-done.1, s32[512,128]{1,0:T(8,128)S(1)} %get-tuple-element.32.starts_ref, ...), custom_call_target="tpu_custom_call" | custom-call | flops 1200000000 | bytes 2097152 | tf_op jit(solution)/shard_map/second/pallas_call | solution.py:305
  27.0 2.4 %collective-permute-done.1.mixed_ref = bf16[1024,128]{1,0:T(8,128)(2,1)S(1)} collective-permute-done((bf16[1024,128]{1,0:T(8,128)(2,1)}, bf16[1024,128]{1,0:T(8,128)(2,1)S(1)}, u32[]{:S(2)}, u32[]{:S(2)}) %collective-permute-start.1) | collective-permute-done | bytes 262176 | tf_op jit(solution)/shard_map/ppermute | solution.py:408
  29.4 0.0 collective-permute-done.2.swapped_ref
  29.4 0.0 copy-done.3
  29.4 3.6 %far.1 = (bf16[512,256]{1,0:T(8,128)(2,1)S(1)}, f32[2,512,128]{2,1,0:T(8,128)S(1)}, f32[2,512,128]{2,1,0:T(8,128)S(1)}, f32[2,512,128]{2,1,0:T(8,128)S(1)}, f32[...) custom-call(s32[1]{0:T(128)} %bitcast.place_ref, ...), custom_call_target="tpu_custom_call" | custom-call | flops 3000000000 | bytes 2097152 | tf_op jit(solution)/shard_map/far/pallas_call | solution.py:305
  33.0 1.9 %collective-permute-start.3 = (bf16[1024,128]{1,0:T(8,128)(2,1)S(1)}, bf16[1024,128]{1,0:T(8,128)(2,1)S(1)}, u32[]{:S(2)}, u32[]{:S(2)}) collective-permute-start(bf16[1024,128]{1,0:T(8,128)(2,1)S(1)} %get-tuple-element.54), channel_id=1, source_target_pairs={{0,4},{4,0},{8,12},{12,8},{16,20},{20,16},{24,28},{28,24},{32,36},... | collective-permute-start | bytes 786440 | tf_op jit(solution)/shard_map/ppermute | solution.py:408
  34.9 5.8 %collective-permute-start.4 = (bf16[1024,128]{1,0:T(8,128)(2,1)S(1)}, bf16[1024,128]{1,0:T(8,128)(2,1)S(1)}, u32[]{:S(2)}, u32[]{:S(2)}) collective-permute-start(bf16[1024,128]{1,0:T(8,128)(2,1)S(1)} %get-tuple-element.55), channel_id=1, source_target_pairs={{4,0},{8,4},{12,8},{16,12},{20,16},{24,20},{28,24},{32,28},{36,32}... | collective-permute-start | bytes 786440 | tf_op jit(solution)/shard_map/ppermute | solution.py:408
  40.7 1.7 %second_back.1 = (f32[2,512,128]{2,1,0:T(8,128)S(1)}, bf16[1024,128]{1,0:T(8,128)(2,1)S(1)}) custom-call(s32[1]{0:T(128)} %get-tuple-element.34.first_ref, bf16[512,256]{1,0:T(8,128)(2,1)S(1)} %copy-done.3, bf16[2,128,512]{2,1,0:T(8,128)(2,1)S(1)} %get-tuple-element.30.qt_ref, bf16[2,128,512]{2,1,0:T(8,128)(2,1)S(1)} %get-tuple-element.31.dot_ref, ...), custom_call_target="tpu_custom_call" | custom-call | flops 1500000000 | bytes 2097152 | tf_op jit(solution)/shard_map/second_back/pallas_call | solution.py:305
  42.4 0.0 collective-permute-done.3.b_ref
  42.5 2.1 %collective-permute-done.4.c_ref = bf16[1024,128]{1,0:T(8,128)(2,1)S(1)} collective-permute-done((bf16[1024,128]{1,0:T(8,128)(2,1)S(1)}, bf16[1024,128]{1,0:T(8,128)(2,1)S(1)}, u32[]{:S(2)}, u32[]{:S(2)}) %collective-permute-start.4) | collective-permute-done | bytes 262176 | tf_op jit(solution)/shard_map/ppermute | solution.py:408
  44.6 0.1 merge.2
  44.7 1.9 %collective-permute-start.5 = (bf16[1024,128]{1,0:T(8,128)(2,1)S(1)}, bf16[1024,128]{1,0:T(8,128)(2,1)S(1)}, u32[]{:S(2)}, u32[]{:S(2)}) collective-permute-start(bf16[1024,128]{1,0:T(8,128)(2,1)S(1)} %merge.2), channel_id=1, source_target_pairs={{8,0},{12,4},{16,8},{20,12},{24,16},{28,20},{32,24},{36,28},{40,32... | collective-permute-start | bytes 786440 | tf_op jit(solution)/shard_map/ppermute | solution.py:408
  46.6 3.2 %own.1 = (bf16[512,256]{1,0:T(8,128)(2,1)}, bf16[1024,128]{1,0:T(8,128)(2,1)S(1)}, bf16[512,256]{1,0:T(8,128)(2,1)}) custom-call(bf16[512,256]{1,0:T(8,128)(2,1)S(1)} %copy-done.1, bf16[512,256]{1,0:T(8,128)(2,1)S(1)} %copy-done.3, bf16[2,128,512]{2,1,0:T(8,128)(2,1)S(1)} %get-tuple-element.30.qt_ref, bf16[2,128,512]{2,1,0:T(8,128)(2,1)S(1)} %get-tuple-element.31.dot_ref, ...), custom_call_target="tpu_custom_call" | custom-call | flops 2500000000 | bytes 2097152 | tf_op jit(solution)/shard_map/own/pallas_call | solution.py:305
  49.8 3.5 %collective-permute-done.5.b_ref = bf16[1024,128]{1,0:T(8,128)(2,1)S(1)} collective-permute-done((bf16[1024,128]{1,0:T(8,128)(2,1)S(1)}, bf16[1024,128]{1,0:T(8,128)(2,1)S(1)}, u32[]{:S(2)}, u32[]{:S(2)}) %collective-permute-start.5) | collective-permute-done | bytes 262176 | tf_op jit(solution)/shard_map/ppermute | solution.py:408
  53.3 0.1 merge.3
  53.4 11.7 %all_to_all.10 = bf16[4,256,128]{2,1,0:T(8,128)(2,1)S(1)} all-to-all(bf16[4,256,128]{2,1,0:T(8,128)(2,1)S(1)} %bitcast.5), channel_id=1, replica_groups=mesh['ctx'=128,'head'=4] {'head'}, dimensions={0} | all-to-all | bytes 524288 | tf_op jit(solution)/shard_map/all_to_all | solution.py:401
  65.2 10.0 %all_to_all.11 = bf16[4,256,128]{2,1,0:T(8,128)(2,1)S(1)} all-to-all(bf16[4,256,128]{2,1,0:T(8,128)(2,1)S(1)} %broadcast_in_dim.2), channel_id=1, replica_groups=mesh['ctx'=128,'head'=4] {'head'}, dimensions={0} | all-to-all | bytes 524288 | tf_op jit(solution)/shard_map/all_to_all | solution.py:404
  75.2 0.7 fusion
  (2 shorter events, 0.1 us)
Async XLA Ops:
  9.7 13.5 %collective-permute-start = (bf16[1024,128]{1,0:T(8,128)(2,1)}, bf16[1024,128]{1,0:T(8,128)(2,1)S(1)}, u32[]{:S(2)}, u32[]{:S(2)}) collective-permute-start(bf16[1024,128]{1,0:T(8,128)(2,1)} %pack.1.own_ref), channel_id=1, source_target_pairs={{0,8},{4,12},{8,16},{12,20},{16,24},{20,28},{24,32},{28,36},{32,40... | collective-permute-start | bytes 786440 | tf_op jit(solution)/shard_map/ppermute | solution.py:408
  13.1 1.0 %copy-start = (bf16[512,256]{1,0:T(8,128)(2,1)S(1)}, bf16[512,256]{1,0:T(8,128)(2,1)}, u32[]{:S(2)}) copy-start(bf16[512,256]{1,0:T(8,128)(2,1)} %q_ref.7) | copy-start | bytes 786436
  14.1 0.9 %copy-start.2 = (bf16[512,256]{1,0:T(8,128)(2,1)S(1)}, bf16[512,256]{1,0:T(8,128)(2,1)}, u32[]{:S(2)}) copy-start(bf16[512,256]{1,0:T(8,128)(2,1)} %do_ref.7) | copy-start | bytes 786436
  15.0 0.7 copy-start.4
  15.7 9.4 %copy-start.1 = (bf16[512,256]{1,0:T(8,128)(2,1)S(1)}, bf16[512,256]{1,0:T(8,128)(2,1)}, u32[]{:S(2)}) copy-start(bf16[512,256]{1,0:T(8,128)(2,1)} %q_ref.7) | copy-start | bytes 786436
  17.9 11.5 %collective-permute-start.1 = (bf16[1024,128]{1,0:T(8,128)(2,1)}, bf16[1024,128]{1,0:T(8,128)(2,1)S(1)}, u32[]{:S(2)}, u32[]{:S(2)}) collective-permute-start(bf16[1024,128]{1,0:T(8,128)(2,1)} %pack.1.own_ref), channel_id=1, source_target_pairs={{0,4},{4,16},{8,12},{12,24},{16,20},{20,32},{24,28},{28,40},{32,36... | collective-permute-start | bytes 786440 | tf_op jit(solution)/shard_map/ppermute | solution.py:408
  23.2 6.2 %collective-permute-start.2 = (bf16[1024,128]{1,0:T(8,128)(2,1)S(1)}, bf16[1024,128]{1,0:T(8,128)(2,1)S(1)}, u32[]{:S(2)}, u32[]{:S(2)}) collective-permute-start(bf16[1024,128]{1,0:T(8,128)(2,1)S(1)} %collective-permute-done.block_ref), channel_id=1, source_target_pairs={{0,4},{4,0},{8,12},{12,8},{16,20},{20,16},{24,28},{28,24},{32,36},... | collective-permute-start | bytes 786440 | tf_op jit(solution)/shard_map/ppermute | solution.py:408
  25.1 4.3 %copy-start.3 = (bf16[512,256]{1,0:T(8,128)(2,1)S(1)}, bf16[512,256]{1,0:T(8,128)(2,1)}, u32[]{:S(2)}) copy-start(bf16[512,256]{1,0:T(8,128)(2,1)} %do_ref.7) | copy-start | bytes 786436
  33.0 9.5 %collective-permute-start.3 = (bf16[1024,128]{1,0:T(8,128)(2,1)S(1)}, bf16[1024,128]{1,0:T(8,128)(2,1)S(1)}, u32[]{:S(2)}, u32[]{:S(2)}) collective-permute-start(bf16[1024,128]{1,0:T(8,128)(2,1)S(1)} %get-tuple-element.54), channel_id=1, source_target_pairs={{0,4},{4,0},{8,12},{12,8},{16,20},{20,16},{24,28},{28,24},{32,36},... | collective-permute-start | bytes 786440 | tf_op jit(solution)/shard_map/ppermute | solution.py:408
  34.9 9.7 %collective-permute-start.4 = (bf16[1024,128]{1,0:T(8,128)(2,1)S(1)}, bf16[1024,128]{1,0:T(8,128)(2,1)S(1)}, u32[]{:S(2)}, u32[]{:S(2)}) collective-permute-start(bf16[1024,128]{1,0:T(8,128)(2,1)S(1)} %get-tuple-element.55), channel_id=1, source_target_pairs={{4,0},{8,4},{12,8},{16,12},{20,16},{24,20},{28,24},{32,28},{36,32}... | collective-permute-start | bytes 786440 | tf_op jit(solution)/shard_map/ppermute | solution.py:408
  44.7 8.6 %collective-permute-start.5 = (bf16[1024,128]{1,0:T(8,128)(2,1)S(1)}, bf16[1024,128]{1,0:T(8,128)(2,1)S(1)}, u32[]{:S(2)}, u32[]{:S(2)}) collective-permute-start(bf16[1024,128]{1,0:T(8,128)(2,1)S(1)} %merge.2), channel_id=1, source_target_pairs={{8,0},{12,4},{16,8},{20,12},{24,16},{28,20},{32,24},{36,28},{40,32... | collective-permute-start | bytes 786440 | tf_op jit(solution)/shard_map/ppermute | solution.py:408

commit v6 on v5

--- a/solution.py
+++ b/solution.py
@@ -389,8 +389,9 @@
         pack_kernel,
         out_shape=jax.ShapeDtypeStruct((2 * rows, head), BF),
         in_specs=[pl.BlockSpec(memory_space=pl.ANY)] * 2,
-        out_specs=pl.BlockSpec(memory_space=pl.ANY),
+        out_specs=VMEM,
         scratch_shapes=[pltpu.SemaphoreType.DMA((2,))],
+        compiler_params=pltpu.CompilerParams(vmem_limit_bytes=2 << 20),
         name="pack",
     )(keys, values)
 

time: 76.4 us -> 68.2 us (0.89)
  Pallas kernels: 21.8 us -> 9.09 us
  waiting for transfers between devices: 11.4 us -> 14.2 us
  local copies, waits for them, and re-layouts: 3.31 us -> 5.11 us
    pallas_call x1, Pallas kernels: 9.06 us -> 0.32 us  [packed(): pl.pallas_call(pack_kernel, out_shape=jax.ShapeDtypeStruct((2 * rows, hea...]
    pallas_call x7, Pallas kernels: 12.8 us -> 8.76 us  [on_core(): pl.pallas_call(kernel, out_shape=tuple(outs), in_specs=[SMEM if x.ndim ==...]
    ppermute x6, waiting for transfers between devices: 11.4 us -> 14.2 us  [moved(): return lax.ppermute(value, 'ctx', pairs)]
    unnamed x10 -> x14, local copies, waits for them, and re-layouts: 2.56 us -> 4.36 us
  transfers between devices with their start and end apart: 6 -> 6, of which waited for: 4 -> 4; matrix products, arithmetic and copies ran while one was open for 0% -> 0% of each run, Pallas kernels for 12% -> 7%
where the time goes in v6:
time: 68.2 us; the launch traced here: 67.8 us
  blocking collectives  21.7 us (32%)
  starting transfers between devices  16.9 us (25%)
  waiting for transfers between devices  14.2 us (21%)
  Pallas kernels  9.09 us (13%)
  local copies, waits for them, and re-layouts  5.11 us (7%)
  between operations  0.8 us (1%)
    ppermute x6, starting transfers between devices, moved(): return lax.ppermute(value, 'ctx', pairs)  16.9 us
    ppermute x6, waiting for transfers between devices, moved(): return lax.ppermute(value, 'ctx', pairs)  14.2 us
    all_to_all x1, blocking collectives, head_sum(): theirs = lax.all_to_all(pieces, 'head', split_axis=0, concat_axis=0)  11.7 us
    all_to_all x1, blocking collectives, head_sum(): lax.all_to_all(mine, 'head', split_axis=0, concat_axis=0)  9.96 us
    pallas_call x7, Pallas kernels, on_core(): pl.pallas_call(kernel, out_shape=tuple(outs), in_specs=[SMEM if x.ndim ==...  8.76 us
    unnamed x14, local copies, waits for them, and re-layouts  4.36 us
  transfers between devices with their start and end apart: 6, of which 4 were waited for; matrix products, arithmetic and copies ran while one was open for 0% of the time, Pallas kernels for 7%

profile of v6, /device:TPU:384, one launch (start us, length us, event | category | flops | bytes accessed | tf_op | source)
XLA Modules:
  0.0 67.8 jit_solution(4029265249999867048)
XLA Ops:
  0.6 0.0 copy-start
  0.6 0.9 %copy-done = bf16[512,128]{1,0:T(8,128)(2,1)S(1)} copy-done((bf16[512,128]{1,0:T(8,128)(2,1)S(1)}, bf16[512,128]{1,0:T(8,128)(2,1)}, u32[]{:S(2)}) %copy-start) | copy-done | bytes 131096
  1.5 0.0 copy-start.1
  1.5 0.9 %copy-done.1 = bf16[512,128]{1,0:T(8,128)(2,1)S(1)} copy-done((bf16[512,128]{1,0:T(8,128)(2,1)S(1)}, bf16[512,128]{1,0:T(8,128)(2,1)}, u32[]{:S(2)}) %copy-start.1) | copy-done | bytes 131096
  2.4 0.3 pack.1.own_ref
  2.8 3.4 %collective-permute-start = (bf16[1024,128]{1,0:T(8,128)(2,1)S(1)}, bf16[1024,128]{1,0:T(8,128)(2,1)S(1)}, u32[]{:S(2)}, u32[]{:S(2)}) collective-permute-start(bf16[1024,128]{1,0:T(8,128)(2,1)S(1)} %pack.1.own_ref), channel_id=1, source_target_pairs={{0,8},{4,12},{8,16},{12,20},{16,24},{20,28},{24,32},{28,36},{32,40... | collective-permute-start | bytes 786440 | tf_op jit(solution)/shard_map/ppermute | solution.py:409
  6.2 0.0 copy-start.2
  6.2 0.9 %copy-done.2 = bf16[512,256]{1,0:T(8,128)(2,1)S(1)} copy-done((bf16[512,256]{1,0:T(8,128)(2,1)S(1)}, bf16[512,256]{1,0:T(8,128)(2,1)}, u32[]{:S(2)}) %copy-start.2) | copy-done | bytes 262168
  7.1 0.0 copy-start.4
  7.1 0.9 %copy-done.4 = bf16[512,256]{1,0:T(8,128)(2,1)S(1)} copy-done((bf16[512,256]{1,0:T(8,128)(2,1)S(1)}, bf16[512,256]{1,0:T(8,128)(2,1)}, u32[]{:S(2)}) %copy-start.4) | copy-done | bytes 262168
  8.1 0.0 copy-start.6
  8.1 0.7 copy-done.6
  8.7 1.2 %diagonal.1 = (s32[1]{0:T(128)}, s32[512,128]{1,0:T(8,128)S(1)}, f32[2,512,128]{2,1,0:T(8,128)S(1)}, f32[2,512,128]{2,1,0:T(8,128)S(1)}, f32[2,512,128]{2,1,0:T(...) custom-call(s32[1]{0:T(128)} %bitcast.place_ref, s32[1,128]{1,0:T(1,128)S(1)} %bitcast.6, ...), custom_call_target="tpu_custom_call" | custom-call | flops 1200000000 | bytes 2097152 | tf_op jit(solution)/shard_map/diagonal/pallas_call | solution.py:305
  9.9 1.9 %collective-permute-start.1 = (bf16[1024,128]{1,0:T(8,128)(2,1)S(1)}, bf16[1024,128]{1,0:T(8,128)(2,1)S(1)}, u32[]{:S(2)}, u32[]{:S(2)}) collective-permute-start(bf16[1024,128]{1,0:T(8,128)(2,1)S(1)} %pack.1.own_ref), channel_id=1, source_target_pairs={{0,4},{4,16},{8,12},{12,24},{16,20},{20,32},{24,28},{28,40},{32,36... | collective-permute-start | bytes 786440 | tf_op jit(solution)/shard_map/ppermute | solution.py:409
  11.9 4.2 %collective-permute-done.block_ref = bf16[1024,128]{1,0:T(8,128)(2,1)S(1)} collective-permute-done((bf16[1024,128]{1,0:T(8,128)(2,1)S(1)}, bf16[1024,128]{1,0:T(8,128)(2,1)S(1)}, u32[]{:S(2)}, u32[]{:S(2)}) %collective-permute-start) | collective-permute-done | bytes 262176 | tf_op jit(solution)/shard_map/ppermute | solution.py:409
  16.0 1.9 %collective-permute-start.2 = (bf16[1024,128]{1,0:T(8,128)(2,1)S(1)}, bf16[1024,128]{1,0:T(8,128)(2,1)S(1)}, u32[]{:S(2)}, u32[]{:S(2)}) collective-permute-start(bf16[1024,128]{1,0:T(8,128)(2,1)S(1)} %collective-permute-done.block_ref), channel_id=1, source_target_pairs={{0,4},{4,0},{8,12},{12,8},{16,20},{20,16},{24,28},{28,24},{32,36},... | collective-permute-start | bytes 786440 | tf_op jit(solution)/shard_map/ppermute | solution.py:409
  17.9 0.0 copy-start.3
  18.0 0.0 copy-start.5
  18.0 0.8 %second.1 = (f32[2,512,128]{2,1,0:T(8,128)S(1)}, f32[2,512,128]{2,1,0:T(8,128)S(1)}, f32[2,512,128]{2,1,0:T(8,128)S(1)}, f32[2,512,512]{2,1,0:T(8,128)S(1)}) custom-call(s32[1]{0:T(128)} %get-tuple-element.34.first_ref, bf16[512,256]{1,0:T(8,128)(2,1)S(1)} %copy-done.2, s32[512,128]{1,0:T(8,128)S(1)} %get-tuple-element.32.starts_ref, ...), custom_call_target="tpu_custom_call" | custom-call | flops 1200000000 | bytes 2097152 | tf_op jit(solution)/shard_map/second/pallas_call | solution.py:305
  18.8 2.4 %collective-permute-done.1.mixed_ref = bf16[1024,128]{1,0:T(8,128)(2,1)S(1)} collective-permute-done((bf16[1024,128]{1,0:T(8,128)(2,1)S(1)}, bf16[1024,128]{1,0:T(8,128)(2,1)S(1)}, u32[]{:S(2)}, u32[]{:S(2)}) %collective-permute-start.1) | collective-permute-done | bytes 262176 | tf_op jit(solution)/shard_map/ppermute | solution.py:409
  21.2 0.0 collective-permute-done.2.swapped_ref
  21.2 0.0 copy-done.3
  21.2 0.0 copy-done.5
  21.3 3.6 %far.1 = (bf16[512,256]{1,0:T(8,128)(2,1)S(1)}, f32[2,512,128]{2,1,0:T(8,128)S(1)}, f32[2,512,128]{2,1,0:T(8,128)S(1)}, f32[2,512,128]{2,1,0:T(8,128)S(1)}, f32[...) custom-call(s32[1]{0:T(128)} %bitcast.place_ref, ...), custom_call_target="tpu_custom_call" | custom-call | flops 3000000000 | bytes 2097152 | tf_op jit(solution)/shard_map/far/pallas_call | solution.py:305
  24.8 1.9 %collective-permute-start.3 = (bf16[1024,128]{1,0:T(8,128)(2,1)S(1)}, bf16[1024,128]{1,0:T(8,128)(2,1)S(1)}, u32[]{:S(2)}, u32[]{:S(2)}) collective-permute-start(bf16[1024,128]{1,0:T(8,128)(2,1)S(1)} %get-tuple-element.54), channel_id=1, source_target_pairs={{0,4},{4,0},{8,12},{12,8},{16,20},{20,16},{24,28},{28,24},{32,36},... | collective-permute-start | bytes 786440 | tf_op jit(solution)/shard_map/ppermute | solution.py:409
  26.8 5.8 %collective-permute-start.4 = (bf16[1024,128]{1,0:T(8,128)(2,1)S(1)}, bf16[1024,128]{1,0:T(8,128)(2,1)S(1)}, u32[]{:S(2)}, u32[]{:S(2)}) collective-permute-start(bf16[1024,128]{1,0:T(8,128)(2,1)S(1)} %get-tuple-element.55), channel_id=1, source_target_pairs={{4,0},{8,4},{12,8},{16,12},{20,16},{24,20},{28,24},{32,28},{36,32}... | collective-permute-start | bytes 786440 | tf_op jit(solution)/shard_map/ppermute | solution.py:409
  32.6 0.7 %second_back.1 = (f32[2,512,128]{2,1,0:T(8,128)S(1)}, bf16[1024,128]{1,0:T(8,128)(2,1)S(1)}) custom-call(s32[1]{0:T(128)} %get-tuple-element.34.first_ref, bf16[512,256]{1,0:T(8,128)(2,1)S(1)} %copy-done.5, bf16[2,128,512]{2,1,0:T(8,128)(2,1)S(1)} %get-tuple-element.30.qt_ref, bf16[2,128,512]{2,1,0:T(8,128)(2,1)S(1)} %get-tuple-element.31.dot_ref, ...), custom_call_target="tpu_custom_call" | custom-call | flops 1500000000 | bytes 2097152 | tf_op jit(solution)/shard_map/second_back/pallas_call | solution.py:305
  33.3 0.0 collective-permute-done.3.b_ref
  33.3 3.1 %collective-permute-done.4.c_ref = bf16[1024,128]{1,0:T(8,128)(2,1)S(1)} collective-permute-done((bf16[1024,128]{1,0:T(8,128)(2,1)S(1)}, bf16[1024,128]{1,0:T(8,128)(2,1)S(1)}, u32[]{:S(2)}, u32[]{:S(2)}) %collective-permute-start.4) | collective-permute-done | bytes 262176 | tf_op jit(solution)/shard_map/ppermute | solution.py:409
  36.4 0.1 merge.2
  36.6 1.9 %collective-permute-start.5 = (bf16[1024,128]{1,0:T(8,128)(2,1)S(1)}, bf16[1024,128]{1,0:T(8,128)(2,1)S(1)}, u32[]{:S(2)}, u32[]{:S(2)}) collective-permute-start(bf16[1024,128]{1,0:T(8,128)(2,1)S(1)} %merge.2), channel_id=1, source_target_pairs={{8,0},{12,4},{16,8},{20,12},{24,16},{28,20},{32,24},{36,28},{40,32... | collective-permute-start | bytes 786440 | tf_op jit(solution)/shard_map/ppermute | solution.py:409
  38.5 2.2 %own.1 = (bf16[512,256]{1,0:T(8,128)(2,1)}, bf16[1024,128]{1,0:T(8,128)(2,1)S(1)}, bf16[512,256]{1,0:T(8,128)(2,1)}) custom-call(bf16[512,256]{1,0:T(8,128)(2,1)S(1)} %copy-done.3, bf16[512,256]{1,0:T(8,128)(2,1)S(1)} %copy-done.5, bf16[2,128,512]{2,1,0:T(8,128)(2,1)S(1)} %get-tuple-element.30.qt_ref, bf16[2,128,512]{2,1,0:T(8,128)(2,1)S(1)} %get-tuple-element.31.dot_ref, ...), custom_call_target="tpu_custom_call" | custom-call | flops 2500000000 | bytes 2097152 | tf_op jit(solution)/shard_map/own/pallas_call | solution.py:305
  40.7 4.4 %collective-permute-done.5.b_ref = bf16[1024,128]{1,0:T(8,128)(2,1)S(1)} collective-permute-done((bf16[1024,128]{1,0:T(8,128)(2,1)S(1)}, bf16[1024,128]{1,0:T(8,128)(2,1)S(1)}, u32[]{:S(2)}, u32[]{:S(2)}) %collective-permute-start.5) | collective-permute-done | bytes 262176 | tf_op jit(solution)/shard_map/ppermute | solution.py:409
  45.2 0.1 merge.3
  45.3 11.7 %all_to_all.10 = bf16[4,256,128]{2,1,0:T(8,128)(2,1)S(1)} all-to-all(bf16[4,256,128]{2,1,0:T(8,128)(2,1)S(1)} %bitcast.5), channel_id=1, replica_groups=mesh['ctx'=128,'head'=4] {'head'}, dimensions={0} | all-to-all | bytes 524288 | tf_op jit(solution)/shard_map/all_to_all | solution.py:402
  57.1 10.0 %all_to_all.11 = bf16[4,256,128]{2,1,0:T(8,128)(2,1)S(1)} all-to-all(bf16[4,256,128]{2,1,0:T(8,128)(2,1)S(1)} %broadcast_in_dim.2), channel_id=1, replica_groups=mesh['ctx'=128,'head'=4] {'head'}, dimensions={0} | all-to-all | bytes 524288 | tf_op jit(solution)/shard_map/all_to_all | solution.py:405
  67.1 0.7 %fusion = (bf16[2,256,128]{2,1,0:T(8,128)(2,1)}, bf16[2,256,128]{2,1,0:T(8,128)(2,1)}) fusion(bf16[4,256,128]{2,1,0:T(8,128)(2,1)S(1)} %all_to_all.11), kind=kLoop, calls=%fused_computation | loop fusion | bytes 524288 | tf_op jit(solution)/shard_map/slice | solution.py:444
  (2 shorter events, 0.1 us)
Async XLA Ops:
  0.6 0.9 %copy-start = (bf16[512,128]{1,0:T(8,128)(2,1)S(1)}, bf16[512,128]{1,0:T(8,128)(2,1)}, u32[]{:S(2)}) copy-start(bf16[512,128]{1,0:T(8,128)(2,1)} %key_ref.1) | copy-start | bytes 393220
  1.5 0.9 %copy-start.1 = (bf16[512,128]{1,0:T(8,128)(2,1)S(1)}, bf16[512,128]{1,0:T(8,128)(2,1)}, u32[]{:S(2)}) copy-start(bf16[512,128]{1,0:T(8,128)(2,1)} %value_ref.1) | copy-start | bytes 393220
  2.8 13.3 %collective-permute-start = (bf16[1024,128]{1,0:T(8,128)(2,1)S(1)}, bf16[1024,128]{1,0:T(8,128)(2,1)S(1)}, u32[]{:S(2)}, u32[]{:S(2)}) collective-permute-start(bf16[1024,128]{1,0:T(8,128)(2,1)S(1)} %pack.1.own_ref), channel_id=1, source_target_pairs={{0,8},{4,12},{8,16},{12,20},{16,24},{20,28},{24,32},{28,36},{32,40... | collective-permute-start | bytes 786440 | tf_op jit(solution)/shard_map/ppermute | solution.py:409
  6.2 1.0 %copy-start.2 = (bf16[512,256]{1,0:T(8,128)(2,1)S(1)}, bf16[512,256]{1,0:T(8,128)(2,1)}, u32[]{:S(2)}) copy-start(bf16[512,256]{1,0:T(8,128)(2,1)} %q_ref.7) | copy-start | bytes 786436
  7.1 0.9 %copy-start.4 = (bf16[512,256]{1,0:T(8,128)(2,1)S(1)}, bf16[512,256]{1,0:T(8,128)(2,1)}, u32[]{:S(2)}) copy-start(bf16[512,256]{1,0:T(8,128)(2,1)} %do_ref.7) | copy-start | bytes 786436
  8.1 0.7 copy-start.6
  9.9 11.3 %collective-permute-start.1 = (bf16[1024,128]{1,0:T(8,128)(2,1)S(1)}, bf16[1024,128]{1,0:T(8,128)(2,1)S(1)}, u32[]{:S(2)}, u32[]{:S(2)}) collective-permute-start(bf16[1024,128]{1,0:T(8,128)(2,1)S(1)} %pack.1.own_ref), channel_id=1, source_target_pairs={{0,4},{4,16},{8,12},{12,24},{16,20},{20,32},{24,28},{28,40},{32,36... | collective-permute-start | bytes 786440 | tf_op jit(solution)/shard_map/ppermute | solution.py:409
  16.0 5.2 %collective-permute-start.2 = (bf16[1024,128]{1,0:T(8,128)(2,1)S(1)}, bf16[1024,128]{1,0:T(8,128)(2,1)S(1)}, u32[]{:S(2)}, u32[]{:S(2)}) collective-permute-start(bf16[1024,128]{1,0:T(8,128)(2,1)S(1)} %collective-permute-done.block_ref), channel_id=1, source_target_pairs={{0,4},{4,0},{8,12},{12,8},{16,20},{20,16},{24,28},{28,24},{32,36},... | collective-permute-start | bytes 786440 | tf_op jit(solution)/shard_map/ppermute | solution.py:409
  17.9 3.3 %copy-start.3 = (bf16[512,256]{1,0:T(8,128)(2,1)S(1)}, bf16[512,256]{1,0:T(8,128)(2,1)}, u32[]{:S(2)}) copy-start(bf16[512,256]{1,0:T(8,128)(2,1)} %q_ref.7) | copy-start | bytes 786436
  18.0 3.3 %copy-start.5 = (bf16[512,256]{1,0:T(8,128)(2,1)S(1)}, bf16[512,256]{1,0:T(8,128)(2,1)}, u32[]{:S(2)}) copy-start(bf16[512,256]{1,0:T(8,128)(2,1)} %do_ref.7) | copy-start | bytes 786436
  24.8 8.5 %collective-permute-start.3 = (bf16[1024,128]{1,0:T(8,128)(2,1)S(1)}, bf16[1024,128]{1,0:T(8,128)(2,1)S(1)}, u32[]{:S(2)}, u32[]{:S(2)}) collective-permute-start(bf16[1024,128]{1,0:T(8,128)(2,1)S(1)} %get-tuple-element.54), channel_id=1, source_target_pairs={{0,4},{4,0},{8,12},{12,8},{16,20},{20,16},{24,28},{28,24},{32,36},... | collective-permute-start | bytes 786440 | tf_op jit(solution)/shard_map/ppermute | solution.py:409
  26.8 9.7 %collective-permute-start.4 = (bf16[1024,128]{1,0:T(8,128)(2,1)S(1)}, bf16[1024,128]{1,0:T(8,128)(2,1)S(1)}, u32[]{:S(2)}, u32[]{:S(2)}) collective-permute-start(bf16[1024,128]{1,0:T(8,128)(2,1)S(1)} %get-tuple-element.55), channel_id=1, source_target_pairs={{4,0},{8,4},{12,8},{16,12},{20,16},{24,20},{28,24},{32,28},{36,32}... | collective-permute-start | bytes 786440 | tf_op jit(solution)/shard_map/ppermute | solution.py:409
  36.6 8.6 %collective-permute-start.5 = (bf16[1024,128]{1,0:T(8,128)(2,1)S(1)}, bf16[1024,128]{1,0:T(8,128)(2,1)S(1)}, u32[]{:S(2)}, u32[]{:S(2)}) collective-permute-start(bf16[1024,128]{1,0:T(8,128)(2,1)S(1)} %merge.2), channel_id=1, source_target_pairs={{8,0},{12,4},{16,8},{20,12},{24,16},{28,20},{32,24},{36,28},{40,32... | collective-permute-start | bytes 786440 | tf_op jit(solution)/shard_map/ppermute | solution.py:409

commit v7 on v6

--- a/solution.py
+++ b/solution.py
@@ -279,10 +279,9 @@
     part_ref[pl.ds(rows, rows), :] = dv.T.astype(BF)
 
 
-def merge_kernel(weight_ref, a_ref, b_ref, c_ref, out_ref):
-    weight = weight_ref[0].astype(F32)
-    out = a_ref[...].astype(F32) + b_ref[...].astype(F32) + weight * c_ref[...].astype(F32)
-    out_ref[...] = out.astype(BF)
+def sum_kernel(*refs):
+    *terms, out_ref = refs
+    out_ref[...] = sum(x[...].astype(F32) for x in terms).astype(BF)
 
 
 def score_scale(head):
@@ -367,8 +366,8 @@
     return on_core(own_kernel, "own", 2500, 20, [like_q, part, like_q], ins)
 
 
-def merged(weight, a, b, c):
-    return on_core(merge_kernel, "merge", 1, 6, [shape(a.shape, BF)], (weight, a, b, c))[0]
+def summed(*terms):
+    return on_core(sum_kernel, "sum", 1, 6, [shape(terms[0].shape, BF)], terms)[0]
 
 
 def pack_kernel(key_ref, value_ref, both_ref, sems):
@@ -388,7 +387,7 @@
     return pl.pallas_call(
         pack_kernel,
         out_shape=jax.ShapeDtypeStruct((2 * rows, head), BF),
-        in_specs=[pl.BlockSpec(memory_space=pl.ANY)] * 2,
+        in_specs=[pl.BlockSpec(memory_space=pltpu.HBM)] * 2,
         out_specs=VMEM,
         scratch_shapes=[pltpu.SemaphoreType.DMA((2,))],
         compiler_params=pltpu.CompilerParams(vmem_limit_bytes=2 << 20),
@@ -417,31 +416,31 @@
     mixed_on = [(i, i + (3 if i % 2 else 1)) for i in range(count) if i + (3 if i % 2 else 1) < count]
     across = [(i, i ^ 1) for i in range(count)]
 
+    def back(pairs):
+        return [(there, here) for here, there in pairs]
+
     lengths = doc_lengths.reshape(1, -1)
     own = packed(keys, values)
     two = moved(own, two_on)
+    mixed = moved(own, mixed_on)
     first, starts, top, total, out, qt, dot_ = attention_before(place, lengths, queries, d_out, own)
-    own_later, first = lax.optimization_barrier((own, first))
-    mixed = moved(own_later, mixed_on)
+    two, first = lax.optimization_barrier((two, first))
     swapped = moved(two, across)
     top, total, out, tile = attention_second(first, queries, starts, top, total, out, two)
     attended, top, inverse, row_dot, factor, dq, mixed_part, swapped_part = attention_far(
         place, first, queries, d_out, qt, dot_, starts, top, total, out, mixed, swapped
     )
-    from_next = moved(mixed_part, [(i + 1, i) for i in range(count - 1)])
+    from_mixed = moved(mixed_part, back(mixed_on))
     from_core = moved(swapped_part, across)
     dq, two_part = attention_second_back(
         first, queries, d_out, qt, dot_, two, tile, factor, row_dot, dq
     )
-    odd = place & 1
-    passed = merged(odd, two_part, from_core, from_next)
-    from_two = moved(passed, [(there, here) for here, there in two_on])
+    from_two = moved(summed(two_part, from_core), back(two_on))
     d_queries, own_part, attended = attention_own(
         queries, d_out, qt, dot_, own, starts, top, inverse, row_dot, dq, attended
     )
-    mine = merged(1 - odd, own_part, from_two, from_next)
-    summed = head_sum(mine)
-    return (attended, d_queries, summed[:rows], summed[rows:])
+    both = head_sum(summed(own_part, from_two, from_mixed))
+    return (attended, d_queries, both[:rows], both[rows:])
 
 
 def solution(mesh):

time: 68.2 us -> 66.1 us (0.969)
  the two profiles are of different devices: /device:TPU:384 before, /device:TPU:358 now
where the time goes in v7:
time: 66.1 us; the launch traced here: 65.6 us
  blocking collectives  20 us (30%)
  waiting for transfers between devices  14 us (21%)
  Pallas kernels  13.3 us (20%)
  starting transfers between devices  12.4 us (19%)
  local copies, waits for them, and re-layouts  5.11 us (8%)
  between operations  0.82 us (1%)
    ppermute x6, waiting for transfers between devices, moved(): return lax.ppermute(value, 'ctx', pairs)  14 us
    pallas_call x7, Pallas kernels, on_core(): pl.pallas_call(kernel, out_shape=tuple(outs), in_specs=[SMEM if x.ndim ==...  12.9 us
    ppermute x6, starting transfers between devices, moved(): return lax.ppermute(value, 'ctx', pairs)  12.4 us
    all_to_all x1, blocking collectives, head_sum(): theirs = lax.all_to_all(pieces, 'head', split_axis=0, concat_axis=0)  10.9 us
    all_to_all x1, blocking collectives, head_sum(): lax.all_to_all(mine, 'head', split_axis=0, concat_axis=0)  9.07 us
    unnamed x14, local copies, waits for them, and re-layouts  4.36 us
  transfers between devices with their start and end apart: 6, of which 2 were waited for; matrix products, arithmetic and copies ran while one was open for 0% of the time, Pallas kernels for 11%

profile of v7, /device:TPU:358, one launch (start us, length us, event | category | flops | bytes accessed | tf_op | source)
XLA Modules:
  0.0 65.6 jit_solution(14632935760397042861)
XLA Ops:
  0.6 0.0 copy-start
  0.6 0.9 %copy-done = bf16[512,128]{1,0:T(8,128)(2,1)S(1)} copy-done((bf16[512,128]{1,0:T(8,128)(2,1)S(1)}, bf16[512,128]{1,0:T(8,128)(2,1)}, u32[]{:S(2)}) %copy-start) | copy-done | bytes 131096
  1.5 0.0 copy-start.1
  1.5 0.9 %copy-done.1 = bf16[512,128]{1,0:T(8,128)(2,1)S(1)} copy-done((bf16[512,128]{1,0:T(8,128)(2,1)S(1)}, bf16[512,128]{1,0:T(8,128)(2,1)}, u32[]{:S(2)}) %copy-start.1) | copy-done | bytes 131096
  2.4 0.3 pack.1.own_ref
  2.8 2.8 %collective-permute-start = (bf16[1024,128]{1,0:T(8,128)(2,1)S(1)}, bf16[1024,128]{1,0:T(8,128)(2,1)S(1)}, u32[]{:S(2)}, u32[]{:S(2)}) collective-permute-start(bf16[1024,128]{1,0:T(8,128)(2,1)S(1)} %pack.1.own_ref), channel_id=1, source_target_pairs={{0,8},{4,12},{8,16},{12,20},{16,24},{20,28},{24,32},{28,36},{32,40... | collective-permute-start | bytes 786440 | tf_op jit(solution)/shard_map/ppermute | solution.py:408
  5.6 1.9 %collective-permute-start.1 = (bf16[1024,128]{1,0:T(8,128)(2,1)S(1)}, bf16[1024,128]{1,0:T(8,128)(2,1)S(1)}, u32[]{:S(2)}, u32[]{:S(2)}) collective-permute-start(bf16[1024,128]{1,0:T(8,128)(2,1)S(1)} %pack.1.own_ref), channel_id=1, source_target_pairs={{0,4},{4,16},{8,12},{12,24},{16,20},{20,32},{24,28},{28,40},{32,36... | collective-permute-start | bytes 786440 | tf_op jit(solution)/shard_map/ppermute | solution.py:408
  7.6 0.0 copy-start.2
  7.6 0.9 %copy-done.2 = bf16[512,256]{1,0:T(8,128)(2,1)S(1)} copy-done((bf16[512,256]{1,0:T(8,128)(2,1)S(1)}, bf16[512,256]{1,0:T(8,128)(2,1)}, u32[]{:S(2)}) %copy-start.2) | copy-done | bytes 262168
  8.5 0.0 copy-start.4
  8.5 0.9 %copy-done.4 = bf16[512,256]{1,0:T(8,128)(2,1)S(1)} copy-done((bf16[512,256]{1,0:T(8,128)(2,1)S(1)}, bf16[512,256]{1,0:T(8,128)(2,1)}, u32[]{:S(2)}) %copy-start.4) | copy-done | bytes 262168
  9.5 0.0 copy-start.6
  9.5 0.7 copy-done.6
  10.1 1.2 %diagonal.1 = (s32[1]{0:T(128)}, s32[512,128]{1,0:T(8,128)S(1)}, f32[2,512,128]{2,1,0:T(8,128)S(1)}, f32[2,512,128]{2,1,0:T(8,128)S(1)}, f32[2,512,128]{2,1,0:T(...) custom-call(s32[1]{0:T(128)} %bitcast.place_ref, s32[1,128]{1,0:T(1,128)S(1)} %bitcast.6, ...), custom_call_target="tpu_custom_call" | custom-call | flops 1200000000 | bytes 2097152 | tf_op jit(solution)/shard_map/diagonal/pallas_call | solution.py:304
  11.3 4.2 %collective-permute-done.block_ref = bf16[1024,128]{1,0:T(8,128)(2,1)S(1)} collective-permute-done((bf16[1024,128]{1,0:T(8,128)(2,1)S(1)}, bf16[1024,128]{1,0:T(8,128)(2,1)S(1)}, u32[]{:S(2)}, u32[]{:S(2)}) %collective-permute-start) | collective-permute-done | bytes 262176 | tf_op jit(solution)/shard_map/ppermute | solution.py:408
  15.5 1.9 %collective-permute-start.2 = (bf16[1024,128]{1,0:T(8,128)(2,1)S(1)}, bf16[1024,128]{1,0:T(8,128)(2,1)S(1)}, u32[]{:S(2)}, u32[]{:S(2)}) collective-permute-start(bf16[1024,128]{1,0:T(8,128)(2,1)S(1)} %collective-permute-done.block_ref), channel_id=1, source_target_pairs={{0,4},{4,0},{8,12},{12,8},{16,20},{20,16},{24,28},{28,24},{32,36},... | collective-permute-start | bytes 786440 | tf_op jit(solution)/shard_map/ppermute | solution.py:408
  17.4 0.0 copy-start.3
  17.5 0.0 copy-start.5
  17.5 1.9 %second.1 = (f32[2,512,128]{2,1,0:T(8,128)S(1)}, f32[2,512,128]{2,1,0:T(8,128)S(1)}, f32[2,512,128]{2,1,0:T(8,128)S(1)}, f32[2,512,512]{2,1,0:T(8,128)S(1)}) custom-call(s32[1]{0:T(128)} %get-tuple-element.34.first_ref, bf16[512,256]{1,0:T(8,128)(2,1)S(1)} %copy-done.2, s32[512,128]{1,0:T(8,128)S(1)} %get-tuple-element.32.starts_ref, ...), custom_call_target="tpu_custom_call" | custom-call | flops 1200000000 | bytes 2097152 | tf_op jit(solution)/shard_map/second/pallas_call | solution.py:304
  19.4 0.0 collective-permute-done.1.mixed_ref
  19.4 0.0 collective-permute-done.2.swapped_ref
  19.4 0.0 copy-done.3
  19.4 0.0 copy-done.5
  19.4 5.7 %far.1 = (bf16[512,256]{1,0:T(8,128)(2,1)S(1)}, f32[2,512,128]{2,1,0:T(8,128)S(1)}, f32[2,512,128]{2,1,0:T(8,128)S(1)}, f32[2,512,128]{2,1,0:T(8,128)S(1)}, f32[...) custom-call(s32[1]{0:T(128)} %bitcast.place_ref, ...), custom_call_target="tpu_custom_call" | custom-call | flops 3000000000 | bytes 2097152 | tf_op jit(solution)/shard_map/far/pallas_call | solution.py:304
  25.1 1.9 %collective-permute-start.3 = (bf16[1024,128]{1,0:T(8,128)(2,1)S(1)}, bf16[1024,128]{1,0:T(8,128)(2,1)S(1)}, u32[]{:S(2)}, u32[]{:S(2)}) collective-permute-start(bf16[1024,128]{1,0:T(8,128)(2,1)S(1)} %get-tuple-element.54), channel_id=1, source_target_pairs={{0,4},{4,0},{8,12},{12,8},{16,20},{20,16},{24,28},{28,24},{32,36},... | collective-permute-start | bytes 786440 | tf_op jit(solution)/shard_map/ppermute | solution.py:408
  27.0 1.9 %collective-permute-start.5 = (bf16[1024,128]{1,0:T(8,128)(2,1)S(1)}, bf16[1024,128]{1,0:T(8,128)(2,1)S(1)}, u32[]{:S(2)}, u32[]{:S(2)}) collective-permute-start(bf16[1024,128]{1,0:T(8,128)(2,1)S(1)} %get-tuple-element.55), channel_id=1, source_target_pairs={{4,0},{16,4},{12,8},{24,12},{20,16},{32,20},{28,24},{40,28},{36,32... | collective-permute-start | bytes 786440 | tf_op jit(solution)/shard_map/ppermute | solution.py:408
  29.0 1.7 %second_back.1 = (f32[2,512,128]{2,1,0:T(8,128)S(1)}, bf16[1024,128]{1,0:T(8,128)(2,1)S(1)}) custom-call(s32[1]{0:T(128)} %get-tuple-element.34.first_ref, bf16[512,256]{1,0:T(8,128)(2,1)S(1)} %copy-done.5, bf16[2,128,512]{2,1,0:T(8,128)(2,1)S(1)} %get-tuple-element.30.qt_ref, bf16[2,128,512]{2,1,0:T(8,128)(2,1)S(1)} %get-tuple-element.31.dot_ref, ...), custom_call_target="tpu_custom_call" | custom-call | flops 1500000000 | bytes 2097152 | tf_op jit(solution)/shard_map/second_back/pallas_call | solution.py:304
  30.7 0.0 collective-permute-done.3.refs_1_
  30.7 0.1 sum.2
  30.8 1.9 %collective-permute-start.4 = (bf16[1024,128]{1,0:T(8,128)(2,1)S(1)}, bf16[1024,128]{1,0:T(8,128)(2,1)S(1)}, u32[]{:S(2)}, u32[]{:S(2)}) collective-permute-start(bf16[1024,128]{1,0:T(8,128)(2,1)S(1)} %sum.2), channel_id=1, source_target_pairs={{8,0},{12,4},{16,8},{20,12},{24,16},{28,20},{32,24},{36,28},{40,32... | collective-permute-start | bytes 786440 | tf_op jit(solution)/shard_map/ppermute | solution.py:408
  32.7 2.3 %own.1 = (bf16[512,256]{1,0:T(8,128)(2,1)}, bf16[1024,128]{1,0:T(8,128)(2,1)S(1)}, bf16[512,256]{1,0:T(8,128)(2,1)}) custom-call(bf16[512,256]{1,0:T(8,128)(2,1)S(1)} %copy-done.3, bf16[512,256]{1,0:T(8,128)(2,1)S(1)} %copy-done.5, bf16[2,128,512]{2,1,0:T(8,128)(2,1)S(1)} %get-tuple-element.30.qt_ref, bf16[2,128,512]{2,1,0:T(8,128)(2,1)S(1)} %get-tuple-element.31.dot_ref, ...), custom_call_target="tpu_custom_call" | custom-call | flops 2500000000 | bytes 2097152 | tf_op jit(solution)/shard_map/own/pallas_call | solution.py:304
  35.0 0.0 collective-permute-done.5.refs_2_
  35.0 9.7 %collective-permute-done.4.refs_1_ = bf16[1024,128]{1,0:T(8,128)(2,1)S(1)} collective-permute-done((bf16[1024,128]{1,0:T(8,128)(2,1)S(1)}, bf16[1024,128]{1,0:T(8,128)(2,1)S(1)}, u32[]{:S(2)}, u32[]{:S(2)}) %collective-permute-start.4) | collective-permute-done | bytes 262176 | tf_op jit(solution)/shard_map/ppermute | solution.py:408
  44.7 0.1 sum.3
  44.8 10.9 %all_to_all.10 = bf16[4,256,128]{2,1,0:T(8,128)(2,1)S(1)} all-to-all(bf16[4,256,128]{2,1,0:T(8,128)(2,1)S(1)} %bitcast.5), channel_id=1, replica_groups=mesh['ctx'=128,'head'=4] {'head'}, dimensions={0} | all-to-all | bytes 524288 | tf_op jit(solution)/shard_map/all_to_all | solution.py:401
  55.9 9.1 %all_to_all.11 = bf16[4,256,128]{2,1,0:T(8,128)(2,1)S(1)} all-to-all(bf16[4,256,128]{2,1,0:T(8,128)(2,1)S(1)} %broadcast_in_dim.2), channel_id=1, replica_groups=mesh['ctx'=128,'head'=4] {'head'}, dimensions={0} | all-to-all | bytes 524288 | tf_op jit(solution)/shard_map/all_to_all | solution.py:404
  64.9 0.7 %fusion = (bf16[2,256,128]{2,1,0:T(8,128)(2,1)}, bf16[2,256,128]{2,1,0:T(8,128)(2,1)}) fusion(bf16[4,256,128]{2,1,0:T(8,128)(2,1)S(1)} %all_to_all.11), kind=kLoop, calls=%fused_computation | loop fusion | bytes 524288 | tf_op jit(solution)/shard_map/slice | solution.py:443
  (2 shorter events, 0.1 us)
Async XLA Ops:
  0.6 0.9 %copy-start = (bf16[512,128]{1,0:T(8,128)(2,1)S(1)}, bf16[512,128]{1,0:T(8,128)(2,1)}, u32[]{:S(2)}) copy-start(bf16[512,128]{1,0:T(8,128)(2,1)} %key_ref.1) | copy-start | bytes 393220
  1.5 0.9 %copy-start.1 = (bf16[512,128]{1,0:T(8,128)(2,1)S(1)}, bf16[512,128]{1,0:T(8,128)(2,1)}, u32[]{:S(2)}) copy-start(bf16[512,128]{1,0:T(8,128)(2,1)} %value_ref.1) | copy-start | bytes 393220
  2.8 12.7 %collective-permute-start = (bf16[1024,128]{1,0:T(8,128)(2,1)S(1)}, bf16[1024,128]{1,0:T(8,128)(2,1)S(1)}, u32[]{:S(2)}, u32[]{:S(2)}) collective-permute-start(bf16[1024,128]{1,0:T(8,128)(2,1)S(1)} %pack.1.own_ref), channel_id=1, source_target_pairs={{0,8},{4,12},{8,16},{12,20},{16,24},{20,28},{24,32},{28,36},{32,40... | collective-permute-start | bytes 786440 | tf_op jit(solution)/shard_map/ppermute | solution.py:408
  5.6 13.8 %collective-permute-start.1 = (bf16[1024,128]{1,0:T(8,128)(2,1)S(1)}, bf16[1024,128]{1,0:T(8,128)(2,1)S(1)}, u32[]{:S(2)}, u32[]{:S(2)}) collective-permute-start(bf16[1024,128]{1,0:T(8,128)(2,1)S(1)} %pack.1.own_ref), channel_id=1, source_target_pairs={{0,4},{4,16},{8,12},{12,24},{16,20},{20,32},{24,28},{28,40},{32,36... | collective-permute-start | bytes 786440 | tf_op jit(solution)/shard_map/ppermute | solution.py:408
  7.6 1.0 %copy-start.2 = (bf16[512,256]{1,0:T(8,128)(2,1)S(1)}, bf16[512,256]{1,0:T(8,128)(2,1)}, u32[]{:S(2)}) copy-start(bf16[512,256]{1,0:T(8,128)(2,1)} %q_ref.7) | copy-start | bytes 786436
  8.5 0.9 %copy-start.4 = (bf16[512,256]{1,0:T(8,128)(2,1)S(1)}, bf16[512,256]{1,0:T(8,128)(2,1)}, u32[]{:S(2)}) copy-start(bf16[512,256]{1,0:T(8,128)(2,1)} %do_ref.7) | copy-start | bytes 786436
  9.5 0.7 copy-start.6
  15.5 3.9 %collective-permute-start.2 = (bf16[1024,128]{1,0:T(8,128)(2,1)S(1)}, bf16[1024,128]{1,0:T(8,128)(2,1)S(1)}, u32[]{:S(2)}, u32[]{:S(2)}) collective-permute-start(bf16[1024,128]{1,0:T(8,128)(2,1)S(1)} %collective-permute-done.block_ref), channel_id=1, source_target_pairs={{0,4},{4,0},{8,12},{12,8},{16,20},{20,16},{24,28},{28,24},{32,36},... | collective-permute-start | bytes 786440 | tf_op jit(solution)/shard_map/ppermute | solution.py:408
  17.4 2.0 %copy-start.3 = (bf16[512,256]{1,0:T(8,128)(2,1)S(1)}, bf16[512,256]{1,0:T(8,128)(2,1)}, u32[]{:S(2)}) copy-start(bf16[512,256]{1,0:T(8,128)(2,1)} %q_ref.7) | copy-start | bytes 786436
  17.5 2.0 %copy-start.5 = (bf16[512,256]{1,0:T(8,128)(2,1)S(1)}, bf16[512,256]{1,0:T(8,128)(2,1)}, u32[]{:S(2)}) copy-start(bf16[512,256]{1,0:T(8,128)(2,1)} %do_ref.7) | copy-start | bytes 786436
  25.1 5.6 %collective-permute-start.3 = (bf16[1024,128]{1,0:T(8,128)(2,1)S(1)}, bf16[1024,128]{1,0:T(8,128)(2,1)S(1)}, u32[]{:S(2)}, u32[]{:S(2)}) collective-permute-start(bf16[1024,128]{1,0:T(8,128)(2,1)S(1)} %get-tuple-element.54), channel_id=1, source_target_pairs={{0,4},{4,0},{8,12},{12,8},{16,20},{20,16},{24,28},{28,24},{32,36},... | collective-permute-start | bytes 786440 | tf_op jit(solution)/shard_map/ppermute | solution.py:408
  27.0 8.0 %collective-permute-start.5 = (bf16[1024,128]{1,0:T(8,128)(2,1)S(1)}, bf16[1024,128]{1,0:T(8,128)(2,1)S(1)}, u32[]{:S(2)}, u32[]{:S(2)}) collective-permute-start(bf16[1024,128]{1,0:T(8,128)(2,1)S(1)} %get-tuple-element.55), channel_id=1, source_target_pairs={{4,0},{16,4},{12,8},{24,12},{20,16},{32,20},{28,24},{40,28},{36,32... | collective-permute-start | bytes 786440 | tf_op jit(solution)/shard_map/ppermute | solution.py:408
  30.8 13.9 %collective-permute-start.4 = (bf16[1024,128]{1,0:T(8,128)(2,1)S(1)}, bf16[1024,128]{1,0:T(8,128)(2,1)S(1)}, u32[]{:S(2)}, u32[]{:S(2)}) collective-permute-start(bf16[1024,128]{1,0:T(8,128)(2,1)S(1)} %sum.2), channel_id=1, source_target_pairs={{8,0},{12,4},{16,8},{20,12},{24,16},{28,20},{32,24},{36,28},{40,32... | collective-permute-start | bytes 786440 | tf_op jit(solution)/shard_map/ppermute | solution.py:408

commit v8 on v7

--- a/solution.py
+++ b/solution.py
@@ -420,10 +420,12 @@
         return [(there, here) for here, there in pairs]
 
     lengths = doc_lengths.reshape(1, -1)
+    two_keys = moved(keys, two_on)
+    two_values = moved(values, two_on)
     own = packed(keys, values)
-    two = moved(own, two_on)
     mixed = moved(own, mixed_on)
     first, starts, top, total, out, qt, dot_ = attention_before(place, lengths, queries, d_out, own)
+    two = packed(two_keys, two_values)
     two, first = lax.optimization_barrier((two, first))
     swapped = moved(two, across)
     top, total, out, tile = attention_second(first, queries, starts, top, total, out, two)

time: 66.1 us -> 70 us (1.059)
  the two profiles are of different devices: /device:TPU:358 before, /device:TPU:102 now
where the time goes in v8:
time: 70 us; the launch traced here: 69.6 us
  starting transfers between devices  20.2 us (29%)
  blocking collectives  20 us (29%)
  Pallas kernels  13.6 us (19%)
  waiting for transfers between devices  9.77 us (14%)
  local copies, waits for them, and re-layouts  5.11 us (7%)
  between operations  0.85 us (1%)
    ppermute x7, starting transfers between devices, moved(): return lax.ppermute(value, 'ctx', pairs)  20.2 us
    pallas_call x7, Pallas kernels, on_core(): pl.pallas_call(kernel, out_shape=tuple(outs), in_specs=[SMEM if x.ndim ==...  12.9 us
    all_to_all x1, blocking collectives, head_sum(): theirs = lax.all_to_all(pieces, 'head', split_axis=0, concat_axis=0)  10.9 us
    ppermute x7, waiting for transfers between devices, moved(): return lax.ppermute(value, 'ctx', pairs)  9.77 us
    all_to_all x1, blocking collectives, head_sum(): lax.all_to_all(mine, 'head', split_axis=0, concat_axis=0)  9.07 us
    unnamed x14, local copies, waits for them, and re-layouts  4.36 us
  transfers between devices with their start and end apart: 7, of which 1 were waited for; matrix products, arithmetic and copies ran while one was open for 0% of the time, Pallas kernels for 11%

profile of v8, /device:TPU:102, one launch (start us, length us, event | category | flops | bytes accessed | tf_op | source)
XLA Modules:
  0.0 69.6 jit_solution(2363311505468278595)
XLA Ops:
  0.6 5.0 %collective-permute-start = (bf16[512,128]{1,0:T(8,128)(2,1)}, bf16[512,128]{1,0:T(8,128)(2,1)S(1)}, u32[]{:S(2)}, u32[]{:S(2)}) collective-permute-start(bf16[512,128]{1,0:T(8,128)(2,1)} %key_ref.1), channel_id=1, source_target_pairs={{0,8},{4,12},{8,16},{12,20},{16,24},{20,28},{24,32},{28,36},{32,40... | collective-permute-start | bytes 393224 | tf_op jit(solution)/shard_map/ppermute | solution.py:408
  5.6 3.4 %collective-permute-start.1 = (bf16[512,128]{1,0:T(8,128)(2,1)}, bf16[512,128]{1,0:T(8,128)(2,1)S(1)}, u32[]{:S(2)}, u32[]{:S(2)}) collective-permute-start(bf16[512,128]{1,0:T(8,128)(2,1)} %value_ref.1), channel_id=1, source_target_pairs={{0,8},{4,12},{8,16},{12,20},{16,24},{20,28},{24,32},{28,36},{32,40... | collective-permute-start | bytes 393224 | tf_op jit(solution)/shard_map/ppermute | solution.py:408
  9.0 0.0 copy-start
  9.0 0.9 %copy-done = bf16[512,128]{1,0:T(8,128)(2,1)S(1)} copy-done((bf16[512,128]{1,0:T(8,128)(2,1)S(1)}, bf16[512,128]{1,0:T(8,128)(2,1)}, u32[]{:S(2)}) %copy-start) | copy-done | bytes 131096
  9.9 0.0 copy-start.1
  9.9 0.9 %copy-done.1 = bf16[512,128]{1,0:T(8,128)(2,1)S(1)} copy-done((bf16[512,128]{1,0:T(8,128)(2,1)S(1)}, bf16[512,128]{1,0:T(8,128)(2,1)}, u32[]{:S(2)}) %copy-start.1) | copy-done | bytes 131096
  10.8 0.3 pack.2.own_ref
  11.1 1.9 %collective-permute-start.2 = (bf16[1024,128]{1,0:T(8,128)(2,1)S(1)}, bf16[1024,128]{1,0:T(8,128)(2,1)S(1)}, u32[]{:S(2)}, u32[]{:S(2)}) collective-permute-start(bf16[1024,128]{1,0:T(8,128)(2,1)S(1)} %pack.2.own_ref), channel_id=1, source_target_pairs={{0,4},{4,16},{8,12},{12,24},{16,20},{20,32},{24,28},{28,40},{32,36... | collective-permute-start | bytes 786440 | tf_op jit(solution)/shard_map/ppermute | solution.py:408
  13.1 0.0 copy-start.2
  13.1 0.9 %copy-done.2 = bf16[512,256]{1,0:T(8,128)(2,1)S(1)} copy-done((bf16[512,256]{1,0:T(8,128)(2,1)S(1)}, bf16[512,256]{1,0:T(8,128)(2,1)}, u32[]{:S(2)}) %copy-start.2) | copy-done | bytes 262168
  14.0 0.0 copy-start.4
  14.0 0.9 %copy-done.4 = bf16[512,256]{1,0:T(8,128)(2,1)S(1)} copy-done((bf16[512,256]{1,0:T(8,128)(2,1)S(1)}, bf16[512,256]{1,0:T(8,128)(2,1)}, u32[]{:S(2)}) %copy-start.4) | copy-done | bytes 262168
  15.0 0.0 copy-start.6
  15.0 0.7 copy-done.6
  15.6 1.2 %diagonal.1 = (s32[1]{0:T(128)}, s32[512,128]{1,0:T(8,128)S(1)}, f32[2,512,128]{2,1,0:T(8,128)S(1)}, f32[2,512,128]{2,1,0:T(8,128)S(1)}, f32[2,512,128]{2,1,0:T(...) custom-call(s32[1]{0:T(128)} %bitcast.place_ref, s32[1,128]{1,0:T(1,128)S(1)} %bitcast.6, ...), custom_call_target="tpu_custom_call" | custom-call | flops 1200000000 | bytes 2097152 | tf_op jit(solution)/shard_map/diagonal/pallas_call | solution.py:304
  16.8 0.0 collective-permute-done.key_ref
  16.8 0.0 collective-permute-done.1.value_ref
  16.8 0.4 pack.3.block_ref
  17.2 4.1 %collective-permute-start.3 = (bf16[1024,128]{1,0:T(8,128)(2,1)S(1)}, bf16[1024,128]{1,0:T(8,128)(2,1)S(1)}, u32[]{:S(2)}, u32[]{:S(2)}) collective-permute-start(bf16[1024,128]{1,0:T(8,128)(2,1)S(1)} %pack.3.block_ref), channel_id=1, source_target_pairs={{0,4},{4,0},{8,12},{12,8},{16,20},{20,16},{24,28},{28,24},{32,36},... | collective-permute-start | bytes 786440 | tf_op jit(solution)/shard_map/ppermute | solution.py:408
  21.4 0.0 copy-start.3
  21.4 0.0 copy-start.5
  21.4 1.9 %second.1 = (f32[2,512,128]{2,1,0:T(8,128)S(1)}, f32[2,512,128]{2,1,0:T(8,128)S(1)}, f32[2,512,128]{2,1,0:T(8,128)S(1)}, f32[2,512,512]{2,1,0:T(8,128)S(1)}) custom-call(s32[1]{0:T(128)} %get-tuple-element.34.first_ref, bf16[512,256]{1,0:T(8,128)(2,1)S(1)} %copy-done.2, s32[512,128]{1,0:T(8,128)S(1)} %get-tuple-element.32.starts_ref, ...), custom_call_target="tpu_custom_call" | custom-call | flops 1200000000 | bytes 2097152 | tf_op jit(solution)/shard_map/second/pallas_call | solution.py:304
  23.3 0.0 collective-permute-done.2.mixed_ref
  23.3 0.0 collective-permute-done.3.swapped_ref
  23.3 0.0 copy-done.3
  23.3 0.0 copy-done.5
  23.3 5.7 %far.1 = (bf16[512,256]{1,0:T(8,128)(2,1)S(1)}, f32[2,512,128]{2,1,0:T(8,128)S(1)}, f32[2,512,128]{2,1,0:T(8,128)S(1)}, f32[2,512,128]{2,1,0:T(8,128)S(1)}, f32[...) custom-call(s32[1]{0:T(128)} %bitcast.place_ref, ...), custom_call_target="tpu_custom_call" | custom-call | flops 3000000000 | bytes 2097152 | tf_op jit(solution)/shard_map/far/pallas_call | solution.py:304
  29.0 1.9 %collective-permute-start.4 = (bf16[1024,128]{1,0:T(8,128)(2,1)S(1)}, bf16[1024,128]{1,0:T(8,128)(2,1)S(1)}, u32[]{:S(2)}, u32[]{:S(2)}) collective-permute-start(bf16[1024,128]{1,0:T(8,128)(2,1)S(1)} %get-tuple-element.54), channel_id=1, source_target_pairs={{0,4},{4,0},{8,12},{12,8},{16,20},{20,16},{24,28},{28,24},{32,36},... | collective-permute-start | bytes 786440 | tf_op jit(solution)/shard_map/ppermute | solution.py:408
  31.0 1.9 %collective-permute-start.6 = (bf16[1024,128]{1,0:T(8,128)(2,1)S(1)}, bf16[1024,128]{1,0:T(8,128)(2,1)S(1)}, u32[]{:S(2)}, u32[]{:S(2)}) collective-permute-start(bf16[1024,128]{1,0:T(8,128)(2,1)S(1)} %get-tuple-element.55), channel_id=1, source_target_pairs={{4,0},{16,4},{12,8},{24,12},{20,16},{32,20},{28,24},{40,28},{36,32... | collective-permute-start | bytes 786440 | tf_op jit(solution)/shard_map/ppermute | solution.py:408
  32.9 1.7 %second_back.1 = (f32[2,512,128]{2,1,0:T(8,128)S(1)}, bf16[1024,128]{1,0:T(8,128)(2,1)S(1)}) custom-call(s32[1]{0:T(128)} %get-tuple-element.34.first_ref, bf16[512,256]{1,0:T(8,128)(2,1)S(1)} %copy-done.5, bf16[2,128,512]{2,1,0:T(8,128)(2,1)S(1)} %get-tuple-element.30.qt_ref, bf16[2,128,512]{2,1,0:T(8,128)(2,1)S(1)} %get-tuple-element.31.dot_ref, ...), custom_call_target="tpu_custom_call" | custom-call | flops 1500000000 | bytes 2097152 | tf_op jit(solution)/shard_map/second_back/pallas_call | solution.py:304
  34.6 0.0 collective-permute-done.4.refs_1_
  34.6 0.1 sum.2
  34.7 1.9 %collective-permute-start.5 = (bf16[1024,128]{1,0:T(8,128)(2,1)S(1)}, bf16[1024,128]{1,0:T(8,128)(2,1)S(1)}, u32[]{:S(2)}, u32[]{:S(2)}) collective-permute-start(bf16[1024,128]{1,0:T(8,128)(2,1)S(1)} %sum.2), channel_id=1, source_target_pairs={{8,0},{12,4},{16,8},{20,12},{24,16},{28,20},{32,24},{36,28},{40,32... | collective-permute-start | bytes 786440 | tf_op jit(solution)/shard_map/ppermute | solution.py:408
  36.6 2.3 %own.1 = (bf16[512,256]{1,0:T(8,128)(2,1)}, bf16[1024,128]{1,0:T(8,128)(2,1)S(1)}, bf16[512,256]{1,0:T(8,128)(2,1)}) custom-call(bf16[512,256]{1,0:T(8,128)(2,1)S(1)} %copy-done.3, bf16[512,256]{1,0:T(8,128)(2,1)S(1)} %copy-done.5, bf16[2,128,512]{2,1,0:T(8,128)(2,1)S(1)} %get-tuple-element.30.qt_ref, bf16[2,128,512]{2,1,0:T(8,128)(2,1)S(1)} %get-tuple-element.31.dot_ref, ...), custom_call_target="tpu_custom_call" | custom-call | flops 2500000000 | bytes 2097152 | tf_op jit(solution)/shard_map/own/pallas_call | solution.py:304
  38.9 0.0 collective-permute-done.6.refs_2_
  38.9 9.8 %collective-permute-done.5.refs_1_ = bf16[1024,128]{1,0:T(8,128)(2,1)S(1)} collective-permute-done((bf16[1024,128]{1,0:T(8,128)(2,1)S(1)}, bf16[1024,128]{1,0:T(8,128)(2,1)S(1)}, u32[]{:S(2)}, u32[]{:S(2)}) %collective-permute-start.5) | collective-permute-done | bytes 262176 | tf_op jit(solution)/shard_map/ppermute | solution.py:408
  48.7 0.1 sum.3
  48.8 10.9 %all_to_all.10 = bf16[4,256,128]{2,1,0:T(8,128)(2,1)S(1)} all-to-all(bf16[4,256,128]{2,1,0:T(8,128)(2,1)S(1)} %bitcast.5), channel_id=1, replica_groups=mesh['ctx'=128,'head'=4] {'head'}, dimensions={0} | all-to-all | bytes 524288 | tf_op jit(solution)/shard_map/all_to_all | solution.py:401
  59.8 9.1 %all_to_all.11 = bf16[4,256,128]{2,1,0:T(8,128)(2,1)S(1)} all-to-all(bf16[4,256,128]{2,1,0:T(8,128)(2,1)S(1)} %broadcast_in_dim.2), channel_id=1, replica_groups=mesh['ctx'=128,'head'=4] {'head'}, dimensions={0} | all-to-all | bytes 524288 | tf_op jit(solution)/shard_map/all_to_all | solution.py:404
  68.9 0.7 %fusion = (bf16[2,256,128]{2,1,0:T(8,128)(2,1)}, bf16[2,256,128]{2,1,0:T(8,128)(2,1)}) fusion(bf16[4,256,128]{2,1,0:T(8,128)(2,1)S(1)} %all_to_all.11), kind=kLoop, calls=%fused_computation | loop fusion | bytes 524288 | tf_op jit(solution)/shard_map/slice | solution.py:445
  (2 shorter events, 0.1 us)
Async XLA Ops:
  0.6 16.2 %collective-permute-start = (bf16[512,128]{1,0:T(8,128)(2,1)}, bf16[512,128]{1,0:T(8,128)(2,1)S(1)}, u32[]{:S(2)}, u32[]{:S(2)}) collective-permute-start(bf16[512,128]{1,0:T(8,128)(2,1)} %key_ref.1), channel_id=1, source_target_pairs={{0,8},{4,12},{8,16},{12,20},{16,24},{20,28},{24,32},{28,36},{32,40... | collective-permute-start | bytes 393224 | tf_op jit(solution)/shard_map/ppermute | solution.py:408
  5.6 11.2 %collective-permute-start.1 = (bf16[512,128]{1,0:T(8,128)(2,1)}, bf16[512,128]{1,0:T(8,128)(2,1)S(1)}, u32[]{:S(2)}, u32[]{:S(2)}) collective-permute-start(bf16[512,128]{1,0:T(8,128)(2,1)} %value_ref.1), channel_id=1, source_target_pairs={{0,8},{4,12},{8,16},{12,20},{16,24},{20,28},{24,32},{28,36},{32,40... | collective-permute-start | bytes 393224 | tf_op jit(solution)/shard_map/ppermute | solution.py:408
  9.0 0.9 %copy-start = (bf16[512,128]{1,0:T(8,128)(2,1)S(1)}, bf16[512,128]{1,0:T(8,128)(2,1)}, u32[]{:S(2)}) copy-start(bf16[512,128]{1,0:T(8,128)(2,1)} %key_ref.1) | copy-start | bytes 393220
  9.9 0.9 %copy-start.1 = (bf16[512,128]{1,0:T(8,128)(2,1)S(1)}, bf16[512,128]{1,0:T(8,128)(2,1)}, u32[]{:S(2)}) copy-start(bf16[512,128]{1,0:T(8,128)(2,1)} %value_ref.1) | copy-start | bytes 393220
  11.1 12.2 %collective-permute-start.2 = (bf16[1024,128]{1,0:T(8,128)(2,1)S(1)}, bf16[1024,128]{1,0:T(8,128)(2,1)S(1)}, u32[]{:S(2)}, u32[]{:S(2)}) collective-permute-start(bf16[1024,128]{1,0:T(8,128)(2,1)S(1)} %pack.2.own_ref), channel_id=1, source_target_pairs={{0,4},{4,16},{8,12},{12,24},{16,20},{20,32},{24,28},{28,40},{32,36... | collective-permute-start | bytes 786440 | tf_op jit(solution)/shard_map/ppermute | solution.py:408
  13.1 1.0 %copy-start.2 = (bf16[512,256]{1,0:T(8,128)(2,1)S(1)}, bf16[512,256]{1,0:T(8,128)(2,1)}, u32[]{:S(2)}) copy-start(bf16[512,256]{1,0:T(8,128)(2,1)} %q_ref.7) | copy-start | bytes 786436
  14.0 0.9 %copy-start.4 = (bf16[512,256]{1,0:T(8,128)(2,1)S(1)}, bf16[512,256]{1,0:T(8,128)(2,1)}, u32[]{:S(2)}) copy-start(bf16[512,256]{1,0:T(8,128)(2,1)} %do_ref.7) | copy-start | bytes 786436
  15.0 0.7 copy-start.6
  17.2 6.1 %collective-permute-start.3 = (bf16[1024,128]{1,0:T(8,128)(2,1)S(1)}, bf16[1024,128]{1,0:T(8,128)(2,1)S(1)}, u32[]{:S(2)}, u32[]{:S(2)}) collective-permute-start(bf16[1024,128]{1,0:T(8,128)(2,1)S(1)} %pack.3.block_ref), channel_id=1, source_target_pairs={{0,4},{4,0},{8,12},{12,8},{16,20},{20,16},{24,28},{28,24},{32,36},... | collective-permute-start | bytes 786440 | tf_op jit(solution)/shard_map/ppermute | solution.py:408
  21.4 2.0 %copy-start.3 = (bf16[512,256]{1,0:T(8,128)(2,1)S(1)}, bf16[512,256]{1,0:T(8,128)(2,1)}, u32[]{:S(2)}) copy-start(bf16[512,256]{1,0:T(8,128)(2,1)} %q_ref.7) | copy-start | bytes 786436
  21.4 2.0 %copy-start.5 = (bf16[512,256]{1,0:T(8,128)(2,1)S(1)}, bf16[512,256]{1,0:T(8,128)(2,1)}, u32[]{:S(2)}) copy-start(bf16[512,256]{1,0:T(8,128)(2,1)} %do_ref.7) | copy-start | bytes 786436
  29.0 5.6 %collective-permute-start.4 = (bf16[1024,128]{1,0:T(8,128)(2,1)S(1)}, bf16[1024,128]{1,0:T(8,128)(2,1)S(1)}, u32[]{:S(2)}, u32[]{:S(2)}) collective-permute-start(bf16[1024,128]{1,0:T(8,128)(2,1)S(1)} %get-tuple-element.54), channel_id=1, source_target_pairs={{0,4},{4,0},{8,12},{12,8},{16,20},{20,16},{24,28},{28,24},{32,36},... | collective-permute-start | bytes 786440 | tf_op jit(solution)/shard_map/ppermute | solution.py:408
  31.0 8.0 %collective-permute-start.6 = (bf16[1024,128]{1,0:T(8,128)(2,1)S(1)}, bf16[1024,128]{1,0:T(8,128)(2,1)S(1)}, u32[]{:S(2)}, u32[]{:S(2)}) collective-permute-start(bf16[1024,128]{1,0:T(8,128)(2,1)S(1)} %get-tuple-element.55), channel_id=1, source_target_pairs={{4,0},{16,4},{12,8},{24,12},{20,16},{32,20},{28,24},{40,28},{36,32... | collective-permute-start | bytes 786440 | tf_op jit(solution)/shard_map/ppermute | solution.py:408
  34.7 14.0 %collective-permute-start.5 = (bf16[1024,128]{1,0:T(8,128)(2,1)S(1)}, bf16[1024,128]{1,0:T(8,128)(2,1)S(1)}, u32[]{:S(2)}, u32[]{:S(2)}) collective-permute-start(bf16[1024,128]{1,0:T(8,128)(2,1)S(1)} %sum.2), channel_id=1, source_target_pairs={{8,0},{12,4},{16,8},{20,12},{24,16},{28,20},{32,24},{36,28},{40,32... | collective-permute-start | bytes 786440 | tf_op jit(solution)/shard_map/ppermute | solution.py:408

commit v9 on v7

--- a/solution.py
+++ b/solution.py
@@ -279,9 +279,12 @@
     part_ref[pl.ds(rows, rows), :] = dv.T.astype(BF)
 
 
-def sum_kernel(*refs):
-    *terms, out_ref = refs
-    out_ref[...] = sum(x[...].astype(F32) for x in terms).astype(BF)
+def stack_kernel(two_ref, core_ref, own_ref, mixed_ref, out_ref):
+    pieces, _, rows, _ = out_ref.shape
+    for slot, (a, b) in enumerate(((two_ref, core_ref), (own_ref, mixed_ref))):
+        for piece in range(pieces):
+            at = pl.ds(piece * rows, rows)
+            out_ref[piece, slot] = (a[at, :].astype(F32) + b[at, :].astype(F32)).astype(BF)
 
 
 def score_scale(head):
@@ -366,8 +369,10 @@
     return on_core(own_kernel, "own", 2500, 20, [like_q, part, like_q], ins)
 
 
-def summed(*terms):
-    return on_core(sum_kernel, "sum", 1, 6, [shape(terms[0].shape, BF)], terms)[0]
+def stacked(pieces, two, core, own, mixed):
+    rows, head = own.shape
+    out = shape((pieces, 2, rows // pieces, head), BF)
+    return on_core(stack_kernel, "stack", 1, 6, [out], (two, core, own, mixed))[0]
 
 
 def pack_kernel(key_ref, value_ref, both_ref, sems):
@@ -395,13 +400,8 @@
     )(keys, values)
 
 
-def head_sum(part):
-    heads = lax.axis_size("head")
-    pieces = part.reshape(heads, part.shape[0] // heads, part.shape[1])
-    theirs = lax.all_to_all(pieces, "head", split_axis=0, concat_axis=0)
-    mine = jnp.sum(theirs.astype(F32), axis=0).astype(BF)
-    mine = jnp.broadcast_to(mine[None], pieces.shape)
-    return lax.all_to_all(mine, "head", split_axis=0, concat_axis=0).reshape(part.shape)
+def exchanged(pieces):
+    return lax.all_to_all(pieces, "head", split_axis=0, concat_axis=0)
 
 
 def moved(value, pairs):
@@ -435,11 +435,15 @@
     dq, two_part = attention_second_back(
         first, queries, d_out, qt, dot_, two, tile, factor, row_dot, dq
     )
-    from_two = moved(summed(two_part, from_core), back(two_on))
     d_queries, own_part, attended = attention_own(
         queries, d_out, qt, dot_, own, starts, top, inverse, row_dot, dq, attended
     )
-    both = head_sum(summed(own_part, from_two, from_mixed))
+    heads = lax.axis_size("head")
+    quarters = exchanged(stacked(heads, two_part, from_core, own_part, from_mixed))
+    passed, mine = jnp.sum(quarters.astype(F32), axis=0)
+    from_two = moved(passed.astype(BF), back(two_on))
+    mine = (mine + from_two.astype(F32)).astype(BF)
+    both = exchanged(jnp.broadcast_to(mine[None], (heads,) + mine.shape)).reshape(own.shape)
     return (attended, d_queries, both[:rows], both[rows:])
 
 

time: 66.1 us -> 66.9 us (1.012)
  the two profiles are of different devices: /device:TPU:358 before, /device:TPU:6 now
where the time goes in v9:
time: 66.9 us; the launch traced here: 66.5 us
  blocking collectives  22.1 us (33%)
  starting transfers between devices  21.3 us (32%)
  Pallas kernels  8.99 us (13%)
  waiting for transfers between devices  8.03 us (12%)
  local copies, waits for them, and re-layouts  5.12 us (8%)
  between operations  0.79 us (1%)
    all_to_all x2, blocking collectives, exchanged(): return lax.all_to_all(pieces, 'head', split_axis=0, concat_axis=0)  22.1 us
    ppermute x6, starting transfers between devices, moved(): return lax.ppermute(value, 'ctx', pairs)  21.3 us
    pallas_call x6, Pallas kernels, on_core(): pl.pallas_call(kernel, out_shape=tuple(outs), in_specs=[SMEM if x.ndim ==...  8.66 us
    ppermute x6, waiting for transfers between devices, moved(): return lax.ppermute(value, 'ctx', pairs)  8.03 us
    unnamed x14, local copies, waits for them, and re-layouts  4.36 us
  transfers between devices with their start and end apart: 6, of which 4 were waited for; matrix products, arithmetic and copies ran while one was open for 0% of the time, Pallas kernels for 7%

profile of v9, /device:TPU:6, one launch (start us, length us, event | category | flops | bytes accessed | tf_op | source)
XLA Modules:
  0.0 66.5 jit_solution(12899058740230416585)
XLA Ops:
  0.6 0.0 copy-start
  0.6 0.9 %copy-done = bf16[512,128]{1,0:T(8,128)(2,1)S(1)} copy-done((bf16[512,128]{1,0:T(8,128)(2,1)S(1)}, bf16[512,128]{1,0:T(8,128)(2,1)}, u32[]{:S(2)}) %copy-start) | copy-done | bytes 131096
  1.5 0.0 copy-start.1
  1.5 0.9 %copy-done.1 = bf16[512,128]{1,0:T(8,128)(2,1)S(1)} copy-done((bf16[512,128]{1,0:T(8,128)(2,1)S(1)}, bf16[512,128]{1,0:T(8,128)(2,1)}, u32[]{:S(2)}) %copy-start.1) | copy-done | bytes 131096
  2.4 0.3 pack.1.own_ref
  2.8 3.7 %collective-permute-start = (bf16[1024,128]{1,0:T(8,128)(2,1)S(1)}, bf16[1024,128]{1,0:T(8,128)(2,1)S(1)}, u32[]{:S(2)}, u32[]{:S(2)}) collective-permute-start(bf16[1024,128]{1,0:T(8,128)(2,1)S(1)} %pack.1.own_ref), channel_id=1, source_target_pairs={{0,8},{4,12},{8,16},{12,20},{16,24},{20,28},{24,32},{28,36},{32,40... | collective-permute-start | bytes 786440 | tf_op jit(solution)/shard_map/ppermute | solution.py:408
  6.5 1.9 %collective-permute-start.1 = (bf16[1024,128]{1,0:T(8,128)(2,1)S(1)}, bf16[1024,128]{1,0:T(8,128)(2,1)S(1)}, u32[]{:S(2)}, u32[]{:S(2)}) collective-permute-start(bf16[1024,128]{1,0:T(8,128)(2,1)S(1)} %pack.1.own_ref), channel_id=1, source_target_pairs={{0,4},{4,16},{8,12},{12,24},{16,20},{20,32},{24,28},{28,40},{32,36... | collective-permute-start | bytes 786440 | tf_op jit(solution)/shard_map/ppermute | solution.py:408
  8.5 0.0 copy-start.2
  8.5 0.9 %copy-done.2 = bf16[512,256]{1,0:T(8,128)(2,1)S(1)} copy-done((bf16[512,256]{1,0:T(8,128)(2,1)S(1)}, bf16[512,256]{1,0:T(8,128)(2,1)}, u32[]{:S(2)}) %copy-start.2) | copy-done | bytes 262168
  9.4 0.0 copy-start.4
  9.4 0.9 %copy-done.4 = bf16[512,256]{1,0:T(8,128)(2,1)S(1)} copy-done((bf16[512,256]{1,0:T(8,128)(2,1)S(1)}, bf16[512,256]{1,0:T(8,128)(2,1)}, u32[]{:S(2)}) %copy-start.4) | copy-done | bytes 262168
  10.4 0.0 copy-start.6
  10.4 0.7 copy-done.6
  11.0 1.2 %diagonal.1 = (s32[1]{0:T(128)}, s32[512,128]{1,0:T(8,128)S(1)}, f32[2,512,128]{2,1,0:T(8,128)S(1)}, f32[2,512,128]{2,1,0:T(8,128)S(1)}, f32[2,512,128]{2,1,0:T(...) custom-call(s32[1]{0:T(128)} %bitcast.place_ref, s32[1,128]{1,0:T(1,128)S(1)} %bitcast.12, ...), custom_call_target="tpu_custom_call" | custom-call | flops 1200000000 | bytes 2097152 | tf_op jit(solution)/shard_map/diagonal/pallas_call | solution.py:307
  12.2 0.5 collective-permute-done.block_ref
  12.7 3.9 %collective-permute-start.2 = (bf16[1024,128]{1,0:T(8,128)(2,1)S(1)}, bf16[1024,128]{1,0:T(8,128)(2,1)S(1)}, u32[]{:S(2)}, u32[]{:S(2)}) collective-permute-start(bf16[1024,128]{1,0:T(8,128)(2,1)S(1)} %collective-permute-done.block_ref), channel_id=1, source_target_pairs={{0,4},{4,0},{8,12},{12,8},{16,20},{20,16},{24,28},{28,24},{32,36},... | collective-permute-start | bytes 786440 | tf_op jit(solution)/shard_map/ppermute | solution.py:408
  16.7 0.0 copy-start.3
  16.7 0.0 copy-start.5
  16.7 0.8 %second.1 = (f32[2,512,128]{2,1,0:T(8,128)S(1)}, f32[2,512,128]{2,1,0:T(8,128)S(1)}, f32[2,512,128]{2,1,0:T(8,128)S(1)}, f32[2,512,512]{2,1,0:T(8,128)S(1)}) custom-call(s32[1]{0:T(128)} %get-tuple-element.34.first_ref, bf16[512,256]{1,0:T(8,128)(2,1)S(1)} %copy-done.2, s32[512,128]{1,0:T(8,128)S(1)} %get-tuple-element.32.starts_ref, ...), custom_call_target="tpu_custom_call" | custom-call | flops 1200000000 | bytes 2097152 | tf_op jit(solution)/shard_map/second/pallas_call | solution.py:307
  17.5 0.0 collective-permute-done.1.mixed_ref
  17.5 0.3 collective-permute-done.2.swapped_ref
  17.8 0.0 copy-done.3
  17.8 0.0 copy-done.5
  17.8 3.6 %far.1 = (bf16[512,256]{1,0:T(8,128)(2,1)S(1)}, f32[2,512,128]{2,1,0:T(8,128)S(1)}, f32[2,512,128]{2,1,0:T(8,128)S(1)}, f32[2,512,128]{2,1,0:T(8,128)S(1)}, f32[...) custom-call(s32[1]{0:T(128)} %bitcast.place_ref, ...), custom_call_target="tpu_custom_call" | custom-call | flops 3000000000 | bytes 2097152 | tf_op jit(solution)/shard_map/far/pallas_call | solution.py:307
  21.4 2.7 %collective-permute-start.3 = (bf16[1024,128]{1,0:T(8,128)(2,1)S(1)}, bf16[1024,128]{1,0:T(8,128)(2,1)S(1)}, u32[]{:S(2)}, u32[]{:S(2)}) collective-permute-start(bf16[1024,128]{1,0:T(8,128)(2,1)S(1)} %get-tuple-element.53), channel_id=1, source_target_pairs={{0,4},{4,0},{8,12},{12,8},{16,20},{20,16},{24,28},{28,24},{32,36},... | collective-permute-start | bytes 786440 | tf_op jit(solution)/shard_map/ppermute | solution.py:408
  24.1 7.1 %collective-permute-start.4 = (bf16[1024,128]{1,0:T(8,128)(2,1)S(1)}, bf16[1024,128]{1,0:T(8,128)(2,1)S(1)}, u32[]{:S(2)}, u32[]{:S(2)}) collective-permute-start(bf16[1024,128]{1,0:T(8,128)(2,1)S(1)} %get-tuple-element.55), channel_id=1, source_target_pairs={{4,0},{16,4},{12,8},{24,12},{20,16},{32,20},{28,24},{40,28},{36,32... | collective-permute-start | bytes 786440 | tf_op jit(solution)/shard_map/ppermute | solution.py:408
  31.2 0.7 %second_back.1 = (f32[2,512,128]{2,1,0:T(8,128)S(1)}, bf16[1024,128]{1,0:T(8,128)(2,1)S(1)}) custom-call(s32[1]{0:T(128)} %get-tuple-element.34.first_ref, bf16[512,256]{1,0:T(8,128)(2,1)S(1)} %copy-done.5, bf16[2,128,512]{2,1,0:T(8,128)(2,1)S(1)} %get-tuple-element.30.qt_ref, bf16[2,128,512]{2,1,0:T(8,128)(2,1)S(1)} %get-tuple-element.31.dot_ref, ...), custom_call_target="tpu_custom_call" | custom-call | flops 1500000000 | bytes 2097152 | tf_op jit(solution)/shard_map/second_back/pallas_call | solution.py:307
  31.9 2.2 %own.1 = (bf16[512,256]{1,0:T(8,128)(2,1)}, bf16[1024,128]{1,0:T(8,128)(2,1)S(1)}, bf16[512,256]{1,0:T(8,128)(2,1)}) custom-call(bf16[512,256]{1,0:T(8,128)(2,1)S(1)} %copy-done.3, bf16[512,256]{1,0:T(8,128)(2,1)S(1)} %copy-done.5, bf16[2,128,512]{2,1,0:T(8,128)(2,1)S(1)} %get-tuple-element.30.qt_ref, bf16[2,128,512]{2,1,0:T(8,128)(2,1)S(1)} %get-tuple-element.31.dot_ref, ...), custom_call_target="tpu_custom_call" | custom-call | flops 2500000000 | bytes 2097152 | tf_op jit(solution)/shard_map/own/pallas_call | solution.py:307
  34.2 0.0 collective-permute-done.3.core_ref
  34.2 0.9 %collective-permute-done.4.mixed_ref = bf16[1024,128]{1,0:T(8,128)(2,1)S(1)} collective-permute-done((bf16[1024,128]{1,0:T(8,128)(2,1)S(1)}, bf16[1024,128]{1,0:T(8,128)(2,1)S(1)}, u32[]{:S(2)}, u32[]{:S(2)}) %collective-permute-start.4) | collective-permute-done | bytes 262176 | tf_op jit(solution)/shard_map/ppermute | solution.py:408
  35.1 0.1 stack.1
  35.2 13.1 %all_to_all.10 = bf16[4,2,256,128]{3,2,1,0:T(8,128)(2,1)S(1)} all-to-all(bf16[4,2,256,128]{3,2,1,0:T(8,128)(2,1)S(1)} %stack.1), channel_id=1, replica_groups=mesh['ctx'=128,'head'=4] {'head'}, dimensions={0} | all-to-all | bytes 1048576 | tf_op jit(solution)/shard_map/all_to_all | solution.py:404
  48.3 0.1 convert_reduce_fusion
  48.4 1.9 %collective-permute-start.5 = (bf16[256,128]{1,0:T(8,128)(2,1)S(1)}, bf16[256,128]{1,0:T(8,128)(2,1)S(1)}, u32[]{:S(2)}, u32[]{:S(2)}) collective-permute-start(bf16[256,128]{1,0:T(8,128)(2,1)S(1)} %fusion.2), channel_id=1, source_target_pairs={{8,0},{12,4},{16,8},{20,12},{24,16},{28,20},{32,24},{36,28},{40,32... | collective-permute-start | bytes 196616 | tf_op jit(solution)/shard_map/ppermute | solution.py:408
  50.3 6.3 %collective-permute-done.5 = bf16[256,128]{1,0:T(8,128)(2,1)S(1)} collective-permute-done((bf16[256,128]{1,0:T(8,128)(2,1)S(1)}, bf16[256,128]{1,0:T(8,128)(2,1)S(1)}, u32[]{:S(2)}, u32[]{:S(2)}) %collective-permute-start.5) | collective-permute-done | bytes 65568 | tf_op jit(solution)/shard_map/ppermute | solution.py:408
  56.7 9.1 %all_to_all.11 = bf16[4,256,128]{2,1,0:T(8,128)(2,1)S(1)} all-to-all(bf16[4,256,128]{2,1,0:T(8,128)(2,1)S(1)} %broadcast_in_dim.2), channel_id=1, replica_groups=mesh['ctx'=128,'head'=4] {'head'}, dimensions={0} | all-to-all | bytes 524288 | tf_op jit(solution)/shard_map/all_to_all | solution.py:404
  65.8 0.7 %fusion.3 = (bf16[2,256,128]{2,1,0:T(8,128)(2,1)}, bf16[2,256,128]{2,1,0:T(8,128)(2,1)}) fusion(bf16[4,256,128]{2,1,0:T(8,128)(2,1)S(1)} %all_to_all.11), kind=kLoop, calls=%fused_computation.6 | loop fusion | bytes 524288 | tf_op jit(solution)/shard_map/slice | solution.py:447
  (3 shorter events, 0.1 us)
Async XLA Ops:
  0.6 0.9 %copy-start = (bf16[512,128]{1,0:T(8,128)(2,1)S(1)}, bf16[512,128]{1,0:T(8,128)(2,1)}, u32[]{:S(2)}) copy-start(bf16[512,128]{1,0:T(8,128)(2,1)} %key_ref.1) | copy-start | bytes 393220
  1.5 0.9 %copy-start.1 = (bf16[512,128]{1,0:T(8,128)(2,1)S(1)}, bf16[512,128]{1,0:T(8,128)(2,1)}, u32[]{:S(2)}) copy-start(bf16[512,128]{1,0:T(8,128)(2,1)} %value_ref.1) | copy-start | bytes 393220
  2.8 9.9 %collective-permute-start = (bf16[1024,128]{1,0:T(8,128)(2,1)S(1)}, bf16[1024,128]{1,0:T(8,128)(2,1)S(1)}, u32[]{:S(2)}, u32[]{:S(2)}) collective-permute-start(bf16[1024,128]{1,0:T(8,128)(2,1)S(1)} %pack.1.own_ref), channel_id=1, source_target_pairs={{0,8},{4,12},{8,16},{12,20},{16,24},{20,28},{24,32},{28,36},{32,40... | collective-permute-start | bytes 786440 | tf_op jit(solution)/shard_map/ppermute | solution.py:408
  6.5 11.0 %collective-permute-start.1 = (bf16[1024,128]{1,0:T(8,128)(2,1)S(1)}, bf16[1024,128]{1,0:T(8,128)(2,1)S(1)}, u32[]{:S(2)}, u32[]{:S(2)}) collective-permute-start(bf16[1024,128]{1,0:T(8,128)(2,1)S(1)} %pack.1.own_ref), channel_id=1, source_target_pairs={{0,4},{4,16},{8,12},{12,24},{16,20},{20,32},{24,28},{28,40},{32,36... | collective-permute-start | bytes 786440 | tf_op jit(solution)/shard_map/ppermute | solution.py:408
  8.5 1.0 %copy-start.2 = (bf16[512,256]{1,0:T(8,128)(2,1)S(1)}, bf16[512,256]{1,0:T(8,128)(2,1)}, u32[]{:S(2)}) copy-start(bf16[512,256]{1,0:T(8,128)(2,1)} %q_ref.7) | copy-start | bytes 786436
  9.4 0.9 %copy-start.4 = (bf16[512,256]{1,0:T(8,128)(2,1)S(1)}, bf16[512,256]{1,0:T(8,128)(2,1)}, u32[]{:S(2)}) copy-start(bf16[512,256]{1,0:T(8,128)(2,1)} %do_ref.7) | copy-start | bytes 786436
  10.4 0.7 copy-start.6
  12.7 5.1 %collective-permute-start.2 = (bf16[1024,128]{1,0:T(8,128)(2,1)S(1)}, bf16[1024,128]{1,0:T(8,128)(2,1)S(1)}, u32[]{:S(2)}, u32[]{:S(2)}) collective-permute-start(bf16[1024,128]{1,0:T(8,128)(2,1)S(1)} %collective-permute-done.block_ref), channel_id=1, source_target_pairs={{0,4},{4,0},{8,12},{12,8},{16,20},{20,16},{24,28},{28,24},{32,36},... | collective-permute-start | bytes 786440 | tf_op jit(solution)/shard_map/ppermute | solution.py:408
  16.7 1.1 %copy-start.3 = (bf16[512,256]{1,0:T(8,128)(2,1)S(1)}, bf16[512,256]{1,0:T(8,128)(2,1)}, u32[]{:S(2)}) copy-start(bf16[512,256]{1,0:T(8,128)(2,1)} %q_ref.7) | copy-start | bytes 786436
  16.7 1.1 %copy-start.5 = (bf16[512,256]{1,0:T(8,128)(2,1)S(1)}, bf16[512,256]{1,0:T(8,128)(2,1)}, u32[]{:S(2)}) copy-start(bf16[512,256]{1,0:T(8,128)(2,1)} %do_ref.7) | copy-start | bytes 786436
  21.4 12.8 %collective-permute-start.3 = (bf16[1024,128]{1,0:T(8,128)(2,1)S(1)}, bf16[1024,128]{1,0:T(8,128)(2,1)S(1)}, u32[]{:S(2)}, u32[]{:S(2)}) collective-permute-start(bf16[1024,128]{1,0:T(8,128)(2,1)S(1)} %get-tuple-element.53), channel_id=1, source_target_pairs={{0,4},{4,0},{8,12},{12,8},{16,20},{20,16},{24,28},{28,24},{32,36},... | collective-permute-start | bytes 786440 | tf_op jit(solution)/shard_map/ppermute | solution.py:408
  24.1 11.0 %collective-permute-start.4 = (bf16[1024,128]{1,0:T(8,128)(2,1)S(1)}, bf16[1024,128]{1,0:T(8,128)(2,1)S(1)}, u32[]{:S(2)}, u32[]{:S(2)}) collective-permute-start(bf16[1024,128]{1,0:T(8,128)(2,1)S(1)} %get-tuple-element.55), channel_id=1, source_target_pairs={{4,0},{16,4},{12,8},{24,12},{20,16},{32,20},{28,24},{40,28},{36,32... | collective-permute-start | bytes 786440 | tf_op jit(solution)/shard_map/ppermute | solution.py:408
  48.4 8.3 %collective-permute-start.5 = (bf16[256,128]{1,0:T(8,128)(2,1)S(1)}, bf16[256,128]{1,0:T(8,128)(2,1)S(1)}, u32[]{:S(2)}, u32[]{:S(2)}) collective-permute-start(bf16[256,128]{1,0:T(8,128)(2,1)S(1)} %fusion.2), channel_id=1, source_target_pairs={{8,0},{12,4},{16,8},{20,12},{24,16},{28,20},{32,24},{36,28},{40,32... | collective-permute-start | bytes 196616 | tf_op jit(solution)/shard_map/ppermute | solution.py:408

commit v10 on v7

--- a/solution.py
+++ b/solution.py
@@ -114,7 +114,7 @@
     place_ref, first_ref, q_ref, do_ref, qt_ref, dot_ref, starts_ref, top0_ref, total0_ref, out0_ref,
     mixed_ref, swapped_ref,
     att_ref, top_ref, inverse_ref, row_dot_ref, second_ref, dq_ref, mixed_part_ref, swapped_part_ref,
-    key_window, value_window, key_parts, value_parts, tiles, lanes,
+    window, parts,
 ):
     rows, width = q_ref.shape
     head = mixed_ref.shape[1]
@@ -122,101 +122,99 @@
     to_exp2 = exp2_scale(head)
     scale = score_scale(head)
     odd = lax.rem(place_ref[0], 2)
-    mixed_row = pl.multiple_of((1 - odd) * rows, rows)
-    swapped_row = pl.multiple_of(odd * rows, rows)
-    slots = (
-        (mixed_ref, mixed_part_ref, mixed_row),
-        (swapped_ref, swapped_part_ref, swapped_row),
-    )
+    slots = ((mixed_ref, mixed_part_ref, 1 - odd), (swapped_ref, swapped_part_ref, odd))
     low = lowest_block(first_ref, rows)
     live = (low < SPAN).astype(jnp.int32) + (low < 1).astype(jnp.int32)
-    column = lax.broadcasted_iota(jnp.int32, (rows, rows), 1)
-
-    def score_tile(t, carry):
-        at = pl.multiple_of(t * rows, rows)
-        keys = key_window[pl.ds(at, rows), :]
-        allowed = column >= wide(starts_ref[...] + (rows + 2 * at), rows)
+    def on_rows(r0, n, blocks):
+        row = pl.ds(r0, n)
+        keys = [window[b, pl.ds(k0, m), :] for b, k0, m in blocks]
+        values = [window[b, pl.ds(rows + k0, m), :] for b, k0, m in blocks]
+        allowed = [
+            lax.broadcasted_iota(jnp.int32, (n, m), 1)
+            >= wide(starts_ref[row, :] + ((1 + 2 * b) * rows - k0), m)
+            for b, k0, m in blocks
+        ]
+        dv = [jnp.zeros((head, m), F32) for _, _, m in blocks]
+        dk = [jnp.zeros((head, m), F32) for _, _, m in blocks]
         for h in range(heads):
-            s = dot_nt(q_ref[:, pl.ds(h * head, head)], keys)
-            s = jnp.where(allowed, s, -jnp.inf)
-            tiles[h, t] = s
-            lanes[h] = jnp.maximum(lanes[h], folded(s, head, jnp.maximum))
-        return carry
-
-    def out_tile(t, carry):
-        at = pl.multiple_of(t * rows, rows)
-        values = value_window[pl.ds(at, rows), :]
-        for h in range(heads):
-            e = jnp.exp2((tiles[h, t] - wide(top_ref[h], rows)) * to_exp2)
-            tiles[h, t] = e
-            lanes[h] += folded(e, head, jnp.add)
-            dq_ref[h] += dot_nn(e.astype(BF), values)
-        return carry
-
-    def grad_tile(t, carry):
-        at = pl.multiple_of(t * rows, rows)
-        keys = key_window[pl.ds(at, rows), :]
-        values = value_window[pl.ds(at, rows), :]
-        dv = jnp.zeros((head, rows), F32)
-        dk = jnp.zeros((head, rows), F32)
-        for h in range(heads):
-            dw = dot_nt(do_ref[:, pl.ds(h * head, head)], values)
-            w = tiles[h, t] * wide(inverse_ref[h], rows)
-            ds = (w * (dw - wide(row_dot_ref[h], rows))).astype(BF)
-            dv = dv + dot_nn(dot_ref[h], w.astype(BF))
-            dk = dk + dot_nn(qt_ref[h], ds)
-            dq_ref[h] += dot_nn(ds, keys)
-        key_parts[pl.ds(at, rows), :] = (dk * scale).T.astype(BF)
-        value_parts[pl.ds(at, rows), :] = dv.T.astype(BF)
-        return carry
-
-    def zero_tile(t, carry):
-        at = pl.multiple_of(t * rows, rows)
-        key_parts[pl.ds(at, rows), :] = jnp.zeros((rows, head), BF)
-        value_parts[pl.ds(at, rows), :] = jnp.zeros((rows, head), BF)
-        return carry
-
-    @pl.when(live > 0)
-    def _():
-        for block, _, at in slots:
-            key_window[pl.ds(at, rows), :] = block[pl.ds(0, rows), :]
-            value_window[pl.ds(at, rows), :] = block[pl.ds(rows, rows), :]
-        lanes[...] = top0_ref[...]
-        lax.fori_loop(0, live, score_tile, 0)
-        for h in range(heads):
-            top = across_lanes(lanes[h], jnp.max, lanes[h])
-            top_ref[h] = top
-            kept = jnp.exp2((top0_ref[h] - top) * to_exp2)
-            second_ref[h] = kept
-            inverse_ref[h] = total0_ref[h] * kept
-            dq_ref[h] = out0_ref[h] * kept
-        lanes[...] = jnp.zeros(lanes.shape, F32)
-        lax.fori_loop(0, live, out_tile, 0)
-        for h in range(heads):
-            inverse_ref[h] += jnp.sum(lanes[h], axis=1, keepdims=True)
+            cols = pl.ds(h * head, head)
+            top = top0 = top0_ref[h, row, :]
+            total = total0_ref[h, row, :]
+            out = out0_ref[h, row, :]
+            kept = 1.0
+            e = []
+            if blocks:
+                s = [
+                    jnp.where(ok, dot_nt(q_ref[row, cols], k), -jnp.inf)
+                    for ok, k in zip(allowed, keys)
+                ]
+                for x in s:
+                    top = jnp.maximum(top, folded(x, head, jnp.maximum))
+                top = across_lanes(top, jnp.max, top)
+                kept = jnp.exp2((top0 - top) * to_exp2)
+                e = [jnp.exp2((x - wide(top, x.shape[1])) * to_exp2) for x in s]
+                sums = functools.reduce(jnp.add, [folded(x, head, jnp.add) for x in e])
+                total = total * kept + across_lanes(sums, jnp.sum, top)
+                out = out * kept
+                for x, v in zip(e, values):
+                    out = out + dot_nn(x.astype(BF), v)
+            inverse = 1.0 / total
+            attended = (out * inverse).astype(BF)
+            products = do_ref[row, cols].astype(F32) * attended.astype(F32)
+            row_dot = across_lanes(products, jnp.sum, top)
+            att_ref[row, cols] = attended
+            top_ref[h, row, :] = top
+            inverse_ref[h, row, :] = inverse
+            row_dot_ref[h, row, :] = row_dot
+            second_ref[h, row, :] = kept * inverse
+            dq = jnp.zeros((n, head), F32)
+            for i, (x, k, v) in enumerate(zip(e, keys, values)):
+                m = x.shape[1]
+                dw = dot_nt(do_ref[row, cols], v)
+                w = x * wide(inverse, m)
+                ds = (w * (dw - wide(row_dot, m))).astype(BF)
+                dv[i] = dv[i] + dot_nn(dot_ref[h, :, row], w.astype(BF))
+                dk[i] = dk[i] + dot_nn(qt_ref[h, :, row], ds)
+                dq = dq + dot_nn(ds, k)
+            dq_ref[h, row, :] = dq
+        for (b, k0, m), a, c in zip(blocks, dk, dv):
+            parts[b, pl.ds(k0, m), :] = (a * scale).T.astype(BF)
+            parts[b, pl.ds(rows + k0, m), :] = c.T.astype(BF)
+
+    for block, _, at in slots:
+        @pl.when(at < live)
+        def _():
+            window[at] = block[...]
+
+    half = rows // 2
+    near, far = (0, 0, rows), (1, 0, rows)
+    low_half = first_ref[0] < half
+
+    @pl.when(live < 2)
+    def _():
+        parts[1] = jnp.zeros(parts.shape[1:], BF)
 
     @pl.when(live == 0)
     def _():
-        top_ref[...] = top0_ref[...]
-        second_ref[...] = jnp.ones(second_ref.shape, F32)
-        inverse_ref[...] = total0_ref[...]
-        dq_ref[...] = out0_ref[...]
-
-    for h in range(heads):
-        cols = pl.ds(h * head, head)
-        inverse = 1.0 / inverse_ref[h]
-        inverse_ref[h] = inverse
-        second_ref[h] = second_ref[h] * inverse
-        attended = (dq_ref[h] * inverse).astype(BF)
-        att_ref[:, cols] = attended
-        row_dot = jnp.sum(do_ref[:, cols].astype(F32) * attended.astype(F32), axis=1, keepdims=True)
-        row_dot_ref[h] = jnp.broadcast_to(row_dot, (rows, head))
-    dq_ref[...] = jnp.zeros(dq_ref.shape, F32)
-    lax.fori_loop(0, live, grad_tile, 0)
-    lax.fori_loop(live, 2, zero_tile, 0)
+        parts[0] = jnp.zeros(parts.shape[1:], BF)
+        on_rows(0, rows, [])
+
+    @pl.when(live == 1)
+    def _():
+        on_rows(0, rows, [near])
+
+    @pl.when((live == 2) & low_half)
+    def _():
+        on_rows(0, half, [near, far])
+        on_rows(half, half, [])
+
+    @pl.when((live == 2) & jnp.logical_not(low_half))
+    def _():
+        parts[1] = jnp.zeros(parts.shape[1:], BF)
+        on_rows(0, rows, [near, (1, half, half)])
+
     for _, part, at in slots:
-        part[pl.ds(0, rows), :] = key_parts[pl.ds(at, rows), :]
-        part[pl.ds(rows, rows), :] = value_parts[pl.ds(at, rows), :]
+        part[...] = parts[at]
 
 
 def second_back_kernel(
@@ -349,8 +347,7 @@
         24,
         [like_q] + [state] * 5 + [part] * 2,
         (place, first, q, do, qt, dot_, starts, top, total, out, mixed, swapped),
-        [pltpu.VMEM((2 * rows, head), BF)] * 4
-        + [pltpu.VMEM((state.shape[0], 2, rows, rows), F32), pltpu.VMEM(state.shape, F32)],
+        [pltpu.VMEM((2, 2 * rows, head), BF)] * 2,
     )
 
 

time: 66.1 us -> 64.4 us (0.974)
  the two profiles are of different devices: /device:TPU:358 before, /device:TPU:102 now
where the time goes in v10:
time: 64.4 us; the launch traced here: 64 us
  blocking collectives  20 us (31%)
  starting transfers between devices  18.3 us (28%)
  waiting for transfers between devices  11 us (17%)
  Pallas kernels  8.75 us (14%)
  local copies, waits for them, and re-layouts  5.11 us (8%)
  between operations  0.8 us (1%)
    ppermute x6, starting transfers between devices, moved(): return lax.ppermute(value, 'ctx', pairs)  18.3 us
    ppermute x6, waiting for transfers between devices, moved(): return lax.ppermute(value, 'ctx', pairs)  11 us
    all_to_all x1, blocking collectives, head_sum(): theirs = lax.all_to_all(pieces, 'head', split_axis=0, concat_axis=0)  10.9 us
    all_to_all x1, blocking collectives, head_sum(): lax.all_to_all(mine, 'head', split_axis=0, concat_axis=0)  9.07 us
    pallas_call x7, Pallas kernels, on_core(): pl.pallas_call(kernel, out_shape=tuple(outs), in_specs=[SMEM if x.ndim ==...  8.43 us
    unnamed x14, local copies, waits for them, and re-layouts  4.36 us
  transfers between devices with their start and end apart: 6, of which 3 were waited for; matrix products, arithmetic and copies ran while one was open for 0% of the time, Pallas kernels for 8%

profile of v10, /device:TPU:102, one launch (start us, length us, event | category | flops | bytes accessed | tf_op | source)
XLA Modules:
  0.0 64.0 jit_solution(12341549831630163020)
XLA Ops:
  0.6 0.0 copy-start
  0.6 0.9 %copy-done = bf16[512,128]{1,0:T(8,128)(2,1)S(1)} copy-done((bf16[512,128]{1,0:T(8,128)(2,1)S(1)}, bf16[512,128]{1,0:T(8,128)(2,1)}, u32[]{:S(2)}) %copy-start) | copy-done | bytes 131096
  1.5 0.0 copy-start.1
  1.5 0.9 %copy-done.1 = bf16[512,128]{1,0:T(8,128)(2,1)S(1)} copy-done((bf16[512,128]{1,0:T(8,128)(2,1)S(1)}, bf16[512,128]{1,0:T(8,128)(2,1)}, u32[]{:S(2)}) %copy-start.1) | copy-done | bytes 131096
  2.4 0.3 pack.1.own_ref
  2.8 5.0 %collective-permute-start = (bf16[1024,128]{1,0:T(8,128)(2,1)S(1)}, bf16[1024,128]{1,0:T(8,128)(2,1)S(1)}, u32[]{:S(2)}, u32[]{:S(2)}) collective-permute-start(bf16[1024,128]{1,0:T(8,128)(2,1)S(1)} %pack.1.own_ref), channel_id=1, source_target_pairs={{0,8},{4,12},{8,16},{12,20},{16,24},{20,28},{24,32},{28,36},{32,40... | collective-permute-start | bytes 786440 | tf_op jit(solution)/shard_map/ppermute | solution.py:405
  7.7 1.9 %collective-permute-start.1 = (bf16[1024,128]{1,0:T(8,128)(2,1)S(1)}, bf16[1024,128]{1,0:T(8,128)(2,1)S(1)}, u32[]{:S(2)}, u32[]{:S(2)}) collective-permute-start(bf16[1024,128]{1,0:T(8,128)(2,1)S(1)} %pack.1.own_ref), channel_id=1, source_target_pairs={{0,4},{4,16},{8,12},{12,24},{16,20},{20,32},{24,28},{28,40},{32,36... | collective-permute-start | bytes 786440 | tf_op jit(solution)/shard_map/ppermute | solution.py:405
  9.7 0.0 copy-start.2
  9.7 0.9 %copy-done.2 = bf16[512,256]{1,0:T(8,128)(2,1)S(1)} copy-done((bf16[512,256]{1,0:T(8,128)(2,1)S(1)}, bf16[512,256]{1,0:T(8,128)(2,1)}, u32[]{:S(2)}) %copy-start.2) | copy-done | bytes 262168
  10.6 0.0 copy-start.4
  10.6 0.9 %copy-done.4 = bf16[512,256]{1,0:T(8,128)(2,1)S(1)} copy-done((bf16[512,256]{1,0:T(8,128)(2,1)S(1)}, bf16[512,256]{1,0:T(8,128)(2,1)}, u32[]{:S(2)}) %copy-start.4) | copy-done | bytes 262168
  11.6 0.0 copy-start.6
  11.6 0.7 %copy-done.6 = s32[128]{0:T(128)S(1)} copy-done((s32[128]{0:T(128)S(1)}, s32[128]{0:T(128)}, u32[]{:S(2)}) %copy-start.6) | copy-done | bytes 536
  12.2 1.2 %diagonal.1 = (s32[1]{0:T(128)}, s32[512,128]{1,0:T(8,128)S(1)}, f32[2,512,128]{2,1,0:T(8,128)S(1)}, f32[2,512,128]{2,1,0:T(8,128)S(1)}, f32[2,512,128]{2,1,0:T(...) custom-call(s32[1]{0:T(128)} %bitcast.place_ref, s32[1,128]{1,0:T(1,128)S(1)} %bitcast.6, ...), custom_call_target="tpu_custom_call" | custom-call | flops 1200000000 | bytes 2097152 | tf_op jit(solution)/shard_map/diagonal/pallas_call | solution.py:302
  13.4 2.1 %collective-permute-done.block_ref = bf16[1024,128]{1,0:T(8,128)(2,1)S(1)} collective-permute-done((bf16[1024,128]{1,0:T(8,128)(2,1)S(1)}, bf16[1024,128]{1,0:T(8,128)(2,1)S(1)}, u32[]{:S(2)}, u32[]{:S(2)}) %collective-permute-start) | collective-permute-done | bytes 262176 | tf_op jit(solution)/shard_map/ppermute | solution.py:405
  15.5 2.3 %collective-permute-start.2 = (bf16[1024,128]{1,0:T(8,128)(2,1)S(1)}, bf16[1024,128]{1,0:T(8,128)(2,1)S(1)}, u32[]{:S(2)}, u32[]{:S(2)}) collective-permute-start(bf16[1024,128]{1,0:T(8,128)(2,1)S(1)} %collective-permute-done.block_ref), channel_id=1, source_target_pairs={{0,4},{4,0},{8,12},{12,8},{16,20},{20,16},{24,28},{28,24},{32,36},... | collective-permute-start | bytes 786440 | tf_op jit(solution)/shard_map/ppermute | solution.py:405
  17.9 0.0 copy-start.3
  17.9 0.0 copy-start.5
  17.9 0.8 %second.1 = (f32[2,512,128]{2,1,0:T(8,128)S(1)}, f32[2,512,128]{2,1,0:T(8,128)S(1)}, f32[2,512,128]{2,1,0:T(8,128)S(1)}, f32[2,512,512]{2,1,0:T(8,128)S(1)}) custom-call(s32[1]{0:T(128)} %get-tuple-element.34.first_ref, bf16[512,256]{1,0:T(8,128)(2,1)S(1)} %copy-done.2, s32[512,128]{1,0:T(8,128)S(1)} %get-tuple-element.32.starts_ref, ...), custom_call_target="tpu_custom_call" | custom-call | flops 1200000000 | bytes 2097152 | tf_op jit(solution)/shard_map/second/pallas_call | solution.py:302
  18.7 0.0 collective-permute-done.1.mixed_ref
  18.7 0.3 collective-permute-done.2.swapped_ref
  19.0 0.0 copy-done.3
  19.0 0.0 copy-done.5
  19.0 3.3 %far.1 = (bf16[512,256]{1,0:T(8,128)(2,1)S(1)}, f32[2,512,128]{2,1,0:T(8,128)S(1)}, f32[2,512,128]{2,1,0:T(8,128)S(1)}, f32[2,512,128]{2,1,0:T(8,128)S(1)}, f32[...) custom-call(s32[1]{0:T(128)} %bitcast.place_ref, ...), custom_call_target="tpu_custom_call" | custom-call | flops 3000000000 | bytes 2097152 | tf_op jit(solution)/shard_map/far/pallas_call | solution.py:302
  22.3 2.8 %collective-permute-start.3 = (bf16[1024,128]{1,0:T(8,128)(2,1)S(1)}, bf16[1024,128]{1,0:T(8,128)(2,1)S(1)}, u32[]{:S(2)}, u32[]{:S(2)}) collective-permute-start(bf16[1024,128]{1,0:T(8,128)(2,1)S(1)} %get-tuple-element.54), channel_id=1, source_target_pairs={{0,4},{4,0},{8,12},{12,8},{16,20},{20,16},{24,28},{28,24},{32,36},... | collective-permute-start | bytes 786440 | tf_op jit(solution)/shard_map/ppermute | solution.py:405
  25.1 2.6 %collective-permute-start.5 = (bf16[1024,128]{1,0:T(8,128)(2,1)S(1)}, bf16[1024,128]{1,0:T(8,128)(2,1)S(1)}, u32[]{:S(2)}, u32[]{:S(2)}) collective-permute-start(bf16[1024,128]{1,0:T(8,128)(2,1)S(1)} %get-tuple-element.55), channel_id=1, source_target_pairs={{4,0},{16,4},{12,8},{24,12},{20,16},{32,20},{28,24},{40,28},{36,32... | collective-permute-start | bytes 786440 | tf_op jit(solution)/shard_map/ppermute | solution.py:405
  27.7 0.7 %second_back.1 = (f32[2,512,128]{2,1,0:T(8,128)S(1)}, bf16[1024,128]{1,0:T(8,128)(2,1)S(1)}) custom-call(s32[1]{0:T(128)} %get-tuple-element.34.first_ref, bf16[512,256]{1,0:T(8,128)(2,1)S(1)} %copy-done.5, bf16[2,128,512]{2,1,0:T(8,128)(2,1)S(1)} %get-tuple-element.30.qt_ref, bf16[2,128,512]{2,1,0:T(8,128)(2,1)S(1)} %get-tuple-element.31.dot_ref, ...), custom_call_target="tpu_custom_call" | custom-call | flops 1500000000 | bytes 2097152 | tf_op jit(solution)/shard_map/second_back/pallas_call | solution.py:302
  28.4 0.0 collective-permute-done.3.refs_1_
  28.4 0.1 sum.2
  28.5 3.7 %collective-permute-start.4 = (bf16[1024,128]{1,0:T(8,128)(2,1)S(1)}, bf16[1024,128]{1,0:T(8,128)(2,1)S(1)}, u32[]{:S(2)}, u32[]{:S(2)}) collective-permute-start(bf16[1024,128]{1,0:T(8,128)(2,1)S(1)} %sum.2), channel_id=1, source_target_pairs={{8,0},{12,4},{16,8},{20,12},{24,16},{28,20},{32,24},{36,28},{40,32... | collective-permute-start | bytes 786440 | tf_op jit(solution)/shard_map/ppermute | solution.py:405
  32.2 2.3 %own.1 = (bf16[512,256]{1,0:T(8,128)(2,1)}, bf16[1024,128]{1,0:T(8,128)(2,1)S(1)}, bf16[512,256]{1,0:T(8,128)(2,1)}) custom-call(bf16[512,256]{1,0:T(8,128)(2,1)S(1)} %copy-done.3, bf16[512,256]{1,0:T(8,128)(2,1)S(1)} %copy-done.5, bf16[2,128,512]{2,1,0:T(8,128)(2,1)S(1)} %get-tuple-element.30.qt_ref, bf16[2,128,512]{2,1,0:T(8,128)(2,1)S(1)} %get-tuple-element.31.dot_ref, ...), custom_call_target="tpu_custom_call" | custom-call | flops 2500000000 | bytes 2097152 | tf_op jit(solution)/shard_map/own/pallas_call | solution.py:302
  34.5 0.0 collective-permute-done.5.refs_2_
  34.5 8.6 %collective-permute-done.4.refs_1_ = bf16[1024,128]{1,0:T(8,128)(2,1)S(1)} collective-permute-done((bf16[1024,128]{1,0:T(8,128)(2,1)S(1)}, bf16[1024,128]{1,0:T(8,128)(2,1)S(1)}, u32[]{:S(2)}, u32[]{:S(2)}) %collective-permute-start.4) | collective-permute-done | bytes 262176 | tf_op jit(solution)/shard_map/ppermute | solution.py:405
  43.1 0.1 sum.3
  43.2 10.9 %all_to_all.10 = bf16[4,256,128]{2,1,0:T(8,128)(2,1)S(1)} all-to-all(bf16[4,256,128]{2,1,0:T(8,128)(2,1)S(1)} %bitcast.5), channel_id=1, replica_groups=mesh['ctx'=128,'head'=4] {'head'}, dimensions={0} | all-to-all | bytes 524288 | tf_op jit(solution)/shard_map/all_to_all | solution.py:398
  54.2 9.1 %all_to_all.11 = bf16[4,256,128]{2,1,0:T(8,128)(2,1)S(1)} all-to-all(bf16[4,256,128]{2,1,0:T(8,128)(2,1)S(1)} %broadcast_in_dim.2), channel_id=1, replica_groups=mesh['ctx'=128,'head'=4] {'head'}, dimensions={0} | all-to-all | bytes 524288 | tf_op jit(solution)/shard_map/all_to_all | solution.py:401
  63.3 0.7 %fusion = (bf16[2,256,128]{2,1,0:T(8,128)(2,1)}, bf16[2,256,128]{2,1,0:T(8,128)(2,1)}) fusion(bf16[4,256,128]{2,1,0:T(8,128)(2,1)S(1)} %all_to_all.11), kind=kLoop, calls=%fused_computation | loop fusion | bytes 524288 | tf_op jit(solution)/shard_map/slice | solution.py:440
  (2 shorter events, 0.1 us)
Async XLA Ops:
  0.6 0.9 %copy-start = (bf16[512,128]{1,0:T(8,128)(2,1)S(1)}, bf16[512,128]{1,0:T(8,128)(2,1)}, u32[]{:S(2)}) copy-start(bf16[512,128]{1,0:T(8,128)(2,1)} %key_ref.1) | copy-start | bytes 393220
  1.5 0.9 %copy-start.1 = (bf16[512,128]{1,0:T(8,128)(2,1)S(1)}, bf16[512,128]{1,0:T(8,128)(2,1)}, u32[]{:S(2)}) copy-start(bf16[512,128]{1,0:T(8,128)(2,1)} %value_ref.1) | copy-start | bytes 393220
  2.8 12.7 %collective-permute-start = (bf16[1024,128]{1,0:T(8,128)(2,1)S(1)}, bf16[1024,128]{1,0:T(8,128)(2,1)S(1)}, u32[]{:S(2)}, u32[]{:S(2)}) collective-permute-start(bf16[1024,128]{1,0:T(8,128)(2,1)S(1)} %pack.1.own_ref), channel_id=1, source_target_pairs={{0,8},{4,12},{8,16},{12,20},{16,24},{20,28},{24,32},{28,36},{32,40... | collective-permute-start | bytes 786440 | tf_op jit(solution)/shard_map/ppermute | solution.py:405
  7.7 11.0 %collective-permute-start.1 = (bf16[1024,128]{1,0:T(8,128)(2,1)S(1)}, bf16[1024,128]{1,0:T(8,128)(2,1)S(1)}, u32[]{:S(2)}, u32[]{:S(2)}) collective-permute-start(bf16[1024,128]{1,0:T(8,128)(2,1)S(1)} %pack.1.own_ref), channel_id=1, source_target_pairs={{0,4},{4,16},{8,12},{12,24},{16,20},{20,32},{24,28},{28,40},{32,36... | collective-permute-start | bytes 786440 | tf_op jit(solution)/shard_map/ppermute | solution.py:405
  9.7 1.0 %copy-start.2 = (bf16[512,256]{1,0:T(8,128)(2,1)S(1)}, bf16[512,256]{1,0:T(8,128)(2,1)}, u32[]{:S(2)}) copy-start(bf16[512,256]{1,0:T(8,128)(2,1)} %q_ref.7) | copy-start | bytes 786436
  10.6 0.9 %copy-start.4 = (bf16[512,256]{1,0:T(8,128)(2,1)S(1)}, bf16[512,256]{1,0:T(8,128)(2,1)}, u32[]{:S(2)}) copy-start(bf16[512,256]{1,0:T(8,128)(2,1)} %do_ref.7) | copy-start | bytes 786436
  11.6 0.7 %copy-start.6 = (s32[128]{0:T(128)S(1)}, s32[128]{0:T(128)}, u32[]{:S(2)}) copy-start(s32[128]{0:T(128)} %param.9) | copy-start | bytes 1540
  15.5 3.5 %collective-permute-start.2 = (bf16[1024,128]{1,0:T(8,128)(2,1)S(1)}, bf16[1024,128]{1,0:T(8,128)(2,1)S(1)}, u32[]{:S(2)}, u32[]{:S(2)}) collective-permute-start(bf16[1024,128]{1,0:T(8,128)(2,1)S(1)} %collective-permute-done.block_ref), channel_id=1, source_target_pairs={{0,4},{4,0},{8,12},{12,8},{16,20},{20,16},{24,28},{28,24},{32,36},... | collective-permute-start | bytes 786440 | tf_op jit(solution)/shard_map/ppermute | solution.py:405
  17.9 1.1 %copy-start.3 = (bf16[512,256]{1,0:T(8,128)(2,1)S(1)}, bf16[512,256]{1,0:T(8,128)(2,1)}, u32[]{:S(2)}) copy-start(bf16[512,256]{1,0:T(8,128)(2,1)} %q_ref.7) | copy-start | bytes 786436
  17.9 1.1 %copy-start.5 = (bf16[512,256]{1,0:T(8,128)(2,1)S(1)}, bf16[512,256]{1,0:T(8,128)(2,1)}, u32[]{:S(2)}) copy-start(bf16[512,256]{1,0:T(8,128)(2,1)} %do_ref.7) | copy-start | bytes 786436
  22.3 6.1 %collective-permute-start.3 = (bf16[1024,128]{1,0:T(8,128)(2,1)S(1)}, bf16[1024,128]{1,0:T(8,128)(2,1)S(1)}, u32[]{:S(2)}, u32[]{:S(2)}) collective-permute-start(bf16[1024,128]{1,0:T(8,128)(2,1)S(1)} %get-tuple-element.54), channel_id=1, source_target_pairs={{0,4},{4,0},{8,12},{12,8},{16,20},{20,16},{24,28},{28,24},{32,36},... | collective-permute-start | bytes 786440 | tf_op jit(solution)/shard_map/ppermute | solution.py:405
  25.1 9.4 %collective-permute-start.5 = (bf16[1024,128]{1,0:T(8,128)(2,1)S(1)}, bf16[1024,128]{1,0:T(8,128)(2,1)S(1)}, u32[]{:S(2)}, u32[]{:S(2)}) collective-permute-start(bf16[1024,128]{1,0:T(8,128)(2,1)S(1)} %get-tuple-element.55), channel_id=1, source_target_pairs={{4,0},{16,4},{12,8},{24,12},{20,16},{32,20},{28,24},{40,28},{36,32... | collective-permute-start | bytes 786440 | tf_op jit(solution)/shard_map/ppermute | solution.py:405
  28.5 14.6 %collective-permute-start.4 = (bf16[1024,128]{1,0:T(8,128)(2,1)S(1)}, bf16[1024,128]{1,0:T(8,128)(2,1)S(1)}, u32[]{:S(2)}, u32[]{:S(2)}) collective-permute-start(bf16[1024,128]{1,0:T(8,128)(2,1)S(1)} %sum.2), channel_id=1, source_target_pairs={{8,0},{12,4},{16,8},{20,12},{24,16},{28,20},{32,24},{36,28},{40,32... | collective-permute-start | bytes 786440 | tf_op jit(solution)/shard_map/ppermute | solution.py:405

commit v11 on v10

--- a/solution.py
+++ b/solution.py
@@ -57,6 +57,7 @@
     start = (doc_start - begin).astype(jnp.int32)
     starts_ref[...] = jnp.broadcast_to(start, starts_ref.shape)
     first_ref[0] = jnp.min(start) + lead
+    first_ref[1] = jnp.sum(jnp.where(start < 0, 1, 0))
 
     column = lax.broadcasted_iota(jnp.int32, (rows, rows), 1)
     row = lax.broadcasted_iota(jnp.int32, (rows, rows), 0)
@@ -85,29 +86,46 @@
     to_exp2 = exp2_scale(head)
     place = SPAN - 2
     live = lowest_block(first_ref, rows) <= place
-
-    @pl.when(live)
-    def _():
+    reached = first_ref[1]
+    half = rows // 2
+
+    def on_rows(n):
+        row = pl.ds(0, n)
         keys = block_ref[pl.ds(0, rows), :]
         values = block_ref[pl.ds(rows, rows), :]
-        column = lax.broadcasted_iota(jnp.int32, (rows, rows), 1)
-        allowed = column >= wide(starts_ref[...] + (SPAN - place) * rows, rows)
+        column = lax.broadcasted_iota(jnp.int32, (n, rows), 1)
+        allowed = column >= wide(starts_ref[row, :] + (SPAN - place) * rows, rows)
         for h in range(heads):
-            s = jnp.where(allowed, dot_nt(q_ref[:, pl.ds(h * head, head)], keys), -jnp.inf)
-            top0 = top0_ref[h]
+            s = jnp.where(allowed, dot_nt(q_ref[row, pl.ds(h * head, head)], keys), -jnp.inf)
+            top0 = top0_ref[h, row, :]
             top = across_lanes(jnp.maximum(folded(s, head, jnp.maximum), top0), jnp.max, top0)
             e = jnp.exp2((s - wide(top, rows)) * to_exp2)
             kept = jnp.exp2((top0 - top) * to_exp2)
-            tile_ref[h] = e
-            top_ref[h] = top
-            total_ref[h] = total0_ref[h] * kept + across_lanes(folded(e, head, jnp.add), jnp.sum, top)
-            out_ref[h] = out0_ref[h] * kept + dot_nn(e.astype(BF), values)
+            tile_ref[h, row, :] = e
+            top_ref[h, row, :] = top
+            sums = across_lanes(folded(e, head, jnp.add), jnp.sum, top)
+            total_ref[h, row, :] = total0_ref[h, row, :] * kept + sums
+            out_ref[h, row, :] = out0_ref[h, row, :] * kept + dot_nn(e.astype(BF), values)
+
+    def keep_rows(r0):
+        row = pl.ds(r0, rows - r0)
+        for h in range(heads):
+            top_ref[h, row, :] = top0_ref[h, row, :]
+            total_ref[h, row, :] = total0_ref[h, row, :]
+            out_ref[h, row, :] = out0_ref[h, row, :]
+
+    @pl.when(live & (reached <= half))
+    def _():
+        on_rows(half)
+        keep_rows(half)
+
+    @pl.when(live & (reached > half))
+    def _():
+        on_rows(rows)
 
     @pl.when(jnp.logical_not(live))
     def _():
-        top_ref[...] = top0_ref[...]
-        total_ref[...] = total0_ref[...]
-        out_ref[...] = out0_ref[...]
+        keep_rows(0)
 
 
 def far_kernel(
@@ -186,6 +204,15 @@
         def _():
             window[at] = block[...]
 
+    half, quarter = rows // 2, rows // 4
+    near, far = (0, 0, rows), (1, 0, rows)
+    reached = first_ref[1]
+
+    for block, _, at in slots:
+        @pl.when(at < live)
+        def _():
+            window[at] = block[...]
+
     half = rows // 2
     near, far = (0, 0, rows), (1, 0, rows)
     low_half = first_ref[0] < half
@@ -199,19 +226,30 @@
         parts[0] = jnp.zeros(parts.shape[1:], BF)
         on_rows(0, rows, [])
 
-    @pl.when(live == 1)
+    @pl.when((live == 1) & (reached <= half))
+    def _():
+        on_rows(0, half, [near])
+        on_rows(half, half, [])
+
+    @pl.when((live == 1) & (reached > half))
     def _():
         on_rows(0, rows, [near])
 
-    @pl.when((live == 2) & low_half)
+    @pl.when((live == 2) & (reached <= half))
     def _():
         on_rows(0, half, [near, far])
         on_rows(half, half, [])
 
-    @pl.when((live == 2) & jnp.logical_not(low_half))
+    @pl.when((live == 2) & (reached > half) & (reached <= rows - quarter))
     def _():
         parts[1] = jnp.zeros(parts.shape[1:], BF)
-        on_rows(0, rows, [near, (1, half, half)])
+        on_rows(0, rows - quarter, [near, (1, half, half)])
+        on_rows(rows - quarter, quarter, [])
+
+    @pl.when((live == 2) & (reached > rows - quarter))
+    def _():
+        parts[1] = jnp.zeros(parts.shape[1:], BF)
+        on_rows(0, rows, [near, (1, rows - quarter, quarter)])
 
     for _, part, at in slots:
         part[...] = parts[at]
@@ -224,22 +262,34 @@
     heads, rows, head = far_ref.shape
     scale = score_scale(head)
     live = lowest_block(first_ref, rows) <= SPAN - 2
-
-    @pl.when(live)
-    def _():
+    reached = first_ref[1]
+    half = rows // 2
+
+    def on_rows(n):
+        row = pl.ds(0, n)
         keys = block_ref[pl.ds(0, rows), :]
         values = block_ref[pl.ds(rows, rows), :]
         dv = jnp.zeros((head, rows), F32)
         dk = jnp.zeros((head, rows), F32)
         for h in range(heads):
-            dw = dot_nt(do_ref[:, pl.ds(h * head, head)], values)
-            w = tile_ref[h] * wide(factor_ref[h], rows)
-            ds = (w * (dw - wide(row_dot_ref[h], rows))).astype(BF)
-            dv = dv + dot_nn(dot_ref[h], w.astype(BF))
-            dk = dk + dot_nn(qt_ref[h], ds)
-            dq_ref[h] = far_ref[h] + dot_nn(ds, keys)
+            dw = dot_nt(do_ref[row, pl.ds(h * head, head)], values)
+            w = tile_ref[h, row, :] * wide(factor_ref[h, row, :], rows)
+            ds = (w * (dw - wide(row_dot_ref[h, row, :], rows))).astype(BF)
+            dv = dv + dot_nn(dot_ref[h, :, row], w.astype(BF))
+            dk = dk + dot_nn(qt_ref[h, :, row], ds)
+            dq_ref[h, row, :] = far_ref[h, row, :] + dot_nn(ds, keys)
         part_ref[pl.ds(0, rows), :] = (dk * scale).T.astype(BF)
         part_ref[pl.ds(rows, rows), :] = dv.T.astype(BF)
+
+    @pl.when(live & (reached <= half))
+    def _():
+        on_rows(half)
+        for h in range(heads):
+            dq_ref[h, pl.ds(half, half), :] = far_ref[h, pl.ds(half, half), :]
+
+    @pl.when(live & (reached > half))
+    def _():
+        on_rows(rows)
 
     @pl.when(jnp.logical_not(live))
     def _():
@@ -327,7 +377,7 @@
 def attention_before(place, lengths, q, do, own):
     state, turned, _, _, _ = sizes(q, own)
     starts = shape(state.shape[1:], jnp.int32)
-    outs = [shape((1,), jnp.int32), starts, state, state, state, turned, turned]
+    outs = [shape((2,), jnp.int32), starts, state, state, state, turned, turned]
     return on_core(diagonal_kernel, "diagonal", 1200, 20, outs, (place, lengths, q, do, own))
 
 

time: 64.4 us -> 63.9 us (level)
  the two profiles are of different devices: /device:TPU:102 before, /device:TPU:230 now
where the time goes in v11:
time: 63.9 us; the launch traced here: 63.1 us
  blocking collectives  20 us (31%)
  starting transfers between devices  17.6 us (28%)
  waiting for transfers between devices  10.5 us (16%)
  Pallas kernels  9.08 us (14%)
  local copies, waits for them, and re-layouts  5.11 us (8%)
  between operations  0.82 us (1%)
    ppermute x6, starting transfers between devices, moved(): return lax.ppermute(value, 'ctx', pairs)  17.6 us
    all_to_all x1, blocking collectives, head_sum(): theirs = lax.all_to_all(pieces, 'head', split_axis=0, concat_axis=0)  10.9 us
    ppermute x6, waiting for transfers between devices, moved(): return lax.ppermute(value, 'ctx', pairs)  10.5 us
    all_to_all x1, blocking collectives, head_sum(): lax.all_to_all(mine, 'head', split_axis=0, concat_axis=0)  9.07 us
    pallas_call x7, Pallas kernels, on_core(): pl.pallas_call(kernel, out_shape=tuple(outs), in_specs=[SMEM if x.ndim ==...  8.76 us
    unnamed x14, local copies, waits for them, and re-layouts  4.36 us
  transfers between devices with their start and end apart: 6, of which 2 were waited for; matrix products, arithmetic and copies ran while one was open for 0% of the time, Pallas kernels for 10%

profile of v11, /device:TPU:230, one launch (start us, length us, event | category | flops | bytes accessed | tf_op | source)
XLA Modules:
  0.0 63.1 jit_solution(3690563033079647173)
XLA Ops:
  0.6 0.0 copy-start
  0.6 0.9 %copy-done = bf16[512,128]{1,0:T(8,128)(2,1)S(1)} copy-done((bf16[512,128]{1,0:T(8,128)(2,1)S(1)}, bf16[512,128]{1,0:T(8,128)(2,1)}, u32[]{:S(2)}) %copy-start) | copy-done | bytes 131096
  1.5 0.0 copy-start.1
  1.5 0.9 %copy-done.1 = bf16[512,128]{1,0:T(8,128)(2,1)S(1)} copy-done((bf16[512,128]{1,0:T(8,128)(2,1)S(1)}, bf16[512,128]{1,0:T(8,128)(2,1)}, u32[]{:S(2)}) %copy-start.1) | copy-done | bytes 131096
  2.4 0.3 pack.1.own_ref
  2.8 5.0 %collective-permute-start = (bf16[1024,128]{1,0:T(8,128)(2,1)S(1)}, bf16[1024,128]{1,0:T(8,128)(2,1)S(1)}, u32[]{:S(2)}, u32[]{:S(2)}) collective-permute-start(bf16[1024,128]{1,0:T(8,128)(2,1)S(1)} %pack.1.own_ref), channel_id=1, source_target_pairs={{0,8},{4,12},{8,16},{12,20},{16,24},{20,28},{24,32},{28,36},{32,40... | collective-permute-start | bytes 786440 | tf_op jit(solution)/shard_map/ppermute | solution.py:455
  7.7 1.9 %collective-permute-start.1 = (bf16[1024,128]{1,0:T(8,128)(2,1)S(1)}, bf16[1024,128]{1,0:T(8,128)(2,1)S(1)}, u32[]{:S(2)}, u32[]{:S(2)}) collective-permute-start(bf16[1024,128]{1,0:T(8,128)(2,1)S(1)} %pack.1.own_ref), channel_id=1, source_target_pairs={{0,4},{4,16},{8,12},{12,24},{16,20},{20,32},{24,28},{28,40},{32,36... | collective-permute-start | bytes 786440 | tf_op jit(solution)/shard_map/ppermute | solution.py:455
  9.7 0.0 copy-start.2
  9.7 0.9 %copy-done.2 = bf16[512,256]{1,0:T(8,128)(2,1)S(1)} copy-done((bf16[512,256]{1,0:T(8,128)(2,1)S(1)}, bf16[512,256]{1,0:T(8,128)(2,1)}, u32[]{:S(2)}) %copy-start.2) | copy-done | bytes 262168
  10.6 0.0 copy-start.4
  10.6 0.9 %copy-done.4 = bf16[512,256]{1,0:T(8,128)(2,1)S(1)} copy-done((bf16[512,256]{1,0:T(8,128)(2,1)S(1)}, bf16[512,256]{1,0:T(8,128)(2,1)}, u32[]{:S(2)}) %copy-start.4) | copy-done | bytes 262168
  11.6 0.0 copy-start.6
  11.6 0.7 %copy-done.6 = s32[128]{0:T(128)S(1)} copy-done((s32[128]{0:T(128)S(1)}, s32[128]{0:T(128)}, u32[]{:S(2)}) %copy-start.6) | copy-done | bytes 536
  12.2 1.2 %diagonal.1 = (s32[2]{0:T(128)S(1)}, s32[512,128]{1,0:T(8,128)S(1)}, f32[2,512,128]{2,1,0:T(8,128)S(1)}, f32[2,512,128]{2,1,0:T(8,128)S(1)}, f32[2,512,128]{2,1,...) custom-call(s32[1]{0:T(128)} %bitcast.place_ref, s32[1,128]{1,0:T(1,128)S(1)} %bitcast.6, ...), custom_call_target="tpu_custom_call" | custom-call | flops 1200000000 | bytes 2097152 | tf_op jit(solution)/shard_map/diagonal/pallas_call | solution.py:352
  13.4 2.1 %collective-permute-done.block_ref = bf16[1024,128]{1,0:T(8,128)(2,1)S(1)} collective-permute-done((bf16[1024,128]{1,0:T(8,128)(2,1)S(1)}, bf16[1024,128]{1,0:T(8,128)(2,1)S(1)}, u32[]{:S(2)}, u32[]{:S(2)}) %collective-permute-start) | collective-permute-done | bytes 262176 | tf_op jit(solution)/shard_map/ppermute | solution.py:455
  15.5 2.4 %collective-permute-start.2 = (bf16[1024,128]{1,0:T(8,128)(2,1)S(1)}, bf16[1024,128]{1,0:T(8,128)(2,1)S(1)}, u32[]{:S(2)}, u32[]{:S(2)}) collective-permute-start(bf16[1024,128]{1,0:T(8,128)(2,1)S(1)} %collective-permute-done.block_ref), channel_id=1, source_target_pairs={{0,4},{4,0},{8,12},{12,8},{16,20},{20,16},{24,28},{28,24},{32,36},... | collective-permute-start | bytes 786440 | tf_op jit(solution)/shard_map/ppermute | solution.py:455
  17.9 0.0 copy-start.3
  17.9 0.0 copy-start.5
  17.9 1.4 %second.1 = (f32[2,512,128]{2,1,0:T(8,128)S(1)}, f32[2,512,128]{2,1,0:T(8,128)S(1)}, f32[2,512,128]{2,1,0:T(8,128)S(1)}, f32[2,512,512]{2,1,0:T(8,128)S(1)}) custom-call(s32[2]{0:T(128)S(1)} %get-tuple-element.34.first_ref, bf16[512,256]{1,0:T(8,128)(2,1)S(1)} %copy-done.2, s32[512,128]{1,0:T(8,128)S(1)} %get-tuple-element.32.starts_ref, ...), custom_call_target="tpu_custom_call" | custom-call | flops 1200000000 | bytes 2097152 | tf_op jit(solution)/shard_map/second/pallas_call | solution.py:352
  19.3 0.0 collective-permute-done.1.mixed_ref
  19.3 0.0 collective-permute-done.2.swapped_ref
  19.3 0.0 copy-done.3
  19.3 0.0 copy-done.5
  19.3 2.4 %far.1 = (bf16[512,256]{1,0:T(8,128)(2,1)S(1)}, f32[2,512,128]{2,1,0:T(8,128)S(1)}, f32[2,512,128]{2,1,0:T(8,128)S(1)}, f32[2,512,128]{2,1,0:T(8,128)S(1)}, f32[...) custom-call(s32[1]{0:T(128)} %bitcast.place_ref, ...), custom_call_target="tpu_custom_call" | custom-call | flops 3000000000 | bytes 2097152 | tf_op jit(solution)/shard_map/far/pallas_call | solution.py:352
  21.7 3.0 %collective-permute-start.3 = (bf16[1024,128]{1,0:T(8,128)(2,1)S(1)}, bf16[1024,128]{1,0:T(8,128)(2,1)S(1)}, u32[]{:S(2)}, u32[]{:S(2)}) collective-permute-start(bf16[1024,128]{1,0:T(8,128)(2,1)S(1)} %get-tuple-element.54), channel_id=1, source_target_pairs={{0,4},{4,0},{8,12},{12,8},{16,20},{20,16},{24,28},{28,24},{32,36},... | collective-permute-start | bytes 786440 | tf_op jit(solution)/shard_map/ppermute | solution.py:455
  24.7 3.1 %collective-permute-start.5 = (bf16[1024,128]{1,0:T(8,128)(2,1)S(1)}, bf16[1024,128]{1,0:T(8,128)(2,1)S(1)}, u32[]{:S(2)}, u32[]{:S(2)}) collective-permute-start(bf16[1024,128]{1,0:T(8,128)(2,1)S(1)} %get-tuple-element.55), channel_id=1, source_target_pairs={{4,0},{16,4},{12,8},{24,12},{20,16},{32,20},{28,24},{40,28},{36,32... | collective-permute-start | bytes 786440 | tf_op jit(solution)/shard_map/ppermute | solution.py:455
  27.8 1.4 %second_back.1 = (f32[2,512,128]{2,1,0:T(8,128)S(1)}, bf16[1024,128]{1,0:T(8,128)(2,1)S(1)}) custom-call(s32[2]{0:T(128)S(1)} %get-tuple-element.34.first_ref, bf16[512,256]{1,0:T(8,128)(2,1)S(1)} %copy-done.5, bf16[2,128,512]{2,1,0:T(8,128)(2,1)S(1)} %get-tuple-element.30.qt_ref, bf16[2,128,512]{2,1,0:T(8,128)(2,1)S(1)} %get-tuple-element.31.dot_ref, ...), custom_call_target="tpu_custom_call" | custom-call | flops 1500000000 | bytes 2097152 | tf_op jit(solution)/shard_map/second_back/pallas_call | solution.py:352
  29.2 0.0 collective-permute-done.3.refs_1_
  29.2 0.1 sum.2
  29.3 2.3 %collective-permute-start.4 = (bf16[1024,128]{1,0:T(8,128)(2,1)S(1)}, bf16[1024,128]{1,0:T(8,128)(2,1)S(1)}, u32[]{:S(2)}, u32[]{:S(2)}) collective-permute-start(bf16[1024,128]{1,0:T(8,128)(2,1)S(1)} %sum.2), channel_id=1, source_target_pairs={{8,0},{12,4},{16,8},{20,12},{24,16},{28,20},{32,24},{36,28},{40,32... | collective-permute-start | bytes 786440 | tf_op jit(solution)/shard_map/ppermute | solution.py:455
  31.5 2.3 %own.1 = (bf16[512,256]{1,0:T(8,128)(2,1)}, bf16[1024,128]{1,0:T(8,128)(2,1)S(1)}, bf16[512,256]{1,0:T(8,128)(2,1)}) custom-call(bf16[512,256]{1,0:T(8,128)(2,1)S(1)} %copy-done.3, bf16[512,256]{1,0:T(8,128)(2,1)S(1)} %copy-done.5, bf16[2,128,512]{2,1,0:T(8,128)(2,1)S(1)} %get-tuple-element.30.qt_ref, bf16[2,128,512]{2,1,0:T(8,128)(2,1)S(1)} %get-tuple-element.31.dot_ref, ...), custom_call_target="tpu_custom_call" | custom-call | flops 2500000000 | bytes 2097152 | tf_op jit(solution)/shard_map/own/pallas_call | solution.py:352
  33.8 0.0 collective-permute-done.5.refs_2_
  33.8 8.4 %collective-permute-done.4.refs_1_ = bf16[1024,128]{1,0:T(8,128)(2,1)S(1)} collective-permute-done((bf16[1024,128]{1,0:T(8,128)(2,1)S(1)}, bf16[1024,128]{1,0:T(8,128)(2,1)S(1)}, u32[]{:S(2)}, u32[]{:S(2)}) %collective-permute-start.4) | collective-permute-done | bytes 262176 | tf_op jit(solution)/shard_map/ppermute | solution.py:455
  42.2 0.1 sum.3
  42.3 10.9 %all_to_all.10 = bf16[4,256,128]{2,1,0:T(8,128)(2,1)S(1)} all-to-all(bf16[4,256,128]{2,1,0:T(8,128)(2,1)S(1)} %bitcast.5), channel_id=1, replica_groups=mesh['ctx'=128,'head'=4] {'head'}, dimensions={0} | all-to-all | bytes 524288 | tf_op jit(solution)/shard_map/all_to_all | solution.py:448
  53.3 9.1 %all_to_all.11 = bf16[4,256,128]{2,1,0:T(8,128)(2,1)S(1)} all-to-all(bf16[4,256,128]{2,1,0:T(8,128)(2,1)S(1)} %broadcast_in_dim.2), channel_id=1, replica_groups=mesh['ctx'=128,'head'=4] {'head'}, dimensions={0} | all-to-all | bytes 524288 | tf_op jit(solution)/shard_map/all_to_all | solution.py:451
  62.4 0.7 %fusion = (bf16[2,256,128]{2,1,0:T(8,128)(2,1)}, bf16[2,256,128]{2,1,0:T(8,128)(2,1)}) fusion(bf16[4,256,128]{2,1,0:T(8,128)(2,1)S(1)} %all_to_all.11), kind=kLoop, calls=%fused_computation | loop fusion | bytes 524288 | tf_op jit(solution)/shard_map/slice | solution.py:490
  (2 shorter events, 0.1 us)
Async XLA Ops:
  0.6 0.9 %copy-start = (bf16[512,128]{1,0:T(8,128)(2,1)S(1)}, bf16[512,128]{1,0:T(8,128)(2,1)}, u32[]{:S(2)}) copy-start(bf16[512,128]{1,0:T(8,128)(2,1)} %key_ref.1) | copy-start | bytes 393220
  1.5 0.9 %copy-start.1 = (bf16[512,128]{1,0:T(8,128)(2,1)S(1)}, bf16[512,128]{1,0:T(8,128)(2,1)}, u32[]{:S(2)}) copy-start(bf16[512,128]{1,0:T(8,128)(2,1)} %value_ref.1) | copy-start | bytes 393220
  2.8 12.7 %collective-permute-start = (bf16[1024,128]{1,0:T(8,128)(2,1)S(1)}, bf16[1024,128]{1,0:T(8,128)(2,1)S(1)}, u32[]{:S(2)}, u32[]{:S(2)}) collective-permute-start(bf16[1024,128]{1,0:T(8,128)(2,1)S(1)} %pack.1.own_ref), channel_id=1, source_target_pairs={{0,8},{4,12},{8,16},{12,20},{16,24},{20,28},{24,32},{28,36},{32,40... | collective-permute-start | bytes 786440 | tf_op jit(solution)/shard_map/ppermute | solution.py:455
  7.7 11.5 %collective-permute-start.1 = (bf16[1024,128]{1,0:T(8,128)(2,1)S(1)}, bf16[1024,128]{1,0:T(8,128)(2,1)S(1)}, u32[]{:S(2)}, u32[]{:S(2)}) collective-permute-start(bf16[1024,128]{1,0:T(8,128)(2,1)S(1)} %pack.1.own_ref), channel_id=1, source_target_pairs={{0,4},{4,16},{8,12},{12,24},{16,20},{20,32},{24,28},{28,40},{32,36... | collective-permute-start | bytes 786440 | tf_op jit(solution)/shard_map/ppermute | solution.py:455
  9.7 1.0 %copy-start.2 = (bf16[512,256]{1,0:T(8,128)(2,1)S(1)}, bf16[512,256]{1,0:T(8,128)(2,1)}, u32[]{:S(2)}) copy-start(bf16[512,256]{1,0:T(8,128)(2,1)} %q_ref.7) | copy-start | bytes 786436
  10.6 0.9 %copy-start.4 = (bf16[512,256]{1,0:T(8,128)(2,1)S(1)}, bf16[512,256]{1,0:T(8,128)(2,1)}, u32[]{:S(2)}) copy-start(bf16[512,256]{1,0:T(8,128)(2,1)} %do_ref.7) | copy-start | bytes 786436
  11.6 0.7 %copy-start.6 = (s32[128]{0:T(128)S(1)}, s32[128]{0:T(128)}, u32[]{:S(2)}) copy-start(s32[128]{0:T(128)} %param.9) | copy-start | bytes 1540
  15.5 3.8 %collective-permute-start.2 = (bf16[1024,128]{1,0:T(8,128)(2,1)S(1)}, bf16[1024,128]{1,0:T(8,128)(2,1)S(1)}, u32[]{:S(2)}, u32[]{:S(2)}) collective-permute-start(bf16[1024,128]{1,0:T(8,128)(2,1)S(1)} %collective-permute-done.block_ref), channel_id=1, source_target_pairs={{0,4},{4,0},{8,12},{12,8},{16,20},{20,16},{24,28},{28,24},{32,36},... | collective-permute-start | bytes 786440 | tf_op jit(solution)/shard_map/ppermute | solution.py:455
  17.9 1.4 %copy-start.3 = (bf16[512,256]{1,0:T(8,128)(2,1)S(1)}, bf16[512,256]{1,0:T(8,128)(2,1)}, u32[]{:S(2)}) copy-start(bf16[512,256]{1,0:T(8,128)(2,1)} %q_ref.7) | copy-start | bytes 786436
  17.9 1.4 %copy-start.5 = (bf16[512,256]{1,0:T(8,128)(2,1)S(1)}, bf16[512,256]{1,0:T(8,128)(2,1)}, u32[]{:S(2)}) copy-start(bf16[512,256]{1,0:T(8,128)(2,1)} %do_ref.7) | copy-start | bytes 786436
  21.7 7.5 %collective-permute-start.3 = (bf16[1024,128]{1,0:T(8,128)(2,1)S(1)}, bf16[1024,128]{1,0:T(8,128)(2,1)S(1)}, u32[]{:S(2)}, u32[]{:S(2)}) collective-permute-start(bf16[1024,128]{1,0:T(8,128)(2,1)S(1)} %get-tuple-element.54), channel_id=1, source_target_pairs={{0,4},{4,0},{8,12},{12,8},{16,20},{20,16},{24,28},{28,24},{32,36},... | collective-permute-start | bytes 786440 | tf_op jit(solution)/shard_map/ppermute | solution.py:455
  24.7 9.1 %collective-permute-start.5 = (bf16[1024,128]{1,0:T(8,128)(2,1)S(1)}, bf16[1024,128]{1,0:T(8,128)(2,1)S(1)}, u32[]{:S(2)}, u32[]{:S(2)}) collective-permute-start(bf16[1024,128]{1,0:T(8,128)(2,1)S(1)} %get-tuple-element.55), channel_id=1, source_target_pairs={{4,0},{16,4},{12,8},{24,12},{20,16},{32,20},{28,24},{40,28},{36,32... | collective-permute-start | bytes 786440 | tf_op jit(solution)/shard_map/ppermute | solution.py:455
  29.3 12.9 %collective-permute-start.4 = (bf16[1024,128]{1,0:T(8,128)(2,1)S(1)}, bf16[1024,128]{1,0:T(8,128)(2,1)S(1)}, u32[]{:S(2)}, u32[]{:S(2)}) collective-permute-start(bf16[1024,128]{1,0:T(8,128)(2,1)S(1)} %sum.2), channel_id=1, source_target_pairs={{8,0},{12,4},{16,8},{20,12},{24,16},{28,20},{32,24},{36,28},{40,32... | collective-permute-start | bytes 786440 | tf_op jit(solution)/shard_map/ppermute | solution.py:455
